TPU v7x, 32 devices: a whole 2x2x4 slice. The times are simulated.
32 devices in a mesh: dp: 8 (over y, x, core), tensor: 4 (over z).
Axes of the slice: x: 2, y: 2, z: 4, core: 2. Of those that a mesh axis runs over, the one named last changes fastest.
Arguments:
- patches: float32 [16384, 1152], P(('dp', 'tensor')), may hold values from -16 to 16
- conditioning: float32 [64, 1152], P(('dp', 'tensor')), may hold values from -10 to 10
- time_bins: int32 [64], P(('dp', 'tensor')), may hold values from 0 to 511
- lengths: int32 [64], P(('dp', 'tensor')), may hold values from 32 to 256, as said below
- positions: int32 [2, 16384], P(None, ('dp', 'tensor')), may hold values from 0 to 127, as said below
- time_table: float32 [512, 1152], replicated, may hold values from -3 to 3
- w_ada: bfloat16 [1152, 6912], replicated, may hold values from -0.1875 to 0.1875
- b_ada: float32 [6912], replicated, may hold values from -3 to 3
- w_qkv: bfloat16 [1152, 3, 1152], P(None, None, 'tensor'), may hold values from -0.1875 to 0.1875
- w_out: bfloat16 [1152, 1152], P('tensor'), may hold values from -0.75 to 0.75
- branch_bias: float32 [2304], replicated, may hold values from -2 to 2
- w_gu: bfloat16 [1152, 2, 3072], P(None, None, 'tensor'), may hold values from -0.1875 to 0.1875
- w_down: bfloat16 [3072, 1152], P('tensor'), may hold values from -0.109375 to 0.109375
- d_out: float32 [16384, 1152], P(('dp', 'tensor')), may hold values from -6 to 6
Outputs:
- output: float32 [16384, 1152], P(('dp', 'tensor'))
- d_patches: float32 [16384, 1152], P(('dp', 'tensor'))
- d_conditioning: float32 [64, 1152], P(('dp', 'tensor'))
- d_w_qkv: float32 [1152, 3, 1152], P('dp', None, 'tensor')
- d_w_out: float32 [1152, 1152], P('tensor', 'dp')
- d_w_gu: float32 [1152, 2, 3072], P('dp', None, 'tensor')
- d_w_down: float32 [3072, 1152], P('tensor', 'dp')
- d_w_ada: float32 [1152, 6912], P(None, ('dp', 'tensor'))
- d_b_ada: float32 [6912], P(('dp', 'tensor'))
- d_branch_bias: float32 [2304], P(('dp', 'tensor'))
- d_time_table: float32 [512, 1152], P(('dp', 'tensor'))
- rms: float32 [3], replicated
Inputs may be any that keep to these rules, and one draw needn't show every extreme that they name: `lengths`: among the images of each index of dp one, drawn, has exactly 256 valid tokens. `positions`: token i of an image whose grid is w patches wide sits at row i // w and column i % w; w is drawn per image, and the first image's grid is 2 wide.
All inputs are finite; a program needn't handle non-finite values.
Results may differ from a plain program's by a relative error of at most 0.025.
The roundings to bfloat16 on the way count: a program that leaves them out, or rounds other values in their place, can miss the bound.
Values may be sent and summed in bfloat16 or wider, within the bound.
No kernel may reach another device: no remote copies, remote signals or barrier semaphores. Data moves between devices by JAX's collectives and lax.ppermute only.
A program may use at most 256 MiB of HBM per device.

v0:
```python
import jax
import jax.numpy as jnp
from jax import lax
from jax.sharding import PartitionSpec as P

HD = 72


EXACT = lax.Precision.HIGHEST
EPSILON = 1e-06


def layer_stats(values):
    centered = values - jnp.mean(values, axis=-1, keepdims=True)
    inverse = lax.rsqrt(jnp.mean(centered * centered, axis=-1, keepdims=True) + EPSILON)
    return (centered * inverse, inverse)


def layer_back(d_normed, normed, inverse, scale_row):
    d_hat = d_normed * (1.0 + scale_row)
    return inverse * (
        d_hat
        - jnp.mean(d_hat, axis=-1, keepdims=True)
        - normed * jnp.mean(d_hat * normed, axis=-1, keepdims=True)
    )


def angle_tables(row_pos, col_pos, head_size):
    quarter = head_size // 4
    frequency = 10000.0 ** (-jnp.arange(quarter, dtype=jnp.float32) / quarter)
    angle_row = row_pos[:, None, None] * frequency
    angle_col = col_pos[:, None, None] * frequency
    return (jnp.cos(angle_row), jnp.sin(angle_row), jnp.cos(angle_col), jnp.sin(angle_col))


def rotate(vector, tables, direction):
    cos_row, sin_row, cos_col, sin_col = tables
    sin_row = direction * sin_row
    sin_col = direction * sin_col
    quarter = vector.shape[-1] // 4
    part_one = vector[..., :quarter]
    part_two = vector[..., quarter : 2 * quarter]
    part_three = vector[..., 2 * quarter : 3 * quarter]
    part_four = vector[..., 3 * quarter :]
    return jnp.concatenate(
        [
            part_one * cos_row - part_two * sin_row,
            part_two * cos_row + part_one * sin_row,
            part_three * cos_col - part_four * sin_col,
            part_four * cos_col + part_three * sin_col,
        ],
        axis=-1,
    )


def masked_scores(queries, keys_low, key_ok, attn_scale):
    scores = (
        jnp.einsum("gqhd,gkhd->ghqk", queries, keys_low, preferred_element_type=jnp.float32)
        * attn_scale
    )
    return jnp.where(key_ok[:, None, None, :], scores, -1e30)


def local(
    patches,
    conditioning,
    time_bins,
    lengths,
    positions,
    time_table,
    w_ada,
    b_ada,
    w_qkv,
    w_out,
    branch_bias,
    w_gu,
    w_down,
    d_out,
):
    image_count = conditioning.shape[0]
    local_rows = patches.shape[0]
    seq_len = local_rows // image_count
    model_width = patches.shape[1]
    local_heads = w_qkv.shape[2] // HD
    local_hidden = w_gu.shape[2]
    attn_scale = HD ** (-0.5)
    onehot = (
        time_bins[:, None] == jnp.arange(time_table.shape[0], dtype=jnp.int32)[None, :]
    ).astype(jnp.float32)
    cond_vec = conditioning + jnp.dot(onehot, time_table, precision=EXACT)
    cond_sig = jax.nn.sigmoid(cond_vec)
    silu_low = (cond_vec * cond_sig).astype(jnp.bfloat16)
    modulation = (jnp.dot(silu_low, w_ada, preferred_element_type=jnp.float32) + b_ada).reshape(
        image_count, 6, 1, model_width
    )
    shift_one = modulation[:, 0]
    scale_one = modulation[:, 1]
    gate_one = modulation[:, 2]
    shift_two = modulation[:, 3]
    scale_two = modulation[:, 4]
    gate_two = modulation[:, 5]
    row_mask = (jnp.arange(seq_len, dtype=jnp.int32)[None, :] < lengths[:, None]).astype(
        jnp.float32
    )[:, :, None]
    inputs = patches.reshape(image_count, seq_len, model_width)
    normed_one, inverse_one = layer_stats(inputs)
    attn_in = (
        (normed_one * (1.0 + scale_one) + shift_one)
        .astype(jnp.bfloat16)
        .reshape(local_rows, model_width)
    )
    attn_all, pos_all, len_all = (
        lax.all_gather(attn_in, "tensor", axis=0, tiled=True),
        lax.all_gather(positions.astype(jnp.bfloat16), "tensor", axis=1, tiled=True),
        lax.all_gather(lengths.astype(jnp.bfloat16), "tensor", axis=0, tiled=True),
    )
    all_rows = attn_all.shape[0]
    group_images = all_rows // seq_len
    head_shape = (group_images, seq_len, local_heads, HD)
    flat_heads = (all_rows, local_heads, HD)
    tables = angle_tables(pos_all[0].astype(jnp.float32), pos_all[1].astype(jnp.float32), HD)
    w_qkv_flat = w_qkv.reshape(model_width, -1)
    projected = jnp.dot(attn_all, w_qkv_flat, preferred_element_type=jnp.float32).reshape(
        all_rows, 3, local_heads, HD
    )
    queries = rotate(projected[:, 0], tables, 1.0).astype(jnp.bfloat16).reshape(head_shape)
    keys_low = rotate(projected[:, 1], tables, 1.0).astype(jnp.bfloat16).reshape(head_shape)
    values_low = projected[:, 2].astype(jnp.bfloat16).reshape(head_shape)
    key_ok = jnp.arange(seq_len, dtype=jnp.float32)[None, :] < len_all.astype(jnp.float32)[:, None]
    scores = masked_scores(queries, keys_low, key_ok, attn_scale)
    row_top = jnp.max(scores, axis=-1, keepdims=True)
    exponent = jnp.exp(scores - row_top)
    row_total = jnp.sum(exponent, axis=-1, keepdims=True)
    probs_full = exponent / row_total
    log_total = row_top + jnp.log(row_total)
    attended = (
        jnp.einsum(
            "ghqk,gkhd->gqhd",
            probs_full.astype(jnp.bfloat16),
            values_low,
            preferred_element_type=jnp.float32,
        )
        .astype(jnp.bfloat16)
        .reshape(all_rows, local_heads * HD)
    )
    attn_sum = lax.psum_scatter(
        jnp.dot(attended, w_out, preferred_element_type=jnp.float32).astype(jnp.bfloat16),
        "tensor",
        scatter_dimension=0,
        tiled=True,
    ).astype(jnp.float32)
    attn_branch = (attn_sum + branch_bias[:model_width]).reshape(image_count, seq_len, model_width)
    attn_gated = row_mask * gate_one * attn_branch
    residual = inputs + attn_gated
    normed_two, inverse_two = layer_stats(residual)
    mlp_in = (
        (normed_two * (1.0 + scale_two) + shift_two)
        .astype(jnp.bfloat16)
        .reshape(local_rows, model_width)
    )
    mlp_all = lax.all_gather(mlp_in, "tensor", axis=0, tiled=True)
    w_gu_flat = w_gu.reshape(model_width, -1)
    gate_up = jnp.dot(mlp_all, w_gu_flat, preferred_element_type=jnp.float32).reshape(
        all_rows, 2, local_hidden
    )
    gate_pre = gate_up[:, 0]
    up_pre = gate_up[:, 1]
    gate_sig = jax.nn.sigmoid(gate_pre)
    hidden = (gate_pre * gate_sig * up_pre).astype(jnp.bfloat16)
    mlp_sum = lax.psum_scatter(
        jnp.dot(hidden, w_down, preferred_element_type=jnp.float32).astype(jnp.bfloat16),
        "tensor",
        scatter_dimension=0,
        tiled=True,
    ).astype(jnp.float32)
    mlp_branch = (mlp_sum + branch_bias[model_width:]).reshape(image_count, seq_len, model_width)
    mlp_gated = row_mask * gate_two * mlp_branch
    output = residual + mlp_gated
    square_x, square_attn, square_mlp, token_total = lax.psum(
        (
            jnp.sum(row_mask * inputs * inputs),
            jnp.sum(attn_gated * attn_gated),
            jnp.sum(mlp_gated * mlp_gated),
            jnp.sum(lengths).astype(jnp.float32),
        ),
        ("dp", "tensor"),
    )
    rms_values = jnp.sqrt(
        jnp.stack([square_x, square_attn, square_mlp]) / (token_total * model_width)
    )
    upstream = d_out.reshape(image_count, seq_len, model_width)
    d_mlp = row_mask * gate_two * upstream
    d_gate_two = jnp.sum(row_mask * mlp_branch * upstream, axis=1, keepdims=True)
    d_bias_mlp = jnp.sum(d_mlp, axis=(0, 1))
    d_mlp_all = lax.all_gather(
        d_mlp.astype(jnp.bfloat16).reshape(local_rows, model_width), "tensor", axis=0, tiled=True
    )
    grad_down = jnp.einsum("rf,rd->fd", hidden, d_mlp_all, preferred_element_type=jnp.float32)
    d_hidden = jnp.einsum("rd,fd->rf", d_mlp_all, w_down, preferred_element_type=jnp.float32)
    d_gate = d_hidden * up_pre * gate_sig * (1.0 + gate_pre * (1.0 - gate_sig))
    d_up = d_hidden * gate_pre * gate_sig
    d_gate_up = (
        jnp.stack([d_gate, d_up], axis=1).astype(jnp.bfloat16).reshape(all_rows, 2 * local_hidden)
    )
    grad_gu = jnp.einsum(
        "rd,rk->dk", mlp_all, d_gate_up, preferred_element_type=jnp.float32
    ).reshape(model_width, 2, local_hidden)
    d_mlp_in = (
        lax.psum_scatter(
            jnp.einsum(
                "rk,dk->rd", d_gate_up, w_gu_flat, preferred_element_type=jnp.float32
            ).astype(jnp.bfloat16),
            "tensor",
            scatter_dimension=0,
            tiled=True,
        )
        .astype(jnp.float32)
        .reshape(image_count, seq_len, model_width)
    )
    d_scale_two = jnp.sum(d_mlp_in * normed_two, axis=1, keepdims=True)
    d_shift_two = jnp.sum(d_mlp_in, axis=1, keepdims=True)
    d_residual = upstream + layer_back(d_mlp_in, normed_two, inverse_two, scale_two)
    d_attn = row_mask * gate_one * d_residual
    d_gate_one = jnp.sum(row_mask * attn_branch * d_residual, axis=1, keepdims=True)
    d_bias_attn = jnp.sum(d_attn, axis=(0, 1))
    d_attn_all = lax.all_gather(
        d_attn.astype(jnp.bfloat16).reshape(local_rows, model_width), "tensor", axis=0, tiled=True
    )
    grad_out = jnp.einsum("rk,rd->kd", attended, d_attn_all, preferred_element_type=jnp.float32)
    d_attended = (
        jnp.einsum("rd,kd->rk", d_attn_all, w_out, preferred_element_type=jnp.float32)
        .astype(jnp.bfloat16)
        .reshape(head_shape)
    )
    scores = masked_scores(queries, keys_low, key_ok, attn_scale)
    probs_full = jnp.exp(scores - log_total)
    d_probs = jnp.einsum(
        "gqhd,gkhd->ghqk", d_attended, values_low, preferred_element_type=jnp.float32
    )
    d_values = jnp.einsum(
        "ghqk,gqhd->gkhd",
        probs_full.astype(jnp.bfloat16),
        d_attended,
        preferred_element_type=jnp.float32,
    )
    d_scores = (
        probs_full * (d_probs - jnp.sum(d_probs * probs_full, axis=-1, keepdims=True))
    ).astype(jnp.bfloat16)
    d_queries = (
        jnp.einsum("ghqk,gkhd->gqhd", d_scores, keys_low, preferred_element_type=jnp.float32)
        * attn_scale
    )
    d_keys = (
        jnp.einsum("ghqk,gqhd->gkhd", d_scores, queries, preferred_element_type=jnp.float32)
        * attn_scale
    )
    d_projected = (
        jnp.stack(
            [
                rotate(d_queries.reshape(flat_heads), tables, -1.0),
                rotate(d_keys.reshape(flat_heads), tables, -1.0),
                d_values.reshape(flat_heads),
            ],
            axis=1,
        )
        .astype(jnp.bfloat16)
        .reshape(all_rows, -1)
    )
    grad_qkv = jnp.einsum(
        "rd,rk->dk", attn_all, d_projected, preferred_element_type=jnp.float32
    ).reshape(model_width, 3, local_heads * HD)
    d_attn_in = (
        lax.psum_scatter(
            jnp.einsum(
                "rk,dk->rd", d_projected, w_qkv_flat, preferred_element_type=jnp.float32
            ).astype(jnp.bfloat16),
            "tensor",
            scatter_dimension=0,
            tiled=True,
        )
        .astype(jnp.float32)
        .reshape(image_count, seq_len, model_width)
    )
    d_scale_one = jnp.sum(d_attn_in * normed_one, axis=1, keepdims=True)
    d_shift_one = jnp.sum(d_attn_in, axis=1, keepdims=True)
    d_inputs = d_residual + layer_back(d_attn_in, normed_one, inverse_one, scale_one)
    d_modulation = jnp.concatenate(
        [d_shift_one, d_scale_one, d_gate_one, d_shift_two, d_scale_two, d_gate_two], axis=1
    ).reshape(image_count, 6 * model_width)
    d_b_ada_local = jnp.sum(d_modulation, axis=0)
    d_mod_low = d_modulation.astype(jnp.bfloat16)
    d_silu = jnp.einsum("bk,dk->bd", d_mod_low, w_ada, preferred_element_type=jnp.float32)
    d_cond = d_silu * cond_sig * (1.0 + cond_vec * (1.0 - cond_sig))
    d_table_local = jnp.dot(onehot.T, d_cond, precision=EXACT)
    d_bias_local = jnp.concatenate([d_bias_attn, d_bias_mlp])
    grad_qkv_part, grad_out_part, grad_gu_part, grad_down_part = (
        lax.psum_scatter(
            grad_qkv.astype(jnp.bfloat16), "dp", scatter_dimension=0, tiled=True
        ).astype(jnp.float32),
        lax.psum_scatter(
            grad_out.astype(jnp.bfloat16), "dp", scatter_dimension=1, tiled=True
        ).astype(jnp.float32),
        lax.psum_scatter(
            grad_gu.astype(jnp.bfloat16), "dp", scatter_dimension=0, tiled=True
        ).astype(jnp.float32),
        lax.psum_scatter(
            grad_down.astype(jnp.bfloat16), "dp", scatter_dimension=1, tiled=True
        ).astype(jnp.float32),
    )
    grad_ada_local = jnp.einsum(
        "bd,bk->dk", silu_low, d_mod_low, preferred_element_type=jnp.float32
    )
    grad_ada, grad_b_ada, grad_bias, grad_table = (
        lax.psum_scatter(grad_ada_local, ("dp", "tensor"), scatter_dimension=1, tiled=True),
        lax.psum_scatter(d_b_ada_local, ("dp", "tensor"), scatter_dimension=0, tiled=True),
        lax.psum_scatter(d_bias_local, ("dp", "tensor"), scatter_dimension=0, tiled=True),
        lax.psum_scatter(d_table_local, ("dp", "tensor"), scatter_dimension=0, tiled=True),
    )
    return (
        output.reshape(local_rows, model_width),
        d_inputs.reshape(local_rows, model_width),
        d_cond,
        grad_qkv_part,
        grad_out_part,
        grad_gu_part,
        grad_down_part,
        grad_ada,
        grad_b_ada,
        grad_bias,
        grad_table,
        rms_values,
    )


def solution(mesh):
    return jax.shard_map(
        local,
        mesh=mesh,
        in_specs=(
            P(("dp", "tensor"), None),
            P(("dp", "tensor"), None),
            P(("dp", "tensor")),
            P(("dp", "tensor")),
            P(None, ("dp", "tensor")),
            P(),
            P(),
            P(),
            P(None, None, "tensor"),
            P("tensor", None),
            P(),
            P(None, None, "tensor"),
            P("tensor", None),
            P(("dp", "tensor"), None),
        ),
        out_specs=(
            P(("dp", "tensor"), None),
            P(("dp", "tensor"), None),
            P(("dp", "tensor"), None),
            P("dp", None, "tensor"),
            P("tensor", "dp"),
            P("dp", None, "tensor"),
            P("tensor", "dp"),
            P(None, ("dp", "tensor")),
            P(("dp", "tensor")),
            P(("dp", "tensor")),
            P(("dp", "tensor"), None),
            P(),
        ),
        check_vma=False,
    )
```

profile of v0, /device:TPU:0, one launch (start us, length us, event | category | flops | bytes accessed | tf_op | source)
XLA Modules:
  0.0 1469.7 jit_solution(5678752300720621455)
XLA Ops:
  12.9 7.8 convolution_add_fusion
  25.9 13.5 all-reduce
  39.4 12.2 all_gather.20
  54.0 62.1 %all-gather.5.cloned.1.call-done = bf16[2048,1152]{1,0:T(8,128)(2,1)} async-done(((bf16[512,1152]{1,0:T(8,128)(2,1)}), bf16[2048,1152]{1,0:T(8,128)(2,1)}) %all-gather.5.cloned.1.call-update) | async-done | bytes 4718608 | tf_op jit(solution)/shard_map/all_gather | solution.py:113
  116.1 7.3 fusion.4
  155.8 4.4 fusion.24
  163.6 2.8 fusion.55
  168.6 4.6 convolution_convert_fusion.1
  175.2 81.9 %reduce-scatter.13.cloned.1.call-done = bf16[512,1152]{1,0:T(8,128)(2,1)} async-done(((bf16[2048,1152]{1,0:T(8,128)(2,1)}), bf16[512,1152]{1,0:T(8,128)(2,1)}) %reduce-scatter.13.cloned.1.call-update) | async-done | bytes 1179664 | tf_op jit(solution)/shard_map/reduce_scatter | solution.py:146
  257.1 3.8 fusion.77
  264.7 4.5 copy.190
  269.2 5.8 copy.138
  275.0 79.1 %all-gather.7.cloned.1.call-done = bf16[2048,1152]{1,0:T(8,128)(2,1)} async-done(((bf16[512,1152]{1,0:T(8,128)(2,1)}), bf16[2048,1152]{1,0:T(8,128)(2,1)}) %all-gather.7.cloned.1.call-update) | async-done | bytes 4718608 | tf_op jit(solution)/shard_map/all_gather | solution.py:161
  354.1 14.1 fusion.9
  368.2 75.8 %all-gather.9.cloned.1.call-done = bf16[2048,1152]{1,0:T(8,128)(2,1)} async-done(((bf16[512,1152]{1,0:T(8,128)(2,1)}), bf16[2048,1152]{1,0:T(8,128)(2,1)}) %all-gather.9.cloned.1.call-update) | async-done | bytes 4718608 | tf_op jit(solution)/shard_map/all_gather | solution.py:195
  444.0 10.0 multiply_bitcast_fusion.1
  456.7 10.1 bitcast_convert_fusion
  466.9 6.6 multiply_convert_fusion.1
  475.1 6.1 convolution_convert_fusion
  481.2 69.5 %reduce-scatter.17.cloned.1.call-done = bf16[512,1152]{1,0:T(8,128)(2,1)} async-done(((bf16[2048,1152]{1,0:T(8,128)(2,1)}), bf16[512,1152]{1,0:T(8,128)(2,1)}) %reduce-scatter.17.cloned.1.call-update) | async-done | bytes 1179664 | tf_op jit(solution)/shard_map/reduce_scatter | solution.py:209
  554.0 84.6 %reduce-scatter.15.cloned.1.call-done = bf16[512,1152]{1,0:T(8,128)(2,1)} async-done(((bf16[2048,1152]{1,0:T(8,128)(2,1)}), bf16[512,1152]{1,0:T(8,128)(2,1)}) %reduce-scatter.15.cloned.1.call-update) | async-done | bytes 1179664 | tf_op jit(solution)/shard_map/reduce_scatter | solution.py:170
  638.7 4.9 fusion.46
  644.4 89.2 %all-gather.11.cloned.1.call-done = bf16[2048,1152]{1,0:T(8,128)(2,1)} async-done(((bf16[512,1152]{1,0:T(8,128)(2,1)}), bf16[2048,1152]{1,0:T(8,128)(2,1)}) %all-gather.11.cloned.1.call-update) | async-done | bytes 4718608 | tf_op jit(solution)/shard_map/all_gather | solution.py:226
  733.7 4.4 convolution_convert_fusion.5
  738.7 5.9 fusion.51
  744.6 4.1 multiply_reduce_fusion
  748.8 2.6 multiply_convert_fusion
  751.4 2.9 multiply_bitcast_fusion.2
  766.3 7.2 convolution_convert_fusion.2
  773.8 8.4 convolution_convert_fusion.3
  782.3 13.4 fusion.11
  799.9 6.0 convolution_convert_fusion.4
  806.3 11.1 fusion.20
  817.5 40.0 %reduce-scatter.19.cloned.1.call-done = bf16[512,1152]{1,0:T(8,128)(2,1)} async-done(((bf16[2048,1152]{1,0:T(8,128)(2,1)}), bf16[512,1152]{1,0:T(8,128)(2,1)}) %reduce-scatter.19.cloned.1.call-update) | async-done | bytes 1179664 | tf_op jit(solution)/shard_map/reduce_scatter | solution.py:273
  857.4 5.0 fusion.38
  863.2 10.0 fusion.43
  873.2 2.8 fusion.62
  876.4 13.0 fusion.76
  890.2 10.5 reduce-scatter.27.cloned.1.call-done
  902.5 49.7 %reduce-scatter.25.cloned.1.call-done = bf16[144,2,768]{2,0,1:T(8,128)(2,1)} async-done(((bf16[1152,2,768]{2,0,1:T(8,128)(2,1)}), bf16[144,2,768]{2,0,1:T(8,128)(2,1)}) %reduce-scatter.25.cloned.1.call-update) | async-done | bytes 442384 | tf_op jit(solution)/shard_map/reduce_scatter | solution.py:303
  954.5 36.1 %reduce-scatter.23.cloned.1.call-done = bf16[288,144]{0,1:T(8,128)(2,1)} async-done(((bf16[288,1152]{0,1:T(8,128)(2,1)}), bf16[288,144]{0,1:T(8,128)(2,1)}) %reduce-scatter.23.cloned.1.call-update) | async-done | bytes 82960 | tf_op jit(solution)/shard_map/reduce_scatter | solution.py:300
  992.2 46.0 %reduce-scatter.21.cloned.1.call-done = bf16[144,3,288]{2,0,1:T(8,128)(2,1)} async-done(((bf16[1152,3,288]{2,0,1:T(8,128)(2,1)}), bf16[144,3,288]{2,0,1:T(8,128)(2,1)}) %reduce-scatter.21.cloned.1.call-update) | async-done | bytes 248848 | tf_op jit(solution)/shard_map/reduce_scatter | solution.py:297
  1041.4 5.6 fusion.25
  1047.0 40.5 %all-reduce.4 = (f32[6912]{0:T(1024)S(1)}, f32[2304]{0:T(1024)S(1)}, f32[1]{0:T(128)}, f32[1]{0:T(128)}, f32[1]{0:T(128)}, /*index=5*/f32[]{:T(128)}) all-reduce(f32[6912]{0:T(1024)} %reduce_sum.226, f32[2304]{0:T(1024)S(1)} %pad_maximum_fusion.2, f32[1]{0:T(128)} %bitcast.53, ...), channel_id=11, replica_groups=mesh['dp'=8,'tensor'=4] {'dp','tensor'}, use_global_device_ids=true, to_apply=%region_27.28.clone | all-reduce | flops 9220 | bytes 73760
  1090.8 4.9 fusion.35
  1095.7 2.6 fusion.65
  1098.3 44.8 %reduce-scatter.29.cloned.1.call-done = f32[16,1152]{1,0:T(8,128)} async-done(((f32[512,1152]{1,0:T(8,128)}), f32[16,1152]{1,0:T(8,128)}) %reduce-scatter.29.cloned.1.call-update) | async-done | bytes 73744 | tf_op jit(solution)/shard_map/reduce_scatter | solution.py:317
  1143.0 319.6 %reduce-scatter.31.cloned.1.call-done = f32[1152,216]{0,1:T(8,128)} async-done(((f32[1152,6912]{0,1:T(8,128)}), f32[1152,216]{0,1:T(8,128)}) %reduce-scatter.31.cloned.1.call-update) | async-done | bytes 995344
  (273 shorter events, 94.5 us)
Async XLA Ops:
  7.2 4.2 copy-start
  7.2 4.2 copy-start.65
  7.2 4.2 copy-start.63
  7.2 108.9 %all-gather.5.cloned.1.call-start = ((), (), s32[]{:S(2)}) async-start(), calls=%async_computation.10 | async-start | bytes 5898240 | tf_op jit(solution)/shard_map/all_gather | solution.py:113
  9.3 12.2 copy-start.44
  9.3 3.6 copy-start.59
  11.4 10.1 copy-start.48
  12.9 9.2 copy-start.2
  22.1 17.4 %copy-start.64 = (s32[2,512]{1,0:T(2,128)S(1)}, s32[2,512]{1,0:T(2,128)}, u32[]{:S(2)}) copy-start(s32[2,512]{1,0:T(2,128)} %param.18) | copy-start | bytes 12292
  23.8 233.4 %reduce-scatter.13.cloned.1.call-start = ((), (), s32[]{:S(2)}) async-start(), calls=%async_computation.11 | async-start | bytes 5898240 | tf_op jit(solution)/shard_map/reduce_scatter | solution.py:146
  51.8 110.7 %copy-start.56 = (pred[8,256]{1,0:T(8,128)(4,1)}, pred[8,256]{1,0:T(8,128)(4,1)S(1)}, u32[]{:S(2)}) copy-start(pred[8,256]{1,0:T(8,128)(4,1)S(1)} %iota_compare_fusion) | copy-start | bytes 6148
  54.0 72.7 %copy-start.11 = (f32[2048,18]{0,1:T(8,128)}, f32[2048,18]{0,1:T(8,128)S(1)}, u32[]{:S(2)}) copy-start(f32[2048,18]{0,1:T(8,128)S(1)} %get-tuple-element.130) | copy-start | bytes 442372
  54.0 72.7 %copy-start.13 = (f32[2048,18]{0,1:T(8,128)}, f32[2048,18]{0,1:T(8,128)S(1)}, u32[]{:S(2)}) copy-start(f32[2048,18]{0,1:T(8,128)S(1)} %get-tuple-element.142) | copy-start | bytes 442372
  132.8 29.6 %copy-start.15 = (bf16[36,8,8,256]{3,2,1,0:T(8,128)(2,1)}, bf16[36,8,8,256]{3,2,1,0:T(8,128)(2,1)S(1)}, u32[]{:S(2)}) copy-start(bf16[36,8,8,256]{3,2,1,0:T(8,128)(2,1)S(1)} %copy.188) | copy-start | bytes 3538948
  155.8 4.4 copy-start.29
  162.4 4.1 copy-start.42
  173.3 180.8 %all-gather.7.cloned.1.call-start = ((), (), s32[]{:S(2)}) async-start(), calls=%async_computation.12 | async-start | bytes 5898240 | tf_op jit(solution)/shard_map/all_gather | solution.py:161
  174.6 86.4 %copy-start.58 = (f32[1,2,2,128]{3,1,2,0:T(2,128)}, f32[1,2,2,128]{3,1,2,0:T(2,128)S(1)}, u32[]{:S(2)}) copy-start(f32[1,2,2,128]{3,1,2,0:T(2,128)S(1)} %copy.187) | copy-start | bytes 6148
  175.2 85.8 %copy-start.43 = (f32[1152]{0:T(1024)}, f32[1152]{0:T(1024)S(1)}, u32[]{:S(2)}) copy-start(f32[1152]{0:T(1024)S(1)} %get-tuple-element.127) | copy-start | bytes 13828
  175.2 86.2 %copy-start.35 = (f32[2,1152]{1,0:T(2,128)}, f32[2,1152]{1,0:T(2,128)S(1)}, u32[]{:S(2)}) copy-start(f32[2,1152]{1,0:T(2,128)S(1)} %get-tuple-element.149) | copy-start | bytes 27652
  175.2 85.7 %copy-start.39 = (f32[2,1152]{1,0:T(2,128)}, f32[2,1152]{1,0:T(2,128)S(1)}, u32[]{:S(2)}) copy-start(f32[2,1152]{1,0:T(2,128)S(1)} %get-tuple-element.150) | copy-start | bytes 27652
  261.0 377.7 %copy-start.46 = (f32[512]{0:T(512)}, f32[512]{0:T(512)S(1)}, u32[]{:S(2)}) copy-start(f32[512]{0:T(512)S(1)} %broadcast_multiply_fusion.6) | copy-start | bytes 6148
  264.0 180.0 %all-gather.9.cloned.1.call-start = ((), (), s32[]{:S(2)}) async-start(), calls=%async_computation.14 | async-start | bytes 5898240 | tf_op jit(solution)/shard_map/all_gather | solution.py:195
  264.6 286.1 %reduce-scatter.17.cloned.1.call-start = ((), (), s32[]{:S(2)}) async-start(), calls=%async_computation.15 | async-start | bytes 5898240 | tf_op jit(solution)/shard_map/reduce_scatter | solution.py:209
  354.1 89.9 %copy-start.70 = (bf16[768,1152]{1,0:T(8,128)(2,1)S(1)}, bf16[768,1152]{1,0:T(8,128)(2,1)}, u32[]{:S(2)}) copy-start(bf16[768,1152]{1,0:T(8,128)(2,1)} %param.26) | copy-start | bytes 5308420
  444.0 12.7 copy-start.17
  466.8 171.8 %reduce-scatter.15.cloned.1.call-start = ((), (), s32[]{:S(2)}) async-start(), calls=%async_computation.13 | async-start | bytes 5898240 | tf_op jit(solution)/shard_map/reduce_scatter | solution.py:170
  481.1 69.5 %copy-start.6 = (f32[512,1152]{1,0:T(8,128)S(1)}, f32[512,1152]{1,0:T(8,128)}, u32[]{:S(2)}) copy-start(f32[512,1152]{1,0:T(8,128)} %copy-done.5) | copy-start | bytes 7077892
  481.2 252.5 %all-gather.11.cloned.1.call-start = ((), (), s32[]{:S(2)}) async-start(), calls=%async_computation.16 | async-start | bytes 5898240 | tf_op jit(solution)/shard_map/all_gather | solution.py:226
  550.7 88.0 %copy-start.9 = (bf16[512,1152]{1,0:T(8,128)(2,1)S(1)}, bf16[512,1152]{1,0:T(8,128)(2,1)}, u32[]{:S(2)}) copy-start(bf16[512,1152]{1,0:T(8,128)(2,1)} %reduce-scatter.17.cloned.1.call-done) | copy-start | bytes 3538948
  643.6 213.9 %reduce-scatter.19.cloned.1.call-start = ((), (), s32[]{:S(2)}) async-start(), calls=%async_computation.17 | async-start | bytes 5898240 | tf_op jit(solution)/shard_map/reduce_scatter | solution.py:273
  733.7 10.9 slice-start
  738.7 5.9 slice-start.1
  738.7 5.9 copy-start.16
  773.6 127.2 %reduce-scatter.27.cloned.1.call-start = ((), (), s32[]{:S(2)}) async-start(), calls=%async_computation.21 | async-start | bytes 1990656 | tf_op jit(solution)/shard_map/reduce_scatter | solution.py:306
  782.3 169.9 %reduce-scatter.25.cloned.1.call-start = ((), (), s32[]{:S(2)}) async-start(), calls=%async_computation.20 | async-start | bytes 3981312 | tf_op jit(solution)/shard_map/reduce_scatter | solution.py:303
  795.7 3.6 copy-start.61
  795.7 4.2 copy-start.32
  795.8 194.8 %reduce-scatter.23.cloned.1.call-start = ((), (), s32[]{:S(2)}) async-start(), calls=%async_computation.19 | async-start | bytes 995328 | tf_op jit(solution)/shard_map/reduce_scatter | solution.py:300
  806.0 232.2 %reduce-scatter.21.cloned.1.call-start = ((), (), s32[]{:S(2)}) async-start(), calls=%async_computation.18 | async-start | bytes 2985984 | tf_op jit(solution)/shard_map/reduce_scatter | solution.py:297
  806.3 51.2 %copy-start.8 = (bf16[512,1152]{1,0:T(8,128)(2,1)S(1)}, bf16[512,1152]{1,0:T(8,128)(2,1)}, u32[]{:S(2)}) copy-start(bf16[512,1152]{1,0:T(8,128)(2,1)} %reduce-scatter.13.cloned.1.call-done) | copy-start | bytes 3538948
  817.4 40.0 %copy-start.3 = (f32[512,1152]{1,0:T(8,128)S(1)}, f32[512,1152]{1,0:T(8,128)}, u32[]{:S(2)}) copy-start(f32[512,1152]{1,0:T(8,128)} %param.14) | copy-start | bytes 7077892
  817.4 325.6 %reduce-scatter.29.cloned.1.call-start = ((), (), s32[]{:S(2)}) async-start(), calls=%async_computation.22 | async-start | bytes 2433024 | tf_op jit(solution)/shard_map/reduce_scatter | solution.py:317
  857.4 5.7 copy-start.37
  863.2 10.0 copy-start.66
  876.1 586.6 %reduce-scatter.31.cloned.1.call-start = ((), (), s32[]{:S(2)}) async-start(), calls=%async_computation.23 | async-start | bytes 32845824
  889.5 151.9 %copy-start.7 = (bf16[512,1152]{1,0:T(8,128)(2,1)S(1)}, bf16[512,1152]{1,0:T(8,128)(2,1)}, u32[]{:S(2)}) copy-start(bf16[512,1152]{1,0:T(8,128)(2,1)} %reduce-scatter.19.cloned.1.call-done) | copy-start | bytes 3538948
  1089.9 372.7 %copy-start.1 = (f32[512,1152]{1,0:T(8,128)S(1)}, f32[512,1152]{1,0:T(8,128)}, u32[]{:S(2)}) copy-start(f32[512,1152]{1,0:T(8,128)} %param.19) | copy-start | bytes 7077892
  (43 other events, 86.5 us)
Sparse Core Ops, SparseCore 0:
  23.9 92.1 all-gather.4
  173.4 83.6 reduce-scatter.12
  264.1 89.9 all-gather.6
  356.1 87.8 all-gather.8
  466.9 83.6 reduce-scatter.16
  552.8 85.7 reduce-scatter.14
  643.7 89.9 all-gather.10
  773.7 83.6 reduce-scatter.18
  860.8 39.9 reduce-scatter.26
  904.1 48.0 reduce-scatter.24
  955.4 35.0 reduce-scatter.22
  994.3 43.7 reduce-scatter.20
  1044.0 99.0 reduce-scatter.28
  1151.0 311.5 reduce-scatter.30
where the time goes:
time: 1480 us; the launch traced here: 1470 us
  waiting for transfers between devices  1090 us (74%)
  matrix products  158 us (11%)
  local copies, waits for them, and re-layouts  69.8 us (5%)
  other arithmetic  67 us (5%)
  blocking collectives  66.2 us (4%)
  between operations  17.4 us (1%)
    unnamed x15, waiting for transfers between devices  320 us
    all_gather x1, waiting for transfers between devices, local(): lax.all_gather(d_attn.astype(jnp.bfloat16).reshape(local_rows, model_widt...  89.2 us
    reduce_scatter x1, waiting for transfers between devices, local(): lax.psum_scatter(jnp.dot(hidden, w_down, preferred_element_type=jnp.float...  84.6 us
    reduce_scatter x1, waiting for transfers between devices, local(): lax.psum_scatter(jnp.dot(attended, w_out, preferred_element_type=jnp.floa...  81.9 us
    all_gather x1, waiting for transfers between devices, local(): mlp_all = lax.all_gather(mlp_in, 'tensor', axis=0, tiled=True)  79.1 us
    all_gather x1, waiting for transfers between devices, local(): lax.all_gather(d_mlp.astype(jnp.bfloat16).reshape(local_rows, model_width...  75.8 us
    reduce_scatter x1, waiting for transfers between devices, local(): lax.psum_scatter(jnp.einsum('rk,dk->rd', d_gate_up, w_gu_flat, preferred_...  69.5 us
    all_gather x1, waiting for transfers between devices, local(): lax.all_gather(attn_in, 'tensor', axis=0, tiled=True)  62.1 us
  transfers between devices with their start and end apart: 14, of which 14 were waited for; matrix products, arithmetic and copies ran while one was open for 10% of the time, Pallas kernels for 0%

commit v1 on v0

v1 whole, which is shorter than its diff:
```python
import functools

import jax
import jax.numpy as jnp
import numpy as np
from jax import lax
from jax.experimental import pallas as pl
from jax.experimental.pallas import tpu as pltpu
from jax.sharding import Mesh
from jax.sharding import PartitionSpec as P

HD = 72
EXACT = lax.Precision.HIGHEST
EPSILON = 1e-06
NEG = -1e30
VMEM_LIMIT = 58 * 1024 * 1024
UNROLL = 4
BF = jnp.bfloat16
F32 = jnp.float32
NT = (((1,), (1,)), ((), ()))
TN = (((0,), (0,)), ((), ()))


def dot(a, b):
    return jnp.dot(a, b, preferred_element_type=F32)


def dot_nt(a, b):
    return lax.dot_general(a, b, NT, preferred_element_type=F32)


def dot_tn(a, b):
    return lax.dot_general(a, b, TN, preferred_element_type=F32)


def call(kernel, name, grid, ins, outs, scratch=(), scalars=(), flops=0, moved=0, exps=0, deps=()):
    def spec(shape, block, index):
        if block is None:
            return pl.BlockSpec(shape, lambda *_: (0,) * len(shape))
        return pl.BlockSpec(block, lambda *at: index(*at[: len(grid)]))

    arrays = [item[0] for item in ins]
    in_specs = [spec(item[0].shape, item[1], item[2]) for item in ins]
    out_specs = [spec(item[0].shape, item[1], item[2]) for item in outs]
    count_s, count_i, count_d = len(scalars), len(ins), len(deps)

    def body(*refs):
        kept = refs[: count_s + count_i] + refs[count_s + count_i + count_d :]
        kernel(*kept)

    return pl.pallas_call(
        body,
        grid_spec=pltpu.PrefetchScalarGridSpec(
            num_scalar_prefetch=count_s,
            grid=grid,
            in_specs=in_specs + [pl.BlockSpec(memory_space=pl.ANY)] * count_d,
            out_specs=out_specs,
            scratch_shapes=list(scratch),
        ),
        out_shape=[item[0] for item in outs],
        compiler_params=pltpu.CompilerParams(
            dimension_semantics=("arbitrary",) * len(grid), vmem_limit_bytes=VMEM_LIMIT
        ),
        cost_estimate=pl.CostEstimate(flops=flops, bytes_accessed=moved, transcendentals=exps),
        name=name,
    )(*scalars, *arrays, *deps)


def shape(dims, dtype):
    return jax.ShapeDtypeStruct(tuple(dims), dtype)


def swap_matrix(width):
    quarter = HD // 4
    out = np.zeros((width, width), np.float32)
    for lane in range(width):
        if (lane % HD) % (2 * quarter) < quarter:
            out[lane + quarter, lane] = -1.0
        else:
            out[lane - quarter, lane] = 1.0
    return out


def head_mask(heads, which, dtype):
    lane = lax.broadcasted_iota(jnp.int32, (1, heads * HD), 1)
    inside = (lane >= which * HD) & (lane < (which + 1) * HD)
    return jnp.where(inside, 1.0, 0.0).astype(F32).astype(dtype)


def pick_weight(step, refs, scratch, last=None):
    for r, ref in enumerate(refs):

        @pl.when(step == r)
        def _(ref=ref):
            blocks, part = ref.shape[:2]
            for b in range(blocks):
                if last is not None and b == blocks - 1:
                    last[...] = ref[b]
                else:
                    scratch[b * part : (b + 1) * part, :] = ref[b]


def add_into(step, acc, rows, part):
    @pl.when(step == 0)
    def _():
        acc[rows, :] = part

    @pl.when(step > 0)
    def _():
        acc[rows, :] = acc[rows, :] + part


def hand_out(acc, own_ref, peer_ref):
    @pl.when(pl.program_id(0) == pl.num_programs(0) - 1)
    def _():
        half = own_ref.shape[0]
        own_ref[...] = acc[:half, :]
        peer_ref[...] = acc[half:, :].astype(BF)


def rows_of(step, count, body):
    for r in range(count):

        @pl.when(step == r)
        def _(r=r):
            body(r)


def copy_blocks(ref, blocks, scratch, first):
    part = ref.shape[1]
    for j, b in enumerate(blocks):
        scratch[first + j * part : first + (j + 1) * part, :] = ref[b]


def finish(left, right, own_ref, peer_ref, tile):
    half = own_ref.shape[0]
    for t in range(half // tile):
        at = slice(t * tile, (t + 1) * tile)
        own_ref[at, :] = dot_tn(left[:, at], right[...])
    for t in range(half // tile):
        there = slice(half + t * tile, half + (t + 1) * tile)
        peer_ref[t * tile : (t + 1) * tile, :] = dot_tn(left[:, there], right[...]).astype(BF)


def attn_fwd(lens, a_all, weights, cos, sin, heads, seq, deps=()):
    count, (rows, width), hw = len(weights), a_all.shape, heads * HD
    images = rows // seq
    scale = HD ** (-0.5)

    def kernel(lens, a_ref, cos_ref, sin_ref, swap_ref, *refs):
        w_refs, refs = refs[:count], refs[count:]
        q_ref, k_ref, v_ref, o_ref, own_ref, peer_ref, wcat, wout, full, o_all = refs
        step = pl.program_id(0)

        def pick(r):
            copy_blocks(w_refs[r], (0, 1, 2), wcat, 0)
            copy_blocks(w_refs[r], (3,), wout, r * hw)

        rows_of(step, count, pick)
        wcat[3 * hw :, :] = dot(swap_ref[...], wcat[: 2 * hw, :]).astype(BF)
        full[...] = dot_nt(wcat[...], a_ref[...])

        def image(i, carry):
            at = pl.ds(pl.multiple_of(i * seq, seq), seq)
            cos, sin = cos_ref[:, at], sin_ref[:, at]
            ok = lax.broadcasted_iota(jnp.int32, (seq, 1), 0) < lens[i]
            outs = []
            for h in range(heads):
                part = lambda j: full[j * hw + h * HD : j * hw + (h + 1) * HD, at]
                q = (part(0) * cos + part(3) * sin).astype(BF)
                k = (part(1) * cos + part(4) * sin).astype(BF)
                v = part(2).astype(BF)
                q_ref[0, h, :, at] = q
                k_ref[0, h, :, at] = k
                v_ref[0, h, :, at] = v
                st = jnp.where(ok, dot_tn(k, q) * scale, NEG)
                ex = jnp.exp(st - jnp.max(st, axis=0, keepdims=True))
                probs = (ex * (1.0 / jnp.sum(ex, axis=0, keepdims=True))).astype(BF)
                outs.append(dot(v, probs))
            o_ref[0, :, at] = jnp.concatenate(outs, axis=0).astype(BF)
            return carry

        lax.fori_loop(0, images, image, 0, unroll=UNROLL)

        def keep(r):
            o_all[r * hw : (r + 1) * hw, :] = o_ref[0]

        rows_of(step, count, keep)

        @pl.when(step == count - 1)
        def _():
            finish(o_all, wout, own_ref, peer_ref, seq)

    head = (shape((count, heads, HD, rows), BF), (1, heads, HD, rows), lambda z: (z, 0, 0, 0))
    return call(
        kernel,
        "attn_fwd",
        (count,),
        [(x, None, None) for x in (a_all, cos, sin, jnp.asarray(swap_matrix(2 * hw).T, BF))]
        + [(w, None, None) for w in weights],
        [
            head,
            head,
            head,
            (shape((count, hw, rows), BF), (1, hw, rows), lambda z: (z, 0, 0)),
            (shape((rows // 2, width), F32), None, None),
            (shape((rows // 2, width), BF), None, None),
        ],
        scratch=[
            pltpu.VMEM((5 * hw, width), BF),
            pltpu.VMEM((count * hw, width), BF),
            pltpu.VMEM((5 * hw, rows), F32),
            pltpu.VMEM((count * hw, rows), BF),
        ],
        scalars=(lens,),
        flops=2 * count * rows * width * 6 * hw + 8 * count * rows * heads * seq * 256,
        moved=20_000_000,
        exps=count * rows * heads * seq,
        deps=deps,
    )


def attn_bwd(lens, da_all, weights, cos, sin, q, k, v, heads, seq, deps=()):
    count, (rows, width), hw = len(weights), da_all.shape, heads * HD
    images = rows // seq
    scale = HD ** (-0.5)

    def kernel(lens, da_ref, cos_ref, sin_ref, swap_ref, q_ref, k_ref, v_ref, *refs):
        w_refs, refs = refs[:count], refs[count:]
        dqkv_ref, own_ref, peer_ref, w_all, wout, do_all, d_all = refs
        step = pl.program_id(0)

        def pick(r):
            copy_blocks(w_refs[r], (0, 1, 2), w_all, r * 3 * hw)
            copy_blocks(w_refs[r], (3,), wout, 0)

        rows_of(step, count, pick)
        do_all[...] = dot_nt(wout[...], da_ref[...])

        def image(i, carry):
            at = pl.ds(pl.multiple_of(i * seq, seq), seq)
            cos, sin = cos_ref[:, at], sin_ref[:, at]
            ok = lax.broadcasted_iota(jnp.int32, (seq, 1), 0) < lens[i]
            dqs, dks, dvs = [], [], []
            for h in range(heads):
                do = do_all[h * HD : (h + 1) * HD, at].astype(BF)
                q, k, v = q_ref[0, h, :, at], k_ref[0, h, :, at], v_ref[0, h, :, at]
                st = jnp.where(ok, dot_tn(k, q) * scale, NEG)
                dp = dot_tn(v, do)
                ex = jnp.exp(st - jnp.max(st, axis=0, keepdims=True))
                probs = ex * (1.0 / jnp.sum(ex, axis=0, keepdims=True))
                inner = jnp.sum(dp * probs, axis=0, keepdims=True)
                ds = (probs * (dp - inner)).astype(BF)
                dvs.append(dot_nt(do, probs.astype(BF)))
                dk = dot_nt(q, ds), dot_nt(dot(swap_ref[...], q).astype(BF), ds)
                dq = dot(k, ds), dot(dot(swap_ref[...], k).astype(BF), ds)
                dqs.append((dq[0] * cos - dq[1] * sin) * scale)
                dks.append((dk[0] * cos - dk[1] * sin) * scale)
            dqkv_ref[0, :, at] = jnp.concatenate(dqs + dks + dvs, axis=0).astype(BF)
            return carry

        lax.fori_loop(0, images, image, 0, unroll=UNROLL)

        def keep(r):
            d_all[r * 3 * hw : (r + 1) * 3 * hw, :] = dqkv_ref[0]

        rows_of(step, count, keep)

        @pl.when(step == count - 1)
        def _():
            finish(d_all, w_all, own_ref, peer_ref, seq)

    head = lambda x: (x, (1, heads, HD, rows), lambda z: (z, 0, 0, 0))
    return call(
        kernel,
        "attn_bwd",
        (count,),
        [(x, None, None) for x in (da_all, cos, sin, jnp.asarray(swap_matrix(HD).T, BF))]
        + [head(q), head(k), head(v)]
        + [(w, None, None) for w in weights],
        [
            (shape((count, 3 * hw, rows), BF), (1, 3 * hw, rows), lambda z: (z, 0, 0)),
            (shape((rows // 2, width), F32), None, None),
            (shape((rows // 2, width), BF), None, None),
        ],
        scratch=[
            pltpu.VMEM((count * 3 * hw, width), BF),
            pltpu.VMEM((hw, width), BF),
            pltpu.VMEM((hw, rows), F32),
            pltpu.VMEM((count * 3 * hw, rows), BF),
        ],
        scalars=(lens,),
        flops=2 * count * rows * width * 4 * hw + 20 * count * rows * heads * seq * 256,
        moved=20_000_000,
        exps=count * rows * heads * seq,
        deps=deps,
    )


def tiles(total, tile, body):
    def step(i, carry):
        body(pl.ds(pl.multiple_of(i * tile, tile), tile))
        return carry

    lax.fori_loop(0, total // tile, step, 0)


def mlp_fwd(a_all, weights, deps=()):
    count, (rows, width) = len(weights), a_all.shape
    cols = weights[0].shape[0] * weights[0].shape[1]
    units = cols // 2

    def kernel(a_ref, *refs):
        w_refs, (gu_ref, hid_ref, wcat) = refs[:count], refs[count:]
        pick_weight(pl.program_id(0), w_refs, wcat)

        def block(at):
            gu = dot_nt(a_ref[at, :], wcat[...])
            gu_ref[0, at, :] = gu
            g, u = gu[:, :units], gu[:, units:]
            hid_ref[0, at, :] = (g * jax.nn.sigmoid(g) * u).astype(BF)

        tiles(rows, 256, block)

    each = lambda z: (z, 0, 0)
    return call(
        kernel,
        "mlp_fwd",
        (count,),
        [(a_all, None, None)] + [(w, None, None) for w in weights],
        [
            (shape((count, rows, cols), F32), (1, rows, cols), each),
            (shape((count, rows, units), BF), (1, rows, units), each),
        ],
        scratch=[pltpu.VMEM((cols, width), BF)],
        flops=2 * count * rows * width * cols,
        moved=26_000_000,
        exps=count * rows * units,
        deps=deps,
    )


def mlp_bwd(dm_all, downs, gus, gate_up, deps=()):
    count, (rows, width) = len(gus), dm_all.shape
    cols = gus[0].shape[0] * gus[0].shape[1]
    units = cols // 2

    def kernel(dm_ref, gu_ref, *refs):
        d_refs, g_refs, refs = refs[:count], refs[count : 2 * count], refs[2 * count :]
        dgu_ref, own_ref, peer_ref, wd, wgu, acc = refs
        step = pl.program_id(0)
        pick_weight(step, d_refs, wd)
        pick_weight(step, g_refs, wgu)

        def block(at):
            dhid = dot_nt(dm_ref[at, :], wd[...])
            g, u = gu_ref[0, at, :units], gu_ref[0, at, units:]
            sig = jax.nn.sigmoid(g)
            dg = dhid * u * sig * (1.0 + g * (1.0 - sig))
            du = dhid * g * sig
            low = jnp.concatenate([dg, du], axis=1).astype(BF)
            dgu_ref[0, at, :] = low
            add_into(step, acc, at, dot(low, wgu[...]))

        tiles(rows, 256, block)
        hand_out(acc, own_ref, peer_ref)

    each = lambda z: (z, 0, 0)
    return call(
        kernel,
        "mlp_bwd",
        (count,),
        [(dm_all, None, None), (gate_up, (1, rows, cols), each)]
        + [(w, None, None) for w in downs + gus],
        [
            (shape((count, rows, cols), BF), (1, rows, cols), each),
            (shape((rows // 2, width), F32), None, None),
            (shape((rows // 2, width), BF), None, None),
        ],
        scratch=[
            pltpu.VMEM((units, width), BF),
            pltpu.VMEM((cols, width), BF),
            pltpu.VMEM((rows, width), F32),
        ],
        flops=3 * count * rows * width * cols,
        moved=30_000_000,
        exps=count * rows * units,
        deps=deps,
    )


def mlp_out(hidden, downs, deps=()):
    count, rows, units = hidden.shape
    width = downs[0].shape[2]

    def kernel(hid_ref, *refs):
        d_refs, (own_ref, peer_ref, wd, acc) = refs[:count], refs[count:]
        step = pl.program_id(0)
        pick_weight(step, d_refs, wd)
        tiles(rows, 256, lambda at: add_into(step, acc, at, dot(hid_ref[0, at, :], wd[...])))
        hand_out(acc, own_ref, peer_ref)

    return call(
        kernel,
        "mlp_out",
        (count,),
        [(hidden, (1, rows, units), lambda z: (z, 0, 0))] + [(w, None, None) for w in downs],
        [
            (shape((rows // 2, width), F32), None, None),
            (shape((rows // 2, width), BF), None, None),
        ],
        scratch=[pltpu.VMEM((units, width), BF), pltpu.VMEM((rows, width), F32)],
        flops=2 * count * rows * width * units,
        moved=12_000_000,
        deps=deps,
    )


ROLES = ((1, 3), (0, 2), (2, 3), (0, 1))


def grad_split(place, pairs, deps=()):
    rows, width = pairs[0][0].shape
    count = pairs[0][1].shape[0]
    last = [right.shape[2] == rows for _, right in pairs]
    widths = [right.shape[1 if flip else 2] for (_, right), flip in zip(pairs, last)]
    cols, strip = sum(widths), width // 8

    def kernel(place, *refs):
        n = len(pairs)
        lefts, rights, outs, refs = refs[:n], refs[n : 2 * n], refs[2 * n : 2 * n + 4], refs[2 * n + 4 :]
        turned, res = refs[:n], refs[n]

        @pl.when(pl.program_id(0) == 0)
        def _():
            for left, lt in zip(lefts, turned):
                lt[...] = left[...].T

        begin = 0
        for lt, right, size, flip in zip(turned, rights, widths, last):
            part = dot_nt(lt[...], right[0]) if flip else dot(lt[...], right[0])
            res[:, begin : begin + size] = part
            begin += size
        for core, ref, blocks in zip((0, 0, 1, 1), outs, ROLES):
            for j, rel in enumerate(blocks):
                first = ((place[0] ^ rel) * 2 + (place[1] ^ core)) * strip
                ref[0, j] = res[pl.ds(pl.multiple_of(first, 16), strip), :].astype(BF)

    return call(
        kernel,
        "grad_split",
        (count,),
        [(left, None, None) for left, _ in pairs]
        + [(right, (1,) + right.shape[1:], lambda z: (z, 0, 0)) for _, right in pairs],
        [(shape((count, 2, strip, cols), BF), (1, 2, strip, cols), lambda z: (z, 0, 0, 0))] * 4,
        scratch=[pltpu.VMEM((width, rows), BF)] * len(pairs) + [pltpu.VMEM((width, cols), F32)],
        scalars=(place,),
        flops=2 * count * rows * width * cols,
        moved=2 * rows * width + 2 * count * rows * cols + 2 * count * width * cols,
        deps=deps,
    )


def assemble(place, near, first_x, second_y, first_y, second_x, deps=()):
    part, width = near.shape
    half = first_x.shape[0]

    def kernel(place, near, fx, sy, fy, sx, out):
        q = place[0]
        out[q] = near[...]
        out[q ^ 1, :half] = fx[...]
        out[q ^ 1, half:] = sx[0]
        out[q ^ 2, :half] = fy[0]
        out[q ^ 2, half:] = sy[...]
        out[q ^ 3, :half] = fy[1]
        out[q ^ 3, half:] = sx[1]

    return call(
        kernel,
        "assemble",
        (1,),
        [(x, None, None) for x in (near, first_x, second_y, first_y, second_x)],
        [(shape((4, part, width), BF), None, None)],
        scalars=(place,),
        moved=16 * part * width,
        deps=deps,
    )[0]


def norm(x):
    centered = x - jnp.mean(x, axis=-1, keepdims=True)
    inverse = lax.rsqrt(jnp.mean(centered * centered, axis=-1, keepdims=True) + EPSILON)
    return centered * inverse, inverse


def norm_back(d_normed, normed, inverse, scale):
    d_hat = d_normed * (1.0 + scale)
    return inverse * (
        d_hat
        - jnp.mean(d_hat, axis=-1, keepdims=True)
        - normed * jnp.mean(d_hat * normed, axis=-1, keepdims=True)
    )


def total(x):
    return jnp.sum(x, axis=0, keepdims=True)


SHIFT_ONE, SCALE_ONE, GATE_ONE, SHIFT_TWO, SCALE_TWO, GATE_TWO = range(6)


def by_image(body, name, lengths, mod, rows_in, bias, outs, sums, deps=()):
    images, _, width = mod.shape
    seq = rows_in[0].shape[0] // images
    count = len(rows_in)

    def kernel(lens, mod_ref, bias_ref, *refs):
        row_id = lax.broadcasted_iota(jnp.int32, (seq, 1), 0)
        mask = jnp.where(row_id < lens[pl.program_id(0)], 1.0, 0.0).astype(F32)
        values = [ref[...].astype(F32) for ref in refs[:count]]
        got = body(mask, [mod_ref[0, j : j + 1, :] for j in range(6)], bias_ref[...], *values)
        for ref, value in zip(refs[count:-1], got):
            ref[...] = value.astype(ref.dtype)
        for j, value in enumerate(got[len(outs) :]):
            refs[-1][0, j : j + 1, :] = value

    block = ((seq, width), lambda i: (i, 0))
    return call(
        kernel,
        name,
        (images,),
        [(mod, (1, 6, width), lambda i: (i, 0, 0)), (bias, None, None)]
        + [(x,) + block for x in rows_in],
        [(shape(rows_in[0].shape, dtype),) + block for dtype in outs]
        + [(shape((images, sums, width), F32), (1, sums, width), lambda i: (i, 0, 0))],
        scalars=(lengths,),
        flops=30 * seq * width * images,
        moved=sum(x.size * x.dtype.itemsize for x in rows_in) + 4 * seq * width * images,
        deps=deps,
    )


def pre_attention(mask, mod, bias, x, upstream):
    normed, _ = norm(x)
    dm = mask * mod[GATE_TWO] * upstream
    return normed * (1.0 + mod[SCALE_ONE]) + mod[SHIFT_ONE], dm, total(dm), total(mask * x * x)


def pre_mlp(mask, mod, bias, x, att_own, att_peer):
    gated = mask * mod[GATE_ONE] * (att_own + att_peer + bias)
    residual = x + gated
    normed, _ = norm(residual)
    return residual, normed * (1.0 + mod[SCALE_TWO]) + mod[SHIFT_TWO], total(gated * gated)


def post_mlp(mask, mod, bias, residual, upstream, mlp_own, mlp_peer):
    branch = mlp_own + mlp_peer + bias
    gated = mask * mod[GATE_TWO] * branch
    return residual + gated, total(mask * branch * upstream), total(gated * gated)


def back_mlp(mask, mod, bias, residual, upstream, att_own, att_peer, da_own, da_peer):
    normed, inverse = norm(residual)
    da = da_own + da_peer
    dh = upstream + norm_back(da, normed, inverse, mod[SCALE_TWO])
    d_att = mask * mod[GATE_ONE] * dh
    branch = att_own + att_peer + bias
    return dh, d_att, total(mask * branch * dh), total(da), total(da * normed), total(d_att)


def back_attention(mask, mod, bias, x, dh, da_own, da_peer):
    normed, inverse = norm(x)
    da = da_own + da_peer
    return dh + norm_back(da, normed, inverse, mod[SCALE_ONE]), total(da), total(da * normed)


def ring(count, shift):
    return [(i, (i + shift) % count) for i in range(count)]


def take(array, index, axis):
    return lax.dynamic_index_in_dim(array, index, axis, keepdims=False)


def local(
    sizes,
    patches,
    conditioning,
    time_bins,
    lengths,
    positions,
    time_table,
    w_ada,
    b_ada,
    w_qkv,
    w_out,
    branch_bias,
    w_gu,
    w_down,
    d_out,
):
    axes = tuple(sizes)
    ny, nx, nc, tn = sizes.values()
    square = nx == 2 and ny == 2
    at_y, at_x, at_c, at_z = (lax.axis_index(name) for name in axes)
    at_q = at_y * nx + at_x
    devices = ny * nx * nc * tn
    image_count, width = conditioning.shape
    rows = patches.shape[0]
    seq = rows // image_count
    heads = w_qkv.shape[2] // HD // nc
    hw = heads * HD
    units = w_gu.shape[2] // nc
    strip = width // (ny * nx * nc)
    place = jnp.stack([at_q, at_c]).astype(jnp.int32)
    swap = ring(2, 1)

    def peer(value):
        return lax.ppermute(value, "c", ring(nc, 1))

    def core_share(weight, axis):
        size = weight.shape[axis] // nc
        return lax.dynamic_slice_in_dim(weight, at_c * size, size, axis)

    def after(value, *others):
        return lax.optimization_barrier((value, others))[0] if others else value

    flow = {"z": [], "plane": []}

    def weight_gather(base, batches):
        if not square:
            flat = base.reshape(ny * nx, -1, width)
            piece = take(flat, at_q, 0)
            got = [lax.ppermute(piece, "z", ring(tn, r)) for r in range(1, tn)]
            whole = lax.all_gather(jnp.stack(got), ("y", "x"), axis=1)
            return [base] + [whole[r].reshape(base.shape) for r in range(tn - 1)]
        part = base.shape[1]
        half = part // 32 * 16
        piece = after(take(base, at_q, 0), *flow["z"])
        near = [lax.ppermute(piece, "z", ring(tn, r)) for r in range(1, tn)]
        flow["z"] = near
        out = [base]
        for batch in batches:
            mine = [near[r - 1] for r in batch]
            mine = after(mine, *flow["plane"])
            first = jnp.stack([x[:half] for x in mine])
            second = jnp.stack([x[half:] for x in mine])
            first_x = lax.ppermute(first, "x", swap)
            second_y = lax.ppermute(second, "y", swap)
            first_y = lax.ppermute(jnp.stack([first, first_x], axis=1), "y", swap)
            second_x = lax.ppermute(jnp.stack([second, second_y], axis=1), "x", swap)
            flow["plane"] = [first_y, second_x]
            for j in range(len(batch)):
                out.append(
                    assemble(place, mine[j], first_x[j], second_y[j], first_y[j], second_x[j])
                )
        return out

    heads_own = jnp.concatenate(
        [core_share(w_qkv.transpose(1, 2, 0), 1), core_share(w_out, 0)[None]], axis=0
    )
    heads_all = weight_gather(heads_own, ((1,), (2, 3)))
    gu_own = core_share(w_gu.transpose(1, 2, 0), 1).reshape(4, units // 2, width)
    gu_all = weight_gather(gu_own, ((1, 2, 3),))
    down_all = weight_gather(core_share(w_down, 0).reshape(4, units // 4, width), ((1, 2, 3),))

    def grad_reduce(pairs, deps=()):
        if square:
            send_a, keep_a, send_b, keep_b = grad_split(place, pairs, deps)
            got_a = lax.ppermute(send_a, "x", swap)
            got_b = lax.ppermute(send_b, "y", swap)

            def part(keep, got, j):
                return keep[:, j].astype(F32) + got[:, j].astype(F32)

            got_a2 = lax.ppermute(part(keep_a, got_a, 1).astype(BF), "y", swap)
            got_b2 = lax.ppermute(part(keep_b, got_b, 1).astype(BF), "x", swap)
            mine = part(keep_a, got_a, 0) + got_a2.astype(F32)
            other = part(keep_b, got_b, 0) + got_b2.astype(F32)
        else:
            flip = lambda right: right.swapaxes(1, 2) if right.shape[2] == 2 * rows else right
            full = jnp.concatenate(
                [
                    jnp.einsum("rd,zrn->zdn", left, flip(right), preferred_element_type=F32)
                    for left, right in pairs
                ],
                axis=2,
            )
            full = full.astype(BF).reshape(tn, ny * nx, nc, strip, -1)
            summed = lax.psum_scatter(full, ("y", "x"), scatter_dimension=1, tiled=False)
            mine = take(summed, at_c, 1).astype(F32)
            other = take(summed, 1 - at_c, 1).astype(F32)
        blocks = jnp.stack([mine, other], axis=1)
        summed = blocks[0]
        for r in range(1, tn):
            sent = blocks[r].astype(BF)
            summed = summed + lax.ppermute(sent, "z", ring(tn, -r)).astype(F32)
        got = peer(summed[1].astype(BF)).astype(F32)
        own = summed[0]
        low, high = jnp.where(at_c == 0, own, got), jnp.where(at_c == 0, got, own)
        return low, high

    bins = jnp.arange(time_table.shape[0], dtype=jnp.int32)
    onehot = (time_bins[:, None] == bins[None, :]).astype(F32)
    cond_vec = conditioning + jnp.dot(onehot, time_table, precision=EXACT)
    cond_sig = jax.nn.sigmoid(cond_vec)
    silu_low = (cond_vec * cond_sig).astype(BF)
    mod = (dot(silu_low, w_ada) + b_ada).reshape(image_count, 6, width)
    bias_attn, bias_mlp = branch_bias[None, :width], branch_bias[None, width:]
    elementwise = functools.partial(by_image, lengths=lengths, mod=mod)
    a1_own, dm_own, sums_pre = elementwise(
        pre_attention, "pre_attention", rows_in=(patches, d_out), bias=bias_attn, outs=(BF, BF), sums=2
    )
    a1_all = jnp.concatenate([a1_own, peer(a1_own)], axis=0)
    dm_all = jnp.concatenate([dm_own, peer(dm_own)], axis=0)
    facts = jnp.concatenate([positions.reshape(-1), lengths])
    facts_peer = peer(facts)
    lens = jnp.concatenate([lengths, facts_peer[2 * rows :]])
    pos = jnp.concatenate([positions, facts_peer[: 2 * rows].reshape(2, rows)], axis=1).astype(F32)
    quarter = HD // 4
    frequency = 10000.0 ** (-jnp.arange(quarter, dtype=F32) / quarter)
    angle = pos[:, None, :] * frequency[None, :, None]
    cosine, sine = jnp.cos(angle), jnp.sin(angle)
    cos = jnp.concatenate([cosine[0], cosine[0], cosine[1], cosine[1]], axis=0)
    sin = jnp.concatenate([sine[0], sine[0], sine[1], sine[1]], axis=0)

    q, k, v, attended, att_own, att_peer = attn_fwd(
        lens, a1_all, heads_all, cos, sin, heads, seq
    )
    att = (att_own, peer(att_peer))
    residual, a2_own, sums_att = elementwise(
        pre_mlp, "pre_mlp", rows_in=(patches,) + att, bias=bias_attn, outs=(F32, BF), sums=1
    )
    a2_all = jnp.concatenate([a2_own, peer(a2_own)], axis=0)

    gate_up, hidden = mlp_fwd(a2_all, gu_all)
    down_low, down_high = grad_reduce([(dm_all, hidden)])
    d_gate_up, da2_own, da2_peer = mlp_bwd(dm_all, down_all, gu_all, gate_up)
    gu_low, gu_high = grad_reduce([(a2_all, d_gate_up)])
    dh, da_own, sums_back = elementwise(
        back_mlp,
        "back_mlp",
        rows_in=(residual, d_out) + att + (da2_own, peer(da2_peer)),
        bias=bias_attn,
        outs=(F32, BF),
        sums=4,
    )
    da_all = jnp.concatenate([da_own, peer(da_own)], axis=0)
    mlp_own, mlp_peer = mlp_out(hidden, down_all)
    output, sums_mlp = elementwise(
        post_mlp,
        "post_mlp",
        rows_in=(residual, d_out, mlp_own, peer(mlp_peer)),
        bias=bias_mlp,
        outs=(F32,),
        sums=2,
    )

    d_qkv, da1_own, da1_peer = attn_bwd(
        lens, da_all, heads_all, cos, sin, q, k, v, heads, seq
    )
    heads_low, heads_high = grad_reduce([(a1_all, d_qkv), (da_all, attended)])
    d_inputs, sums_one = elementwise(
        back_attention,
        "back_attention",
        rows_in=(patches, dh, da1_own, peer(da1_peer)),
        bias=bias_attn,
        outs=(F32,),
        sums=2,
    )

    d_mod = jnp.concatenate([sums_one, sums_back[:, :3], sums_mlp[:, :1]], axis=1)
    d_mod = d_mod.reshape(image_count, 6 * width)
    d_silu = dot_nt(d_mod.astype(BF), w_ada)
    d_cond = d_silu * cond_sig * (1.0 + cond_vec * (1.0 - cond_sig))
    d_bias = jnp.concatenate([jnp.sum(sums_back[:, 3], axis=0), jnp.sum(sums_pre[:, 0], axis=0)])
    sums = jnp.stack(
        [
            jnp.sum(sums_pre[:, 1]),
            jnp.sum(sums_att),
            jnp.sum(sums_mlp[:, 1]),
            jnp.sum(lengths).astype(F32),
        ]
    )
    ada_cols, bias_cols = 6 * width // devices, 2 * width // devices
    message = jnp.concatenate(
        [
            d_mod.reshape(image_count, devices, ada_cols).transpose(1, 0, 2).reshape(devices, -1),
            d_bias.reshape(devices, bias_cols),
            jnp.broadcast_to(sums[None], (devices, 4)),
        ],
        axis=1,
    )
    arrived = lax.all_to_all(message, axes, 0, 0, tiled=True)
    d_mod_all = arrived[:, : image_count * ada_cols].reshape(devices * image_count, ada_cols)
    rest = jnp.sum(arrived[:, image_count * ada_cols :], axis=0)
    grad_b_ada = jnp.sum(d_mod_all, axis=0)
    grad_bias = rest[:bias_cols]
    sums_all = rest[bias_cols:]
    rms_values = jnp.sqrt(sums_all[:3] / (sums_all[3] * width))
    facts = jnp.concatenate([d_cond, silu_low.astype(F32), time_bins[:, None].astype(F32)], axis=1)
    facts = jnp.broadcast_to(facts[None], (devices,) + facts.shape)
    facts_all = lax.all_to_all(facts, axes, 0, 0, tiled=True).reshape(devices * image_count, -1)
    d_cond_all, silu_all = facts_all[:, :width], facts_all[:, width : 2 * width].astype(BF)
    bins_all = facts_all[:, 2 * width].astype(jnp.int32)
    grad_ada = dot_tn(silu_all, d_mod_all.astype(BF))
    table_rows = time_table.shape[0] // devices
    flat = (at_q * nc + at_c) * tn + at_z
    own_bins = flat * table_rows + jnp.arange(table_rows, dtype=jnp.int32)
    picks = (own_bins[:, None] == bins_all[None, :]).astype(F32)
    grad_table = jnp.dot(picks, d_cond_all, precision=EXACT)

    def halves(low, high, parts):
        both = [value.reshape(strip, parts, -1) for value in (low, high)]
        return jnp.concatenate(both, axis=2)

    return (
        output,
        d_inputs,
        d_cond,
        halves(heads_low[:, : 3 * hw], heads_high[:, : 3 * hw], 3),
        halves(heads_low[:, 3 * hw :], heads_high[:, 3 * hw :], 1)[:, 0].T,
        halves(gu_low, gu_high, 2),
        halves(down_low, down_high, 1)[:, 0].T,
        grad_ada,
        grad_b_ada,
        grad_bias,
        grad_table,
        rms_values,
    )


def solution(mesh):
    groups, tn = mesh.shape["dp"], mesh.shape["tensor"]
    nc, nx = 2, 2
    sizes = {"y": groups // (nx * nc), "x": nx, "c": nc, "z": tn}
    fine = Mesh(mesh.devices.reshape(tuple(sizes.values())), tuple(sizes))
    dp = ("y", "x", "c")
    every = dp + ("z",)
    return jax.shard_map(
        functools.partial(local, sizes),
        mesh=fine,
        in_specs=(
            P(every, None),
            P(every, None),
            P(every),
            P(every),
            P(None, every),
            P(),
            P(),
            P(),
            P(None, None, "z"),
            P("z", None),
            P(),
            P(None, None, "z"),
            P("z", None),
            P(every, None),
        ),
        out_specs=(
            P(every, None),
            P(every, None),
            P(every, None),
            P(dp, None, "z"),
            P("z", dp),
            P(dp, None, "z"),
            P("z", dp),
            P(None, every),
            P(every),
            P(every),
            P(every, None),
            P(),
        ),
        check_vma=False,
    )
```

time: 1480 us -> 614 us (0.41)
  waiting for transfers between devices: 1090 us -> 164 us
  Pallas kernels: 0 us -> 220 us
  matrix products: 158 us -> 23.5 us
  blocking collectives: 66.2 us -> 0 us
  starting transfers between devices: 1.33 us -> 65.9 us
  other arithmetic: 67 us -> 50.6 us
    reduce_scatter x9 -> x0, waiting for transfers between devices: 463 us -> none  [the longest x1 84.6 us: local(): lax.psum_scatter(jnp.dot(hidden, w_down, preferred_element_type=jnp.float...]
    unnamed x15 -> x0, waiting for transfers between devices: 320 us -> none
    all_gather x4 -> x0, waiting for transfers between devices: 306 us -> none  [the longest x1 89.2 us: local(): lax.all_gather(d_attn.astype(jnp.bfloat16).reshape(local_rows, model_widt...]
    pallas_call x0 -> x22, Pallas kernels: none -> 220 us  [call(): pl.pallas_call(body, grid_spec=pltpu.PrefetchScalarGridSpec(num_scalar_pr...]
    ppermute x0 -> x58, waiting for transfers between devices: none -> 150 us  [the longest x9 50 us: grad_reduce(): summed = summed + lax.ppermute(sent, 'z', ring(tn, -r)).astype(F32)]
    dot_general x22 -> x4, matrix products: 157 us -> 20.4 us  [the longest x1 9.83 us: dot_nt(): return lax.dot_general(a, b, NT, preferred_element_type=F32)]
    ppermute x0 -> x58, starting transfers between devices: none -> 58.1 us  [the longest x9 13.1 us: weight_gather(): near = [lax.ppermute(piece, 'z', ring(tn, r)) for r in range(1, tn)]]
    unnamed x2 -> x0, blocking collectives: 54 us -> none
  transfers between devices with their start and end apart: 14 -> 60, of which waited for: 14 -> 20; matrix products, arithmetic and copies ran while one was open for 10% -> 22% of each run, Pallas kernels for 0% -> 36%
where the time goes in v1:
time: 614 us; the launch traced here: 606 us
  Pallas kernels  220 us (36%)
  waiting for transfers between devices  164 us (27%)
  local copies, waits for them, and re-layouts  79 us (13%)
  starting transfers between devices  65.9 us (11%)
  other arithmetic  50.6 us (8%)
  matrix products  23.5 us (4%)
    pallas_call x22, Pallas kernels, call(): pl.pallas_call(body, grid_spec=pltpu.PrefetchScalarGridSpec(num_scalar_pr...  220 us
    ppermute x9, waiting for transfers between devices, grad_reduce(): summed = summed + lax.ppermute(sent, 'z', ring(tn, -r)).astype(F32)  50 us
    ppermute x9, waiting for transfers between devices, weight_gather(): near = [lax.ppermute(piece, 'z', ring(tn, r)) for r in range(1, tn)]  28 us
    ppermute x4, waiting for transfers between devices, weight_gather(): first_y = lax.ppermute(jnp.stack([first, first_x], axis=1), 'y', swap)  23 us
    unnamed x122, local copies, waits for them, and re-layouts  13.8 us
    ppermute x3, waiting for transfers between devices, grad_reduce(): got_b = lax.ppermute(send_b, 'y', swap)  13.7 us
    ppermute x3, waiting for transfers between devices, grad_reduce(): got_b2 = lax.ppermute(part(keep_b, got_b, 1).astype(BF), 'x', swap)  13.3 us
    all_to_all x1, waiting for transfers between devices, local(): arrived = lax.all_to_all(message, axes, 0, 0, tiled=True)  13.3 us
  transfers between devices with their start and end apart: 60, of which 20 were waited for; matrix products, arithmetic and copies ran while one was open for 22% of the time, Pallas kernels for 36%

profile of v1, /device:TPU:0, one launch (start us, length us, event | category | flops | bytes accessed | tf_op | source)
XLA Modules:
  0.0 606.0 jit_solution(13481563368200771435)
XLA Ops:
  6.7 5.0 collective-permute-start.8
  17.1 3.1 fusion.52
  20.2 8.3 %convolution_add_fusion = f32[2,6912]{1,0:T(2,128)} fusion(bf16[1152,6912]{1,0:T(8,128)(2,1)} %param.22, f32[6912]{0:T(1024)S(1)} %copy-done.45, f32[2,1152]{1,0:T(2,128)S(1)} %get-tuple-element.238), kind=kOutput, calls=%fused_computation | convolution fusion | flops 31875840 | bytes 16017408 | tf_op jit(solution)/shard_map/dot_general | solution.py:25
  35.4 5.6 copy.136
  41.9 4.8 pre_attention.1
  54.2 2.9 collective-permute-start.17
  71.2 26.2 %collective-permute-done.16.refs_1_ = bf16[192,1152]{1,0:T(8,128)(2,1)S(1)} collective-permute-done((bf16[192,1152]{1,0:T(8,128)(2,1)}, bf16[192,1152]{1,0:T(8,128)(2,1)S(1)}, u32[]{:S(2)}, u32[]{:S(2)}) %collective-permute-start.16) | collective-permute-done | bytes 442400 | tf_op jit(solution)/shard_map/ppermute | solution.py:640
  102.8 3.2 assemble.9.refs_6_.refs_9_
  111.5 8.4 %collective-permute-done.10 = bf16[2,80,1152]{2,1,0:T(8,128)(2,1)S(1)} collective-permute-done((bf16[2,80,1152]{2,1,0:T(8,128)(2,1)S(1)}, bf16[2,80,1152]{2,1,0:T(8,128)(2,1)S(1)}, u32[]{:S(2)}, u32[]{:S(2)}) %collective-permute-start.10) | collective-permute-done | bytes 368672 | tf_op jit(solution)/shard_map/ppermute | solution.py:649
  122.4 7.7 %collective-permute-done.11 = bf16[2,2,64,1152]{3,2,0,1:T(8,128)(2,1)S(1)} collective-permute-done((bf16[2,2,64,1152]{3,2,0,1:T(8,128)(2,1)S(1)}, bf16[2,2,64,1152]{3,2,0,1:T(8,128)(2,1)S(1)}, u32[]{:S(2)}, u32[]{:S(2)}) %collective-permute-start.11) | collective-permute-done | bytes 589856 | tf_op jit(solution)/shard_map/ppermute | solution.py:650
  130.9 3.3 collective-permute-done.12
  139.7 3.1 assemble.11.refs_8_.refs_11_
  142.8 3.1 assemble.10.refs_7_.refs_10_
  146.0 29.3 %attn_fwd.1 = (bf16[4,2,72,1024]{3,2,1,0:T(8,128)(2,1)}, bf16[4,2,72,1024]{3,2,1,0:T(8,128)(2,1)}, bf16[4,2,72,1024]{3,2,1,0:T(8,128)(2,1)}, bf16[4,144,1024]{2,...) custom-call(s32[4]{0:T(128)} %pad_add_fusion.1.refs_0_, bf16[1024,1152]{1,0:T(8,128)(2,1)} %copy-done.33, ...), custom_call_target="tpu_custom_call" | custom-call | flops 12448694272 | bytes 20000000 | tf_op jit(solution)/shard_map/attn_fwd/pallas_call | solution.py:51
  183.7 5.0 pre_mlp.1
  193.1 15.3 %collective-permute-done.20 = bf16[3,2,96,1152]{3,2,0,1:T(8,128)(2,1)S(1)} collective-permute-done((bf16[3,2,96,1152]{3,2,0,1:T(8,128)(2,1)}, bf16[3,2,96,1152]{3,2,0,1:T(8,128)(2,1)S(1)}, u32[]{:S(2)}, u32[]{:S(2)}) %collective-permute-start.20) | collective-permute-done | bytes 1327136 | tf_op jit(solution)/shard_map/ppermute | solution.py:650
  217.0 3.5 assemble.14.refs_4_.refs_9_
  220.5 3.5 assemble.13.refs_3_.refs_8_
  223.9 3.5 assemble.12.refs_2_.refs_7_
  235.0 17.7 %mlp_fwd.1 = (f32[4,1024,768]{2,1,0:T(8,128)}, bf16[4,1024,384]{2,1,0:T(8,128)(2,1)}) custom-call(bf16[1024,1152]{1,0:T(8,128)(2,1)} %constant_dynamic-update-slice_fusion.2.refs_0_.refs_1_, bf16[4,192,1152]{2,1,0:T(8,128)(2,1)} %bitcast.349, bf16[4,192,1152]{2,1,0:T(8,128)(2,1)} %assemble.12.refs_2_.refs_7_, ...), custom_call_target="tpu_custom_call" | custom-call | flops 7247757312 | bytes 26000000 | tf_op jit(solution)/shard_map/mlp_fwd/pallas_call | solution.py:51
  252.7 10.1 %grad_split.5 = (bf16[4,2,144,384]{3,2,1,0:T(8,128)(2,1)}, bf16[4,2,144,384]{3,2,1,0:T(8,128)(2,1)}, bf16[4,2,144,384]{3,2,1,0:T(8,128)(2,1)}, bf16[4,2,144,384]{3,2,1,0:T(8,128)(2,1)}) custom-call(s32[2]{0:T(128)} %pad_add_fusion.2.refs_0_, bf16[1024,1152]{1,0:T(8,128)(2,1)} %copy-done.31, bf16[4,1024,384]{2,1,0:T(8,128)(2,1)} %get-tuple-element.74.refs_0_.refs_2_), custom_call_target="tpu_custom_call" | custom-call | flops 3623878656 | bytes 9043968 | tf_op jit(solution)/shard_map/grad_split/pallas_call | solution.py:51
  268.4 2.9 assemble.17.refs_4_.refs_5_
  271.3 2.9 assemble.16.refs_3_.refs_4_
  274.2 2.9 assemble.15.refs_2_.refs_3_
  277.1 30.1 %mlp_bwd.1 = (bf16[4,1024,768]{2,1,0:T(8,128)(2,1)}, f32[512,1152]{1,0:T(8,128)}, bf16[512,1152]{1,0:T(8,128)(2,1)}) custom-call(bf16[1024,1152]{1,0:T(8,128)(2,1)} %copy-done.31, f32[4,1024,768]{2,1,0:T(8,128)} %get-tuple-element.83.refs_1_, bf16[4,96,1152]{2,1,0:T(8,128)(2,1)} %bitcast.357, bf16[4,96,1152]{2,1,0:T(8,128)(2,1)} %assemble.15.refs_2_.refs_3_, ...), custom_call_target="tpu_custom_call" | custom-call | flops 10871635968 | bytes 30000000 | tf_op jit(solution)/shard_map/mlp_bwd/pallas_call | solution.py:51
  309.4 13.4 %grad_split.4 = (bf16[4,2,144,768]{3,2,1,0:T(8,128)(2,1)}, bf16[4,2,144,768]{3,2,1,0:T(8,128)(2,1)}, bf16[4,2,144,768]{3,2,1,0:T(8,128)(2,1)}, bf16[4,2,144,768]{3,2,1,0:T(8,128)(2,1)}) custom-call(s32[2]{0:T(128)} %pad_add_fusion.2.refs_0_, bf16[1024,1152]{1,0:T(8,128)(2,1)} %constant_dynamic-update-slice_fusion.2.refs_0_.refs_1_, ...), custom_call_target="tpu_custom_call" | custom-call | flops 7247757312 | bytes 15728640 | tf_op jit(solution)/shard_map/grad_split/pallas_call | solution.py:51
  322.9 2.8 copy.154
  328.7 4.9 collective-permute-start.54
  333.6 13.9 %mlp_out.1 = (f32[512,1152]{1,0:T(8,128)}, bf16[512,1152]{1,0:T(8,128)(2,1)}) custom-call(bf16[4,1024,384]{2,1,0:T(8,128)(2,1)} %get-tuple-element.74.refs_0_.refs_2_, bf16[4,96,1152]{2,1,0:T(8,128)(2,1)} %bitcast.358, bf16[4,96,1152]{2,1,0:T(8,128)(2,1)} %assemble.15.refs_2_.refs_3_, bf16[4,96,1152]{2,1,0:T(8,128)(2,1)} %assemble.16.refs_3_.refs_4_, ...), custom_call_target="tpu_custom_call" | custom-call | flops 3623878656 | bytes 12000000 | tf_op jit(solution)/shard_map/mlp_out/pallas_call | solution.py:51
  353.2 5.4 collective-permute-done.56
  361.2 5.0 collective-permute-done.55
  372.0 8.1 %back_mlp.1 = (f32[512,1152]{1,0:T(8,128)}, bf16[512,1152]{1,0:T(8,128)(2,1)}, f32[2,4,1152]{2,1,0:T(4,128)}) custom-call(s32[2]{0:T(128)} %refs_0_.9, f32[2,6,1152]{2,1,0:T(8,128)} %reshape.170.refs_1_, f32[1,1152]{1,0:T(1,128)} %broadcast_in_dim.11.refs_2_, f32[512,1152]{1,0:T(8,128)} %get-tuple-element.68.refs_3_, f32[512,1152]{1,0:T(8,128)} %refs_4_.7, ...), custom_call_target="tpu_custom_call" | custom-call | flops 17694720 | bytes 14155776 | tf_op jit(solution)/shard_map/back_mlp/pallas_call | solution.py:51
  380.6 5.6 post_mlp.1
  395.9 3.8 collective-permute-done.42
  403.0 13.3 %collective-permute-done.45 = bf16[4,144,768]{2,1,0:T(8,128)(2,1)} collective-permute-done((bf16[4,144,768]{2,1,0:T(8,128)(2,1)}, bf16[4,144,768]{2,1,0:T(8,128)(2,1)}, u32[]{:S(2)}, u32[]{:S(2)}) %collective-permute-start.45) | collective-permute-done | bytes 884768 | tf_op jit(solution)/shard_map/ppermute | solution.py:677
  422.8 32.2 %attn_bwd.1 = (bf16[4,432,1024]{2,1,0:T(8,128)(2,1)}, f32[512,1152]{1,0:T(8,128)}, bf16[512,1152]{1,0:T(8,128)(2,1)}) custom-call(s32[4]{0:T(128)} %pad_add_fusion.1.refs_0_, bf16[1024,1152]{1,0:T(8,128)(2,1)} %copy-done.34, f32[72,1024]{1,0:T(8,128)} %pad_maximum_fusion.18.refs_2_, f32[72,1024]{1,0:T(8,128)} %pad_maximum_fusion.19.refs_3_, ...), custom_call_target="tpu_custom_call" | custom-call | flops 16173236224 | bytes 20000000 | tf_op jit(solution)/shard_map/attn_bwd/pallas_call | solution.py:51
  455.1 2.8 collective-permute-done.47
  458.2 15.2 %grad_split.3 = (bf16[4,2,144,576]{3,2,1,0:T(8,128)(2,1)}, bf16[4,2,144,576]{3,2,1,0:T(8,128)(2,1)}, bf16[4,2,144,576]{3,2,1,0:T(8,128)(2,1)}, bf16[4,2,144,576]{3,2,1,0:T(8,128)(2,1)}) custom-call(s32[2]{0:T(128)} %pad_add_fusion.2.refs_0_, bf16[1024,1152]{1,0:T(8,128)(2,1)} %copy-done.33, bf16[1024,1152]{1,0:T(8,128)(2,1)} %copy-done.34, ...), custom_call_target="tpu_custom_call" | custom-call | flops 5435817984 | bytes 12386304 | tf_op jit(solution)/shard_map/grad_split/pallas_call | solution.py:51
  480.6 6.3 %back_attention.1 = (f32[512,1152]{1,0:T(8,128)}, f32[2,2,1152]{2,1,0:T(2,128)}) custom-call(s32[2]{0:T(128)} %refs_0_.9, f32[2,6,1152]{2,1,0:T(8,128)} %reshape.170.refs_1_, f32[1,1152]{1,0:T(1,128)} %broadcast_in_dim.11.refs_2_, f32[512,1152]{1,0:T(8,128)} %refs_3_.5, f32[512,1152]{1,0:T(8,128)} %get-tuple-element.86.refs_4_, ...), custom_call_target="tpu_custom_call" | custom-call | flops 17694720 | bytes 10616832 | tf_op jit(solution)/shard_map/back_attention/pallas_call | solution.py:51
  488.8 9.8 %fusion.2 = f32[2,1152]{1,0:T(2,128)S(1)} fusion(bf16[2,6912]{1,0:T(2,128)(2,1)S(1)} %bitcast.373, bf16[1152,6912]{1,0:T(8,128)(2,1)} %param.22, f32[2,1152]{1,0:T(2,128)S(1)} %get-tuple-element.238), kind=kOutput, calls=%fused_computation.11 | convolution fusion | flops 31868928 | bytes 15971328 | tf_op jit(solution)/shard_map/dot_general | solution.py:29
  498.6 13.7 %collective-permute-done.36 = bf16[4,2,144,576]{3,2,0,1:T(8,128)(2,1)} collective-permute-done((bf16[4,2,144,576]{3,2,0,1:T(8,128)(2,1)}, bf16[4,2,144,576]{3,2,0,1:T(8,128)(2,1)}, u32[]{:S(2)}, u32[]{:S(2)}) %collective-permute-start.36) | collective-permute-done | bytes 1327136 | tf_op jit(solution)/shard_map/ppermute | solution.py:671
  518.9 4.4 all-to-all-start.1
  523.4 13.3 %all-to-all-done.1 = f32[32,1,508]{2,1,0:T(1,128)S(1)} async-done(((f32[32,1,508]{2,1,0:T(1,128)}), f32[32,1,508]{2,1,0:T(1,128)S(1)}, u32[]{:S(2)}, u32[]{:S(2)}) %all-to-all-start.1) | async-done | bytes 65056 | tf_op jit(solution)/shard_map/all_to_all | solution.py:794
  537.6 3.4 all-to-all-start
  545.6 3.6 collective-permute-start.38
  552.9 8.8 %collective-permute-done.38 = bf16[2,144,576]{2,1,0:T(8,128)(2,1)S(1)} collective-permute-done((bf16[2,144,576]{2,1,0:T(8,128)(2,1)}, bf16[2,144,576]{2,1,0:T(8,128)(2,1)S(1)}, u32[]{:S(2)}, u32[]{:S(2)}) %collective-permute-start.38) | collective-permute-done | bytes 331808 | tf_op jit(solution)/shard_map/ppermute | solution.py:697
  561.6 10.4 %collective-permute-done.40 = bf16[2,144,576]{2,1,0:T(8,128)(2,1)} collective-permute-done((bf16[2,144,576]{2,1,0:T(8,128)(2,1)}, bf16[2,144,576]{2,1,0:T(8,128)(2,1)}, u32[]{:S(2)}, u32[]{:S(2)}) %collective-permute-start.40) | collective-permute-done | bytes 331808 | tf_op jit(solution)/shard_map/ppermute | solution.py:697
  572.1 17.6 %collective-permute-done.39 = bf16[2,144,576]{2,1,0:T(8,128)(2,1)} collective-permute-done((bf16[2,144,576]{2,1,0:T(8,128)(2,1)}, bf16[2,144,576]{2,1,0:T(8,128)(2,1)}, u32[]{:S(2)}, u32[]{:S(2)}) %collective-permute-start.39) | collective-permute-done | bytes 331808 | tf_op jit(solution)/shard_map/ppermute | solution.py:697
  (358 shorter events, 173.7 us)
Async XLA Ops:
  6.7 47.5 %collective-permute-start.8 = (bf16[144,1152]{1,0:T(8,128)(2,1)}, bf16[144,1152]{1,0:T(8,128)(2,1)}, u32[]{:S(2)}, u32[]{:S(2)}) collective-permute-start(bf16[144,1152]{1,0:T(8,128)(2,1)} %fusion.35), channel_id=1, source_target_pairs={{0,3},{1,0},{2,1},{3,2},{4,7},{5,4},{6,5},{7,6},{8,11},{9,8},{10,9... | collective-permute-start | bytes 995336 | tf_op jit(solution)/shard_map/ppermute | solution.py:640
  11.8 42.4 %collective-permute-start.7 = (bf16[144,1152]{1,0:T(8,128)(2,1)}, bf16[144,1152]{1,0:T(8,128)(2,1)}, u32[]{:S(2)}, u32[]{:S(2)}) collective-permute-start(bf16[144,1152]{1,0:T(8,128)(2,1)} %fusion.35), channel_id=1, source_target_pairs={{0,2},{1,3},{2,0},{3,1},{4,6},{5,7},{6,4},{7,5},{8,10},{9,11},{10,... | collective-permute-start | bytes 995336 | tf_op jit(solution)/shard_map/ppermute | solution.py:640
  11.8 42.4 %collective-permute-start.2 = (bf16[144,1152]{1,0:T(8,128)(2,1)}, bf16[144,1152]{1,0:T(8,128)(2,1)}, u32[]{:S(2)}, u32[]{:S(2)}) collective-permute-start(bf16[144,1152]{1,0:T(8,128)(2,1)} %fusion.35), channel_id=1, source_target_pairs={{0,1},{1,2},{2,3},{3,0},{4,5},{5,6},{6,7},{7,4},{8,9},{9,10},{10,1... | collective-permute-start | bytes 995336 | tf_op jit(solution)/shard_map/ppermute | solution.py:640
  14.1 37.9 %collective-permute-start = (s32[1026]{0:T(1024)}, s32[1026]{0:T(1024)}, u32[]{:S(2)}, u32[]{:S(2)}) collective-permute-start(s32[1026]{0:T(1024)} %pad_add_fusion), channel_id=1, source_target_pairs={{0,4},{4,0},{1,5},{5,1},{2,6},{6,2},{3,7},{7,3},{8,12},{12,8},{9,1... | collective-permute-start | bytes 12320 | tf_op jit(solution)/shard_map/ppermute | solution.py:619
  54.2 16.9 %collective-permute-start.17 = (bf16[192,1152]{1,0:T(8,128)(2,1)}, bf16[192,1152]{1,0:T(8,128)(2,1)S(1)}, u32[]{:S(2)}, u32[]{:S(2)}) collective-permute-start(bf16[192,1152]{1,0:T(8,128)(2,1)} %dynamic-slice_bitcast_fusion.2), channel_id=1, source_target_pairs={{0,3},{1,0},{2,1},{3,2},{4,7},{5,4},{6,5},{7,6},{8,11},{9,8},{10,9... | collective-permute-start | bytes 1327112 | tf_op jit(solution)/shard_map/ppermute | solution.py:640
  57.1 40.3 %collective-permute-start.16 = (bf16[192,1152]{1,0:T(8,128)(2,1)}, bf16[192,1152]{1,0:T(8,128)(2,1)S(1)}, u32[]{:S(2)}, u32[]{:S(2)}) collective-permute-start(bf16[192,1152]{1,0:T(8,128)(2,1)} %dynamic-slice_bitcast_fusion.2), channel_id=1, source_target_pairs={{0,2},{1,3},{2,0},{3,1},{4,6},{5,7},{6,4},{7,5},{8,10},{9,11},{10,... | collective-permute-start | bytes 1327112 | tf_op jit(solution)/shard_map/ppermute | solution.py:640
  58.2 39.2 %collective-permute-start.15 = (bf16[192,1152]{1,0:T(8,128)(2,1)}, bf16[192,1152]{1,0:T(8,128)(2,1)S(1)}, u32[]{:S(2)}, u32[]{:S(2)}) collective-permute-start(bf16[192,1152]{1,0:T(8,128)(2,1)} %dynamic-slice_bitcast_fusion.2), channel_id=1, source_target_pairs={{0,1},{1,2},{2,3},{3,0},{4,5},{5,6},{6,7},{7,4},{8,9},{9,10},{10,1... | collective-permute-start | bytes 1327112 | tf_op jit(solution)/shard_map/ppermute | solution.py:640
  65.8 33.1 %collective-permute-start.6 = (bf16[1,2,80,1152]{3,2,1,0:T(8,128)(2,1)S(1)}, bf16[1,2,80,1152]{3,2,1,0:T(8,128)(2,1)S(1)}, u32[]{:S(2)}, u32[]{:S(2)}) collective-permute-start(bf16[1,2,80,1152]{3,2,1,0:T(8,128)(2,1)S(1)} %pad_maximum_fusion.14), channel_id=1, source_target_pairs={{0,8},{8,0},{1,9},{9,1},{2,10},{10,2},{3,11},{11,3},{4,12},{12,4},... | collective-permute-start | bytes 1105928 | tf_op jit(solution)/shard_map/ppermute | solution.py:651
  67.4 30.3 %collective-permute-start.5 = (bf16[1,2,64,1152]{3,2,1,0:T(8,128)(2,1)S(1)}, bf16[1,2,64,1152]{3,2,1,0:T(8,128)(2,1)S(1)}, u32[]{:S(2)}, u32[]{:S(2)}) collective-permute-start(bf16[1,2,64,1152]{3,2,1,0:T(8,128)(2,1)S(1)} %pad_maximum_fusion.20), channel_id=1, source_target_pairs={{0,16},{16,0},{1,17},{17,1},{2,18},{18,2},{3,19},{19,3},{4,20},{20... | collective-permute-start | bytes 884744 | tf_op jit(solution)/shard_map/ppermute | solution.py:650
  71.1 39.7 %collective-permute-start.1 = (bf16[512,1152]{1,0:T(8,128)(2,1)S(1)}, bf16[512,1152]{1,0:T(8,128)(2,1)S(1)}, u32[]{:S(2)}, u32[]{:S(2)}) collective-permute-start(bf16[512,1152]{1,0:T(8,128)(2,1)S(1)} %copy-done.21), channel_id=1, source_target_pairs={{0,4},{4,0},{1,5},{5,1},{2,6},{6,2},{3,7},{7,3},{8,12},{12,8},{9,1... | collective-permute-start | bytes 3538952 | tf_op jit(solution)/shard_map/ppermute | solution.py:619
  97.4 80.4 %collective-permute-start.30 = (bf16[512,1152]{1,0:T(8,128)(2,1)}, bf16[512,1152]{1,0:T(8,128)(2,1)}, u32[]{:S(2)}, u32[]{:S(2)}) collective-permute-start(bf16[512,1152]{1,0:T(8,128)(2,1)} %get-tuple-element.82), channel_id=1, source_target_pairs={{0,4},{4,0},{1,5},{5,1},{2,6},{6,2},{3,7},{7,3},{8,12},{12,8},{9,1... | collective-permute-start | bytes 3538952 | tf_op jit(solution)/shard_map/ppermute | solution.py:619
  97.5 93.7 %collective-permute-start.24 = (bf16[96,1152]{1,0:T(8,128)(2,1)}, bf16[96,1152]{1,0:T(8,128)(2,1)}, u32[]{:S(2)}, u32[]{:S(2)}) collective-permute-start(bf16[96,1152]{1,0:T(8,128)(2,1)} %dynamic-slice_bitcast_fusion.4), channel_id=1, source_target_pairs={{0,3},{1,0},{2,1},{3,2},{4,7},{5,4},{6,5},{7,6},{8,11},{9,8},{10,9... | collective-permute-start | bytes 663560 | tf_op jit(solution)/shard_map/ppermute | solution.py:640
  97.7 93.7 %collective-permute-start.23 = (bf16[96,1152]{1,0:T(8,128)(2,1)}, bf16[96,1152]{1,0:T(8,128)(2,1)}, u32[]{:S(2)}, u32[]{:S(2)}) collective-permute-start(bf16[96,1152]{1,0:T(8,128)(2,1)} %dynamic-slice_bitcast_fusion.4), channel_id=1, source_target_pairs={{0,2},{1,3},{2,0},{3,1},{4,6},{5,7},{6,4},{7,5},{8,10},{9,11},{10,... | collective-permute-start | bytes 663560 | tf_op jit(solution)/shard_map/ppermute | solution.py:640
  110.8 19.3 %collective-permute-start.11 = (bf16[2,2,64,1152]{3,2,0,1:T(8,128)(2,1)S(1)}, bf16[2,2,64,1152]{3,2,0,1:T(8,128)(2,1)S(1)}, u32[]{:S(2)}, u32[]{:S(2)}) collective-permute-start(bf16[2,2,64,1152]{3,2,0,1:T(8,128)(2,1)S(1)} %pad_maximum_fusion.13), channel_id=1, source_target_pairs={{0,16},{16,0},{1,17},{17,1},{2,18},{18,2},{3,19},{19,3},{4,20},{20... | collective-permute-start | bytes 1769480 | tf_op jit(solution)/shard_map/ppermute | solution.py:650
  134.5 42.2 %collective-permute-start.19 = (bf16[3,96,1152]{2,1,0:T(8,128)(2,1)S(1)}, bf16[3,96,1152]{2,1,0:T(8,128)(2,1)S(1)}, u32[]{:S(2)}, u32[]{:S(2)}) collective-permute-start(bf16[3,96,1152]{2,1,0:T(8,128)(2,1)S(1)} %get-tuple-element.186), channel_id=1, source_target_pairs={{0,16},{16,0},{1,17},{17,1},{2,18},{18,2},{3,19},{19,3},{4,20},{20... | collective-permute-start | bytes 1990664 | tf_op jit(solution)/shard_map/ppermute | solution.py:649
  137.2 38.1 %collective-permute-start.18 = (bf16[3,96,1152]{2,1,0:T(8,128)(2,1)S(1)}, bf16[3,96,1152]{2,1,0:T(8,128)(2,1)S(1)}, u32[]{:S(2)}, u32[]{:S(2)}) collective-permute-start(bf16[3,96,1152]{2,1,0:T(8,128)(2,1)S(1)} %get-tuple-element.188), channel_id=1, source_target_pairs={{0,8},{8,0},{1,9},{9,1},{2,10},{10,2},{3,11},{11,3},{4,12},{12,4},... | collective-permute-start | bytes 1990664 | tf_op jit(solution)/shard_map/ppermute | solution.py:648
  176.7 31.7 %collective-permute-start.20 = (bf16[3,2,96,1152]{3,2,0,1:T(8,128)(2,1)}, bf16[3,2,96,1152]{3,2,0,1:T(8,128)(2,1)S(1)}, u32[]{:S(2)}, u32[]{:S(2)}) collective-permute-start(bf16[3,2,96,1152]{3,2,0,1:T(8,128)(2,1)} %pad_maximum_fusion.4), channel_id=1, source_target_pairs={{0,16},{16,0},{1,17},{17,1},{2,18},{18,2},{3,19},{19,3},{4,20},{20... | collective-permute-start | bytes 3981320 | tf_op jit(solution)/shard_map/ppermute | solution.py:650
  177.9 31.7 %collective-permute-start.21 = (bf16[3,2,96,1152]{3,2,1,0:T(8,128)(2,1)}, bf16[3,2,96,1152]{3,2,1,0:T(8,128)(2,1)S(1)}, u32[]{:S(2)}, u32[]{:S(2)}) collective-permute-start(bf16[3,2,96,1152]{3,2,1,0:T(8,128)(2,1)} %pad_maximum_fusion.5), channel_id=1, source_target_pairs={{0,8},{8,0},{1,9},{9,1},{2,10},{10,2},{3,11},{11,3},{4,12},{12,4},... | collective-permute-start | bytes 3981320 | tf_op jit(solution)/shard_map/ppermute | solution.py:651
  191.1 41.4 %collective-permute-start.14 = (bf16[512,1152]{1,0:T(8,128)(2,1)S(1)}, bf16[512,1152]{1,0:T(8,128)(2,1)}, u32[]{:S(2)}, u32[]{:S(2)}) collective-permute-start(bf16[512,1152]{1,0:T(8,128)(2,1)S(1)} %copy-done.22), channel_id=1, source_target_pairs={{0,4},{4,0},{1,5},{5,1},{2,6},{6,2},{3,7},{7,3},{8,12},{12,8},{9,1... | collective-permute-start | bytes 3538952 | tf_op jit(solution)/shard_map/ppermute | solution.py:619
  212.4 16.3 %collective-permute-start.26 = (bf16[3,48,1152]{2,1,0:T(8,128)(2,1)}, bf16[3,48,1152]{2,1,0:T(8,128)(2,1)S(1)}, u32[]{:S(2)}, u32[]{:S(2)}) collective-permute-start(bf16[3,48,1152]{2,1,0:T(8,128)(2,1)} %get-tuple-element.210), channel_id=1, source_target_pairs={{0,16},{16,0},{1,17},{17,1},{2,18},{18,2},{3,19},{19,3},{4,20},{20... | collective-permute-start | bytes 995336 | tf_op jit(solution)/shard_map/ppermute | solution.py:649
  228.3 38.4 %collective-permute-start.27 = (bf16[3,2,48,1152]{3,2,0,1:T(8,128)(2,1)}, bf16[3,2,48,1152]{3,2,0,1:T(8,128)(2,1)S(1)}, u32[]{:S(2)}, u32[]{:S(2)}) collective-permute-start(bf16[3,2,48,1152]{3,2,0,1:T(8,128)(2,1)} %pad_maximum_fusion.11), channel_id=1, source_target_pairs={{0,16},{16,0},{1,17},{17,1},{2,18},{18,2},{3,19},{19,3},{4,20},{20... | collective-permute-start | bytes 1990664 | tf_op jit(solution)/shard_map/ppermute | solution.py:650
  229.6 38.0 %collective-permute-start.28 = (bf16[3,2,48,1152]{3,2,1,0:T(8,128)(2,1)}, bf16[3,2,48,1152]{3,2,1,0:T(8,128)(2,1)S(1)}, u32[]{:S(2)}, u32[]{:S(2)}) collective-permute-start(bf16[3,2,48,1152]{3,2,1,0:T(8,128)(2,1)} %pad_maximum_fusion.12), channel_id=1, source_target_pairs={{0,8},{8,0},{1,9},{9,1},{2,10},{10,2},{3,11},{11,3},{4,12},{12,4},... | collective-permute-start | bytes 1990664 | tf_op jit(solution)/shard_map/ppermute | solution.py:651
  264.4 42.9 %collective-permute-start.52 = (bf16[4,2,144,384]{3,2,0,1:T(8,128)(2,1)S(1)}, bf16[4,2,144,384]{3,2,0,1:T(8,128)(2,1)S(1)}, u32[]{:S(2)}, u32[]{:S(2)}) collective-permute-start(bf16[4,2,144,384]{3,2,0,1:T(8,128)(2,1)S(1)} %copy.163), channel_id=1, source_target_pairs={{0,16},{16,0},{1,17},{17,1},{2,18},{18,2},{3,19},{19,3},{4,20},{20... | collective-permute-start | bytes 2654216 | tf_op jit(solution)/shard_map/ppermute | solution.py:671
  266.2 42.8 %collective-permute-start.50 = (bf16[4,2,144,384]{3,2,0,1:T(8,128)(2,1)S(1)}, bf16[4,2,144,384]{3,2,0,1:T(8,128)(2,1)S(1)}, u32[]{:S(2)}, u32[]{:S(2)}) collective-permute-start(bf16[4,2,144,384]{3,2,0,1:T(8,128)(2,1)S(1)} %copy.160), channel_id=1, source_target_pairs={{0,8},{8,0},{1,9},{9,1},{2,10},{10,2},{3,11},{11,3},{4,12},{12,4},... | collective-permute-start | bytes 2654216 | tf_op jit(solution)/shard_map/ppermute | solution.py:670
  307.4 20.0 %collective-permute-start.53 = (bf16[4,144,384]{2,1,0:T(8,128)(2,1)S(1)}, bf16[4,144,384]{2,1,0:T(8,128)(2,1)S(1)}, u32[]{:S(2)}, u32[]{:S(2)}) collective-permute-start(bf16[4,144,384]{2,1,0:T(8,128)(2,1)S(1)} %fusion.28), channel_id=1, source_target_pairs={{0,8},{8,0},{1,9},{9,1},{2,10},{10,2},{3,11},{11,3},{4,12},{12,4},... | collective-permute-start | bytes 1327112 | tf_op jit(solution)/shard_map/ppermute | solution.py:677
  309.1 18.5 %collective-permute-start.51 = (bf16[4,144,384]{2,1,0:T(8,128)(2,1)S(1)}, bf16[4,144,384]{2,1,0:T(8,128)(2,1)S(1)}, u32[]{:S(2)}, u32[]{:S(2)}) collective-permute-start(bf16[4,144,384]{2,1,0:T(8,128)(2,1)S(1)} %fusion.27), channel_id=1, source_target_pairs={{0,16},{16,0},{1,17},{17,1},{2,18},{18,2},{3,19},{19,3},{4,20},{20... | collective-permute-start | bytes 1327112 | tf_op jit(solution)/shard_map/ppermute | solution.py:676
  325.7 64.1 %collective-permute-start.44 = (bf16[4,2,144,768]{3,2,0,1:T(8,128)(2,1)}, bf16[4,2,144,768]{3,2,0,1:T(8,128)(2,1)}, u32[]{:S(2)}, u32[]{:S(2)}) collective-permute-start(bf16[4,2,144,768]{3,2,0,1:T(8,128)(2,1)} %copy.154), channel_id=1, source_target_pairs={{0,16},{16,0},{1,17},{17,1},{2,18},{18,2},{3,19},{19,3},{4,20},{20... | collective-permute-start | bytes 5308424 | tf_op jit(solution)/shard_map/ppermute | solution.py:671
  328.7 19.4 %collective-permute-start.54 = (bf16[2,144,384]{2,1,0:T(8,128)(2,1)S(1)}, bf16[2,144,384]{2,1,0:T(8,128)(2,1)S(1)}, u32[]{:S(2)}, u32[]{:S(2)}) collective-permute-start(bf16[2,144,384]{2,1,0:T(8,128)(2,1)S(1)} %get-tuple-element.168), channel_id=1, source_target_pairs={{0,3},{1,0},{2,1},{3,2},{4,7},{5,4},{6,5},{7,6},{8,11},{9,8},{10,9... | collective-permute-start | bytes 663560 | tf_op jit(solution)/shard_map/ppermute | solution.py:697
  347.6 33.0 %collective-permute-start.29 = (bf16[512,1152]{1,0:T(8,128)(2,1)}, bf16[512,1152]{1,0:T(8,128)(2,1)}, u32[]{:S(2)}, u32[]{:S(2)}) collective-permute-start(bf16[512,1152]{1,0:T(8,128)(2,1)} %get-tuple-element.80), channel_id=1, source_target_pairs={{0,4},{4,0},{1,5},{5,1},{2,6},{6,2},{3,7},{7,3},{8,12},{12,8},{9,1... | collective-permute-start | bytes 3538952 | tf_op jit(solution)/shard_map/ppermute | solution.py:619
  347.6 24.4 %collective-permute-start.31 = (bf16[512,1152]{1,0:T(8,128)(2,1)}, bf16[512,1152]{1,0:T(8,128)(2,1)}, u32[]{:S(2)}, u32[]{:S(2)}) collective-permute-start(bf16[512,1152]{1,0:T(8,128)(2,1)} %get-tuple-element.85), channel_id=1, source_target_pairs={{0,4},{4,0},{1,5},{5,1},{2,6},{6,2},{3,7},{7,3},{8,12},{12,8},{9,1... | collective-permute-start | bytes 3538952 | tf_op jit(solution)/shard_map/ppermute | solution.py:619
  348.1 18.1 %collective-permute-start.55 = (bf16[2,144,384]{2,1,0:T(8,128)(2,1)}, bf16[2,144,384]{2,1,0:T(8,128)(2,1)}, u32[]{:S(2)}, u32[]{:S(2)}) collective-permute-start(bf16[2,144,384]{2,1,0:T(8,128)(2,1)} %get-tuple-element.170), channel_id=1, source_target_pairs={{0,2},{1,3},{2,0},{3,1},{4,6},{5,7},{6,4},{7,5},{8,10},{9,11},{10,... | collective-permute-start | bytes 663560 | tf_op jit(solution)/shard_map/ppermute | solution.py:697
  358.6 41.0 %collective-permute-start.42 = (bf16[4,2,144,768]{3,2,0,1:T(8,128)(2,1)S(1)}, bf16[4,2,144,768]{3,2,0,1:T(8,128)(2,1)}, u32[]{:S(2)}, u32[]{:S(2)}) collective-permute-start(bf16[4,2,144,768]{3,2,0,1:T(8,128)(2,1)S(1)} %copy.151), channel_id=1, source_target_pairs={{0,8},{8,0},{1,9},{9,1},{2,10},{10,2},{3,11},{11,3},{4,12},{12,4},... | collective-permute-start | bytes 5308424 | tf_op jit(solution)/shard_map/ppermute | solution.py:670
  380.1 21.3 %collective-permute-start.32 = (bf16[512,1152]{1,0:T(8,128)(2,1)}, bf16[512,1152]{1,0:T(8,128)(2,1)}, u32[]{:S(2)}, u32[]{:S(2)}) collective-permute-start(bf16[512,1152]{1,0:T(8,128)(2,1)} %get-tuple-element.87), channel_id=1, source_target_pairs={{0,4},{4,0},{1,5},{5,1},{2,6},{6,2},{3,7},{7,3},{8,12},{12,8},{9,1... | collective-permute-start | bytes 3538952 | tf_op jit(solution)/shard_map/ppermute | solution.py:619
  392.1 24.2 %collective-permute-start.45 = (bf16[4,144,768]{2,1,0:T(8,128)(2,1)}, bf16[4,144,768]{2,1,0:T(8,128)(2,1)}, u32[]{:S(2)}, u32[]{:S(2)}) collective-permute-start(bf16[4,144,768]{2,1,0:T(8,128)(2,1)} %fusion.11), channel_id=1, source_target_pairs={{0,8},{8,0},{1,9},{9,1},{2,10},{10,2},{3,11},{11,3},{4,12},{12,4},... | collective-permute-start | bytes 2654216 | tf_op jit(solution)/shard_map/ppermute | solution.py:677
  401.0 17.7 %collective-permute-start.43 = (bf16[4,144,768]{2,1,0:T(8,128)(2,1)S(1)}, bf16[4,144,768]{2,1,0:T(8,128)(2,1)S(1)}, u32[]{:S(2)}, u32[]{:S(2)}) collective-permute-start(bf16[4,144,768]{2,1,0:T(8,128)(2,1)S(1)} %fusion.10), channel_id=1, source_target_pairs={{0,16},{16,0},{1,17},{17,1},{2,18},{18,2},{3,19},{19,3},{4,20},{20... | collective-permute-start | bytes 2654216 | tf_op jit(solution)/shard_map/ppermute | solution.py:676
  420.6 34.5 %collective-permute-start.46 = (bf16[2,144,768]{2,1,0:T(8,128)(2,1)S(1)}, bf16[2,144,768]{2,1,0:T(8,128)(2,1)S(1)}, u32[]{:S(2)}, u32[]{:S(2)}) collective-permute-start(bf16[2,144,768]{2,1,0:T(8,128)(2,1)S(1)} %get-tuple-element.152), channel_id=1, source_target_pairs={{0,3},{1,0},{2,1},{3,2},{4,7},{5,4},{6,5},{7,6},{8,11},{9,8},{10,9... | collective-permute-start | bytes 1327112 | tf_op jit(solution)/shard_map/ppermute | solution.py:697
  420.6 34.4 %collective-permute-start.48 = (bf16[2,144,768]{2,1,0:T(8,128)(2,1)S(1)}, bf16[2,144,768]{2,1,0:T(8,128)(2,1)S(1)}, u32[]{:S(2)}, u32[]{:S(2)}) collective-permute-start(bf16[2,144,768]{2,1,0:T(8,128)(2,1)S(1)} %get-tuple-element.153), channel_id=1, source_target_pairs={{0,1},{1,2},{2,3},{3,0},{4,5},{5,6},{6,7},{7,4},{8,9},{9,10},{10,1... | collective-permute-start | bytes 1327112 | tf_op jit(solution)/shard_map/ppermute | solution.py:697
  422.8 35.1 %collective-permute-start.47 = (bf16[2,144,768]{2,1,0:T(8,128)(2,1)S(1)}, bf16[2,144,768]{2,1,0:T(8,128)(2,1)S(1)}, u32[]{:S(2)}, u32[]{:S(2)}) collective-permute-start(bf16[2,144,768]{2,1,0:T(8,128)(2,1)S(1)} %get-tuple-element.154), channel_id=1, source_target_pairs={{0,2},{1,3},{2,0},{3,1},{4,6},{5,7},{6,4},{7,5},{8,10},{9,11},{10,... | collective-permute-start | bytes 1327112 | tf_op jit(solution)/shard_map/ppermute | solution.py:697
  455.0 25.6 %collective-permute-start.33 = (bf16[512,1152]{1,0:T(8,128)(2,1)}, bf16[512,1152]{1,0:T(8,128)(2,1)}, u32[]{:S(2)}, u32[]{:S(2)}) collective-permute-start(bf16[512,1152]{1,0:T(8,128)(2,1)} %get-tuple-element.92), channel_id=1, source_target_pairs={{0,4},{4,0},{1,5},{5,1},{2,6},{6,2},{3,7},{7,3},{8,12},{12,8},{9,1... | collective-permute-start | bytes 3538952 | tf_op jit(solution)/shard_map/ppermute | solution.py:619
  458.1 20.7 %collective-permute-start.49 = (bf16[144,768]{1,0:T(8,128)(2,1)S(1)}, bf16[144,768]{1,0:T(8,128)(2,1)S(1)}, u32[]{:S(2)}, u32[]{:S(2)}) collective-permute-start(bf16[144,768]{1,0:T(8,128)(2,1)S(1)} %fusion.40), channel_id=1, source_target_pairs={{0,4},{4,0},{1,5},{5,1},{2,6},{6,2},{3,7},{7,3},{8,12},{12,8},{9,1... | collective-permute-start | bytes 663560 | tf_op jit(solution)/shard_map/ppermute | solution.py:619
  477.3 35.0 %collective-permute-start.36 = (bf16[4,2,144,576]{3,2,0,1:T(8,128)(2,1)}, bf16[4,2,144,576]{3,2,0,1:T(8,128)(2,1)}, u32[]{:S(2)}, u32[]{:S(2)}) collective-permute-start(bf16[4,2,144,576]{3,2,0,1:T(8,128)(2,1)} %copy.143), channel_id=1, source_target_pairs={{0,16},{16,0},{1,17},{17,1},{2,18},{18,2},{3,19},{19,3},{4,20},{20... | collective-permute-start | bytes 3981320 | tf_op jit(solution)/shard_map/ppermute | solution.py:671
  477.6 38.1 %collective-permute-start.34 = (bf16[4,2,144,576]{3,2,0,1:T(8,128)(2,1)}, bf16[4,2,144,576]{3,2,0,1:T(8,128)(2,1)}, u32[]{:S(2)}, u32[]{:S(2)}) collective-permute-start(bf16[4,2,144,576]{3,2,0,1:T(8,128)(2,1)} %copy.140), channel_id=1, source_target_pairs={{0,8},{8,0},{1,9},{9,1},{2,10},{10,2},{3,11},{11,3},{4,12},{12,4},... | collective-permute-start | bytes 3981320 | tf_op jit(solution)/shard_map/ppermute | solution.py:670
  514.5 26.5 %collective-permute-start.37 = (bf16[4,144,576]{2,1,0:T(8,128)(2,1)}, bf16[4,144,576]{2,1,0:T(8,128)(2,1)}, u32[]{:S(2)}, u32[]{:S(2)}) collective-permute-start(bf16[4,144,576]{2,1,0:T(8,128)(2,1)} %fusion.21), channel_id=1, source_target_pairs={{0,8},{8,0},{1,9},{9,1},{2,10},{10,2},{3,11},{11,3},{4,12},{12,4},... | collective-permute-start | bytes 1990664 | tf_op jit(solution)/shard_map/ppermute | solution.py:677
  517.8 24.9 %collective-permute-start.35 = (bf16[4,144,576]{2,1,0:T(8,128)(2,1)}, bf16[4,144,576]{2,1,0:T(8,128)(2,1)}, u32[]{:S(2)}, u32[]{:S(2)}) collective-permute-start(bf16[4,144,576]{2,1,0:T(8,128)(2,1)} %fusion.20), channel_id=1, source_target_pairs={{0,16},{16,0},{1,17},{17,1},{2,18},{18,2},{3,19},{19,3},{4,20},{20... | collective-permute-start | bytes 1990664 | tf_op jit(solution)/shard_map/ppermute | solution.py:676
  518.9 17.7 %all-to-all-start.1 = ((f32[32,1,508]{2,1,0:T(1,128)}), f32[32,1,508]{2,1,0:T(1,128)S(1)}, u32[]{:S(2)}, u32[]{:S(2)}) async-start(f32[32,1,508]{2,1,0:T(1,128)} %copy.170), calls=%async_computation.1 | async-start | bytes 131072 | tf_op jit(solution)/shard_map/all_to_all | solution.py:794
  537.6 54.3 %all-to-all-start = ((f32[32,2,2305]{2,1,0:T(2,128)}), f32[32,2,2305]{2,1,0:T(2,128)}, u32[]{:S(2)}, u32[]{:S(2)}) async-start(f32[32,2,2305]{2,1,0:T(2,128)} %broadcast_in_dim.13), calls=%async_computation | async-start | bytes 1245184 | tf_op jit(solution)/shard_map/all_to_all | solution.py:803
  549.2 22.9 %collective-permute-start.40 = (bf16[2,144,576]{2,1,0:T(8,128)(2,1)}, bf16[2,144,576]{2,1,0:T(8,128)(2,1)}, u32[]{:S(2)}, u32[]{:S(2)}) collective-permute-start(bf16[2,144,576]{2,1,0:T(8,128)(2,1)} %get-tuple-element.156), channel_id=1, source_target_pairs={{0,1},{1,2},{2,3},{3,0},{4,5},{5,6},{6,7},{7,4},{8,9},{9,10},{10,1... | collective-permute-start | bytes 995336 | tf_op jit(solution)/shard_map/ppermute | solution.py:697
  549.2 40.5 %collective-permute-start.39 = (bf16[2,144,576]{2,1,0:T(8,128)(2,1)}, bf16[2,144,576]{2,1,0:T(8,128)(2,1)}, u32[]{:S(2)}, u32[]{:S(2)}) collective-permute-start(bf16[2,144,576]{2,1,0:T(8,128)(2,1)} %get-tuple-element.157), channel_id=1, source_target_pairs={{0,2},{1,3},{2,0},{3,1},{4,6},{5,7},{6,4},{7,5},{8,10},{9,11},{10,... | collective-permute-start | bytes 995336 | tf_op jit(solution)/shard_map/ppermute | solution.py:697
  (69 other events, 888.7 us)

commit v2 on v1

v2 whole, which is shorter than its diff:
```python
import functools

import jax
import jax.numpy as jnp
import numpy as np
from jax import lax
from jax.experimental import pallas as pl
from jax.experimental.pallas import tpu as pltpu
from jax.sharding import Mesh
from jax.sharding import PartitionSpec as P

HD = 72
EXACT = lax.Precision.HIGHEST
EPSILON = 1e-06
NEG = -1e30
VMEM_LIMIT = 58 * 1024 * 1024
UNROLL = 4
MLP_TILE = 256
BF = jnp.bfloat16
F32 = jnp.float32
NT = (((1,), (1,)), ((), ()))
TN = (((0,), (0,)), ((), ()))


def dot(a, b):
    return jnp.dot(a, b, preferred_element_type=F32)


def dot_nt(a, b):
    return lax.dot_general(a, b, NT, preferred_element_type=F32)


def dot_tn(a, b):
    return lax.dot_general(a, b, TN, preferred_element_type=F32)


def call(kernel, name, grid, ins, outs, scratch=(), scalars=(), flops=0, moved=0, exps=0, deps=(), carry=(), dynamic=False):
    def spec(shape, block, index):
        if block is None:
            return pl.BlockSpec(shape, lambda *_: (0,) * len(shape))
        return pl.BlockSpec(block, index if dynamic else lambda *at: index(*at[: len(grid)]))

    arrays = [item[0] for item in ins]
    in_specs = [spec(item[0].shape, item[1], item[2]) for item in ins]
    out_specs = [spec(item[0].shape, item[1], item[2]) for item in outs]
    count_s, count_i, count_d = len(scalars), len(ins), len(deps) + len(carry)

    def body(*refs):
        kept = refs[: count_s + count_i] + refs[count_s + count_i + count_d :]
        kernel(*kept)

    return pl.pallas_call(
        body,
        grid_spec=pltpu.PrefetchScalarGridSpec(
            num_scalar_prefetch=count_s,
            grid=grid,
            in_specs=in_specs + [pl.BlockSpec(memory_space=pl.ANY)] * count_d,
            out_specs=out_specs,
            scratch_shapes=list(scratch),
        ),
        out_shape=[item[0] for item in outs],
        compiler_params=pltpu.CompilerParams(
            dimension_semantics=("arbitrary",) * len(grid), vmem_limit_bytes=VMEM_LIMIT
        ),
        cost_estimate=pl.CostEstimate(flops=flops, bytes_accessed=moved, transcendentals=exps),
        input_output_aliases={count_s + count_i + len(deps) + j: j for j in range(len(carry))},
        name=name,
    )(*scalars, *arrays, *deps, *carry)


def shape(dims, dtype):
    return jax.ShapeDtypeStruct(tuple(dims), dtype)


def swap_matrix(width):
    quarter = HD // 4
    out = np.zeros((width, width), np.float32)
    for lane in range(width):
        if (lane % HD) % (2 * quarter) < quarter:
            out[lane + quarter, lane] = -1.0
        else:
            out[lane - quarter, lane] = 1.0
    return out


def head_mask(heads, which, dtype):
    lane = lax.broadcasted_iota(jnp.int32, (1, heads * HD), 1)
    inside = (lane >= which * HD) & (lane < (which + 1) * HD)
    return jnp.where(inside, 1.0, 0.0).astype(F32).astype(dtype)


def finish(parts, outs, starts, tile):
    half = outs[0].shape[0]
    for j, ref in enumerate(outs):
        for t in range(half // tile):
            at = slice(t * tile, (t + 1) * tile)
            value = parts(slice(j * half + t * tile, j * half + (t + 1) * tile))
            if starts:
                value = value + starts[j][at, :]
            ref[at, :] = value.astype(ref.dtype)


def at_step(step, count, body):
    for r in range(count):

        @pl.when(step == r)
        def _(r=r):
            body(r)


def halves_out(rows, width, last):
    return [(shape((rows, width), F32), None, None), (shape((rows, width), BF if last else F32), None, None)]


def by_step(array, begin=0):
    return (array, (1,) + array.shape[1:], lambda z: (z + begin,) + (0,) * (array.ndim - 1))


def step_out(dims, dtype):
    return (shape(dims, dtype), (1,) + tuple(dims[1:]), lambda z: (z,) + (0,) * (len(dims) - 1))


def attn_fwd(lens, place, both, weights, count, total, carry, starts, cos, sin, heads, seq, deps=()):
    (half, width), hw = both[0].shape, heads * HD
    ahead = 1 if carry else 0
    last = bool(carry)
    rows = 2 * half
    images, given = rows // seq, len(starts)
    scale = HD ** (-0.5)

    def kernel(lens, place, own_in, peer_in, cos_ref, sin_ref, swap_ref, w_ref, *refs):
        starts, refs = refs[:given], refs[given:]
        q_ref, k_ref, v_ref, o_ref, own_ref, peer_ref, wcat, wout, full, o_all = refs
        step = pl.program_id(0)
        for j in range(3):
            wcat[j * hw : (j + 1) * hw, :] = w_ref[0, j]
        wcat[3 * hw :, :] = dot(swap_ref[...], wcat[: 2 * hw, :]).astype(BF)
        full[:, :half] = dot_nt(wcat[...], own_in[...])
        full[:, half:] = dot_nt(wcat[...], peer_in[...])

        def image(i, carry):
            at = pl.ds(pl.multiple_of(i * seq, seq), seq)
            cos, sin = cos_ref[:, at], sin_ref[:, at]
            ok = lax.broadcasted_iota(jnp.int32, (seq, 1), 0) < lens[i]
            outs = []
            for h in range(heads):
                part = lambda j: full[j * hw + h * HD : j * hw + (h + 1) * HD, at]
                q = (part(0) * cos + part(3) * sin).astype(BF)
                k = (part(1) * cos + part(4) * sin).astype(BF)
                v = part(2).astype(BF)
                q_ref[0, h, :, at] = q
                k_ref[0, h, :, at] = k
                v_ref[0, h, :, at] = v
                st = jnp.where(ok, dot_tn(k, q) * scale, NEG)
                ex = jnp.exp(st - jnp.max(st, axis=0, keepdims=True))
                probs = (ex * (1.0 / jnp.sum(ex, axis=0, keepdims=True))).astype(BF)
                outs.append(dot(v, probs))
            o_ref[0, :, at] = jnp.concatenate(outs, axis=0).astype(BF)
            return carry

        lax.fori_loop(0, images, image, 0, unroll=UNROLL)

        def keep(r):
            wout[r * hw : (r + 1) * hw, :] = w_ref[0, 3]
            o_all[r * hw : (r + 1) * hw, :] = o_ref[0]

        at_step(step, count, keep)

        @pl.when(step == count - 1)
        def _():
            finish(lambda at: dot_tn(o_all[:, at], wout[...]), (own_ref, peer_ref), starts, seq)

    def block_of(step, lens, place):
        return (place[2] + ahead + step) % total

    def out(*dims):
        index = lambda *at: (block_of(*at),) + (0,) * len(dims)
        return (shape((total,) + dims, BF), (1,) + dims, index)

    index = (lambda *at: (block_of(*at), 0, 0, 0)) if carry else (lambda *at: (0, 0, 0, 0))
    return call(
        kernel,
        "attn_fwd",
        (count,),
        [(x, None, None) for x in both + (cos, sin, jnp.asarray(swap_matrix(2 * hw).T, BF))]
        + [(weights, (1,) + weights.shape[1:], index)]
        + [(x, None, None) for x in starts],
        [out(heads, HD, rows)] * 3 + [out(hw, rows)] + halves_out(half, width, last),
        scratch=[
            pltpu.VMEM((5 * hw, width), BF),
            pltpu.VMEM((count * hw, width), BF),
            pltpu.VMEM((5 * hw, rows), F32),
            pltpu.VMEM((count * hw, rows), BF),
        ],
        scalars=(lens, place),
        flops=2 * count * rows * width * 6 * hw + 8 * count * rows * heads * seq * 256,
        moved=20_000_000,
        exps=count * rows * heads * seq,
        deps=deps,
        carry=carry,
        dynamic=True,
    )


def attn_bwd(lens, both, weights, part_of, starts, cos, sin, q, k, v, heads, seq, deps=()):
    begin, end = part_of
    count, (half, width), hw = end - begin, both[0].shape, heads * HD
    last = end == weights.shape[0]
    rows = 2 * half
    images, given = rows // seq, len(starts)
    scale = HD ** (-0.5)

    def kernel(lens, own_in, peer_in, cos_ref, sin_ref, swap_ref, q_ref, k_ref, v_ref, w_ref, *refs):
        starts, refs = refs[:given], refs[given:]
        dqkv_ref, own_ref, peer_ref, w_all, do_all, d_all = refs
        step = pl.program_id(0)
        do_all[:, :half] = dot_nt(w_ref[0, 3], own_in[...])
        do_all[:, half:] = dot_nt(w_ref[0, 3], peer_in[...])

        def image(i, carry):
            at = pl.ds(pl.multiple_of(i * seq, seq), seq)
            cos, sin = cos_ref[:, at], sin_ref[:, at]
            ok = lax.broadcasted_iota(jnp.int32, (seq, 1), 0) < lens[i]
            dqs, dks, dvs = [], [], []
            for h in range(heads):
                do = do_all[h * HD : (h + 1) * HD, at].astype(BF)
                q, k, v = q_ref[0, h, :, at], k_ref[0, h, :, at], v_ref[0, h, :, at]
                st = jnp.where(ok, dot_tn(k, q) * scale, NEG)
                dp = dot_tn(v, do)
                ex = jnp.exp(st - jnp.max(st, axis=0, keepdims=True))
                probs = ex * (1.0 / jnp.sum(ex, axis=0, keepdims=True))
                inner = jnp.sum(dp * probs, axis=0, keepdims=True)
                ds = (probs * (dp - inner)).astype(BF)
                dvs.append(dot_nt(do, probs.astype(BF)))
                dk = dot_nt(q, ds), dot_nt(dot(swap_ref[...], q).astype(BF), ds)
                dq = dot(k, ds), dot(dot(swap_ref[...], k).astype(BF), ds)
                dqs.append((dq[0] * cos - dq[1] * sin) * scale)
                dks.append((dk[0] * cos - dk[1] * sin) * scale)
            dqkv_ref[0, :, at] = jnp.concatenate(dqs + dks + dvs, axis=0).astype(BF)
            return carry

        lax.fori_loop(0, images, image, 0, unroll=UNROLL)

        def keep(r):
            for j in range(3):
                first = (r * 3 + j) * hw
                w_all[first : first + hw, :] = w_ref[0, j]
            d_all[r * 3 * hw : (r + 1) * 3 * hw, :] = dqkv_ref[0]

        at_step(step, count, keep)

        @pl.when(step == count - 1)
        def _():
            finish(lambda at: dot_tn(d_all[:, at], w_all[...]), (own_ref, peer_ref), starts, seq)

    return call(
        kernel,
        "attn_bwd",
        (count,),
        [(x, None, None) for x in both + (cos, sin, jnp.asarray(swap_matrix(HD).T, BF))]
        + [by_step(q), by_step(k), by_step(v), by_step(weights, begin)]
        + [(x, None, None) for x in starts],
        [step_out((count, 3 * hw, rows), BF)] + halves_out(half, width, last),
        scratch=[
            pltpu.VMEM((count * 3 * hw, width), BF),
            pltpu.VMEM((hw, rows), F32),
            pltpu.VMEM((count * 3 * hw, rows), BF),
        ],
        scalars=(lens,),
        flops=2 * count * rows * width * 4 * hw + 20 * count * rows * heads * seq * 256,
        moved=20_000_000,
        exps=count * rows * heads * seq,
        deps=deps,
    )


def tiles(refs, tile, body):
    half = refs[0].shape[0]
    for j, ref in enumerate(refs):
        for t in range(half // tile):
            body(ref, slice(t * tile, (t + 1) * tile), slice(j * half + t * tile, j * half + (t + 1) * tile))


def mlp_fwd(both, weights, deps=()):
    count, blocks, part, width = weights.shape
    rows, cols = 2 * both[0].shape[0], blocks * part
    units = cols // 2

    def kernel(own_in, peer_in, w_ref, gu_ref, hid_ref):
        weight = w_ref[0].reshape(cols, width)

        def block(ref, here, at):
            gu = dot_nt(ref[here, :], weight)
            gu_ref[0, at, :] = gu
            g, u = gu[:, :units], gu[:, units:]
            hid_ref[0, at, :] = (g * jax.nn.sigmoid(g) * u).astype(BF)

        tiles((own_in, peer_in), MLP_TILE, block)

    return call(
        kernel,
        "mlp_fwd",
        (count,),
        [(x, None, None) for x in both] + [by_step(weights)],
        [step_out((count, rows, cols), F32), step_out((count, rows, units), BF)],
        flops=2 * count * rows * width * cols,
        moved=26_000_000,
        exps=count * rows * units,
        deps=deps,
    )


def mlp_mid(both, downs, gate_up, deps=()):
    count, blocks, part, width = downs.shape
    rows, units = 2 * both[0].shape[0], blocks * part

    def kernel(own_in, peer_in, w_ref, gu_ref, dgu_ref):
        weight = w_ref[0].reshape(units, width)

        def block(ref, here, at):
            dhid = dot_nt(ref[here, :], weight)
            g, u = gu_ref[0, at, :units], gu_ref[0, at, units:]
            sig = jax.nn.sigmoid(g)
            dgu_ref[0, at, :units] = (dhid * u * sig * (1.0 + g * (1.0 - sig))).astype(BF)
            dgu_ref[0, at, units:] = (dhid * g * sig).astype(BF)

        tiles((own_in, peer_in), MLP_TILE, block)

    return call(
        kernel,
        "mlp_mid",
        (count,),
        [(x, None, None) for x in both] + [by_step(downs), by_step(gate_up)],
        [step_out((count, rows, 2 * units), BF)],
        flops=2 * count * rows * width * units,
        moved=26_000_000,
        exps=count * rows * units,
        deps=deps,
    )[0]


def back_out(values, weights, name, deps=()):
    count, rows, cols = values.shape
    width = weights.shape[3]
    tile = rows // 4

    def kernel(v_ref, w_ref, own_ref, peer_ref):
        t = pl.program_id(0)
        value = sum(dot(v_ref[r], w_ref[r].reshape(cols, width)) for r in range(count))

        @pl.when(t < 2)
        def _():
            own_ref[...] = value

        @pl.when(t >= 2)
        def _():
            peer_ref[...] = value.astype(BF)

    return call(
        kernel,
        name,
        (4,),
        [(values, (count, tile, cols), lambda t: (0, t, 0)), (weights, None, None)],
        [
            (shape((rows // 2, width), F32), (tile, width), lambda t: (jnp.minimum(t, 1), 0)),
            (shape((rows // 2, width), BF), (tile, width), lambda t: (jnp.maximum(t - 2, 0), 0)),
        ],
        flops=2 * count * rows * width * cols,
        moved=2 * values.size + 2 * weights.size + 3 * rows * width,
        deps=deps,
    )


ORDERS = {"x": ((1, 3), (0, 2)), "y": ((2, 3), (0, 1))}


def grad_split(place, pairs, parts, deps=()):
    half, width = pairs[0][0][0].shape
    rows, count = 2 * half, pairs[0][1].shape[0]
    last = [right.shape[2] == rows for _, right in pairs]
    widths = [right.shape[1 if flip else 2] for (_, right), flip in zip(pairs, last)]
    cols, strip, n = sum(widths), width // 8, len(pairs)

    def kernel(place, *refs):
        lefts, refs = refs[: 2 * n], refs[2 * n :]
        rights, refs = refs[:n], refs[n:]
        outs, refs = refs[: 2 * len(parts)], refs[2 * len(parts) :]
        turned, res = refs[:n], refs[n]

        @pl.when(pl.program_id(0) == 0)
        def _():
            for j, lt in enumerate(turned):
                lt[:, :half] = lefts[2 * j][...].T
                lt[:, half:] = lefts[2 * j + 1][...].T

        begin = 0
        for lt, right, size, flip in zip(turned, rights, widths, last):
            part = dot_nt(lt[...], right[0]) if flip else dot(lt[...], right[0])
            res[:, begin : begin + size] = part
            begin += size
        step = pl.program_id(0)
        for k, (begin, size, order, low, high) in enumerate(parts):

            @pl.when((step >= low) & (step < high))
            def _(k=k, begin=begin, size=size, order=order):
                for ref, blocks in zip(outs[2 * k : 2 * k + 2], ORDERS[order]):
                    for j, rel in enumerate(blocks):
                        for core in range(2):
                            first = ((place[0] ^ rel) * 2 + (place[1] ^ core)) * strip
                            rows_at = pl.ds(pl.multiple_of(first, 16), strip)
                            ref[j, 0, core] = res[rows_at, begin : begin + size].astype(BF)

    outs = []
    for _, size, _, low, high in parts:

        def index(z, low=low, high=high):
            return (0, jnp.clip(z, low, high - 1) - low, 0, 0, 0)

        out = (shape((2, high - low, 2, strip, size), BF), (2, 1, 2, strip, size), index)
        outs += [out, out]
    return call(
        kernel,
        "grad_split",
        (count,),
        [(x, None, None) for both, _ in pairs for x in both] + [by_step(right) for _, right in pairs],
        outs,
        scratch=[pltpu.VMEM((width, rows), BF)] * n + [pltpu.VMEM((width, cols), F32)],
        scalars=(place,),
        flops=2 * count * rows * width * cols,
        moved=2 * rows * width + 2 * count * rows * cols + 2 * count * width * cols,
        deps=deps,
    )


def assemble(place, base, chunks, deps=()):
    blocks, part, width = base.shape
    count = chunks[0][0].shape[0]

    def kernel(place, base, *refs):
        out = refs[-1]
        q = place[0]
        own = pl.program_id(0) == place[2]

        @pl.when(own)
        def _():
            out[0] = base[...]

        @pl.when(jnp.logical_not(own))
        def _():
            begin = 0
            for j in range(len(chunks)):
                near, fx, sy, fy, sx = refs[5 * j : 5 * j + 5]
                half, size = fx.shape[-2], near.shape[1]
                a, b = slice(begin, begin + half), slice(begin + half, begin + size)
                out[0, q, begin : begin + size] = near[0]
                out[0, q ^ 1, a] = fx[0, 0]
                out[0, q ^ 1, b] = sx[0, 0]
                out[0, q ^ 2, a] = fy[0, 0]
                out[0, q ^ 2, b] = sy[0, 0]
                out[0, q ^ 3, a] = fy[1, 0]
                out[0, q ^ 3, b] = sx[1, 0]
                begin += size

    def far(array, whole):
        def index(z, place):
            back = (place[2] + count - z) % count
            return (0 if whole else 1, jnp.maximum(back - 1, 0), 0, 0)

        return (array, (2 if whole else 1, 1) + array.shape[2:], index)

    ins = [(base, None, None)]
    for near, *others in chunks:
        ins += [(near, (1,) + near.shape[1:], lambda z, place: (z, 0, 0))] + [far(x, j > 1) for j, x in enumerate(others)]
    return call(
        kernel,
        "assemble",
        (count,),
        ins,
        [(shape((count,) + base.shape, BF), (1,) + base.shape, lambda z, place: (z, 0, 0, 0))],
        scalars=(place,),
        moved=4 * count * base.size,
        deps=deps,
        dynamic=True,
    )[0]


def norm(x):
    centered = x - jnp.mean(x, axis=-1, keepdims=True)
    inverse = lax.rsqrt(jnp.mean(centered * centered, axis=-1, keepdims=True) + EPSILON)
    return centered * inverse, inverse


def norm_back(d_normed, normed, inverse, scale):
    d_hat = d_normed * (1.0 + scale)
    return inverse * (
        d_hat
        - jnp.mean(d_hat, axis=-1, keepdims=True)
        - normed * jnp.mean(d_hat * normed, axis=-1, keepdims=True)
    )


def total(x):
    return jnp.sum(x, axis=0, keepdims=True)


SHIFT_ONE, SCALE_ONE, GATE_ONE, SHIFT_TWO, SCALE_TWO, GATE_TWO = range(6)


def by_image(body, name, lengths, mod, rows_in, bias, outs, sums, deps=()):
    images, _, width = mod.shape
    seq = rows_in[0].shape[0] // images
    count = len(rows_in)

    def kernel(lens, mod_ref, bias_ref, *refs):
        row_id = lax.broadcasted_iota(jnp.int32, (seq, 1), 0)
        mask = jnp.where(row_id < lens[pl.program_id(0)], 1.0, 0.0).astype(F32)
        values = [ref[...].astype(F32) for ref in refs[:count]]
        got = body(mask, [mod_ref[0, j : j + 1, :] for j in range(6)], bias_ref[...], *values)
        for ref, value in zip(refs[count:-1], got):
            ref[...] = value.astype(ref.dtype)
        for j, value in enumerate(got[len(outs) :]):
            refs[-1][0, j : j + 1, :] = value

    block = ((seq, width), lambda i: (i, 0))
    return call(
        kernel,
        name,
        (images,),
        [(mod, (1, 6, width), lambda i: (i, 0, 0)), (bias, None, None)]
        + [(x,) + block for x in rows_in],
        [(shape(rows_in[0].shape, dtype),) + block for dtype in outs]
        + [(shape((images, sums, width), F32), (1, sums, width), lambda i: (i, 0, 0))],
        scalars=(lengths,),
        flops=1,
        moved=1,
        deps=deps,
    )


def pre_attention(mask, mod, bias, x, upstream):
    normed, _ = norm(x)
    dm = mask * mod[GATE_TWO] * upstream
    return normed * (1.0 + mod[SCALE_ONE]) + mod[SHIFT_ONE], dm, total(dm), total(mask * x * x)


def pre_mlp(mask, mod, bias, x, att_own, att_peer):
    gated = mask * mod[GATE_ONE] * (att_own + att_peer + bias)
    residual = x + gated
    normed, _ = norm(residual)
    return residual, normed * (1.0 + mod[SCALE_TWO]) + mod[SHIFT_TWO], total(gated * gated)


def post_mlp(mask, mod, bias, residual, upstream, mlp_own, mlp_peer):
    branch = mlp_own + mlp_peer + bias
    gated = mask * mod[GATE_TWO] * branch
    return residual + gated, total(mask * branch * upstream), total(gated * gated)


def back_mlp(mask, mod, bias, residual, upstream, att_own, att_peer, da_own, da_peer):
    normed, inverse = norm(residual)
    da = da_own + da_peer
    dh = upstream + norm_back(da, normed, inverse, mod[SCALE_TWO])
    d_att = mask * mod[GATE_ONE] * dh
    branch = att_own + att_peer + bias
    return dh, d_att, total(mask * branch * dh), total(da), total(da * normed), total(d_att)


def back_attention(mask, mod, bias, x, dh, da_own, da_peer):
    normed, inverse = norm(x)
    da = da_own + da_peer
    return dh + norm_back(da, normed, inverse, mod[SCALE_ONE]), total(da), total(da * normed)


def ring(count, shift):
    return [(i, (i + shift) % count) for i in range(count)]


def take(array, index, axis):
    return lax.dynamic_index_in_dim(array, index, axis, keepdims=False)


def local(
    sizes,
    patches,
    conditioning,
    time_bins,
    lengths,
    positions,
    time_table,
    w_ada,
    b_ada,
    w_qkv,
    w_out,
    branch_bias,
    w_gu,
    w_down,
    d_out,
):
    axes = tuple(sizes)
    ny, nx, nc, tn = sizes.values()
    square = nx == 2 and ny == 2
    at_y, at_x, at_c, at_z = (lax.axis_index(name) for name in axes)
    at_q = at_y * nx + at_x
    devices = ny * nx * nc * tn
    image_count, width = conditioning.shape
    rows = patches.shape[0]
    seq = rows // image_count
    heads = w_qkv.shape[2] // HD // nc
    hw = heads * HD
    units = w_gu.shape[2] // nc
    strip = width // (ny * nx * nc)
    place = jnp.stack([at_q, at_c, at_z]).astype(jnp.int32)
    swap = ring(2, 1)

    def peer(value):
        return lax.ppermute(value, "c", ring(nc, 1))

    def core_share(weight, axis):
        size = weight.shape[axis] // nc
        return lax.dynamic_slice_in_dim(weight, at_c * size, size, axis)

    def later(values, marks):
        return lax.optimization_barrier((values, marks))[0] if marks else values

    def along_z(piece):
        return lax.all_to_all(jnp.broadcast_to(piece[None], (tn,) + piece.shape), "z", 0, 0)

    def plane_parts(near):
        half = (near.shape[1] // 2 + 15) // 16 * 16
        others = [take(near, (at_z + tn - r) % tn, 0) for r in range(1, tn)]
        return jnp.stack([x[:half] for x in others]), jnp.stack([x[half:] for x in others])

    def plane_first(parts, *marks):
        first, second = parts
        first_x = lax.ppermute(first, "x", swap)
        second_y = lax.ppermute(second, "y", swap)
        first_x, second_y = later((first_x, second_y), marks)
        return jnp.stack([first, first_x]), jnp.stack([second, second_y])

    def plane_second(pairs, *marks):
        crossed = lax.ppermute(pairs[0], "y", swap), lax.ppermute(pairs[1], "x", swap)
        return later(crossed, marks)

    def chunk(near, pairs, crossed):
        return near, pairs[0], pairs[1], crossed[0], crossed[1]

    def plane_plain(near, base):
        whole = lax.all_gather(near, ("y", "x"), axis=1)
        return whole.reshape((tn,) + base.shape)

    qkv_t = w_qkv.transpose(1, 2, 0)
    if square:
        heads_piece = jnp.where(
            at_q < 3,
            lax.dynamic_slice(qkv_t, (jnp.minimum(at_q, 2), at_c * hw, 0), (1, hw, width))[0],
            core_share(w_out, 0),
        )
    heads_own = jnp.concatenate([core_share(qkv_t, 1), core_share(w_out, 0)[None]], axis=0)
    gu_own = core_share(w_gu.transpose(1, 2, 0), 1).reshape(4, units // 2, width)
    down_own = core_share(w_down, 0).reshape(4, units // 4, width)
    if square:
        near_heads = along_z(heads_piece)
    else:
        flat = lambda own: take(own.reshape(ny * nx, -1, width), at_q, 0)
        heads_all, gu_all, down_all = (
            plane_plain(along_z(flat(own)), own) for own in (heads_own, gu_own, down_own)
        )

    def reduce_first(pairs, parts, deps=()):
        outs = grad_split(place, pairs, parts, deps)
        sent, kept = tuple(outs[::2]), tuple(outs[1::2])
        got = tuple(lax.ppermute(x, part[2], swap) for x, part in zip(sent, parts))
        return (kept, got), sent

    def reduce_send(state, *marks):
        kept, got = later(state, marks)
        return tuple((k[1].astype(F32) + g[1].astype(F32)).astype(BF) for k, g in zip(kept, got))

    def reduce_second(state, sends, parts, *marks):
        other = {"x": "y", "y": "x"}
        got = tuple(lax.ppermute(x, other[part[2]], swap) for x, part in zip(sends, parts))
        got = later(got, marks)
        return tuple(
            (k[0].astype(F32) + g[0].astype(F32) + h.astype(F32)).astype(BF)
            for k, g, h in zip(*state, got)
        )

    def reduce_plain(pairs):
        flip = lambda right: right.swapaxes(1, 2) if right.shape[2] == 2 * rows else right
        full = jnp.concatenate(
            [
                jnp.einsum(
                    "rd,zrn->zdn", jnp.concatenate(both), flip(right), preferred_element_type=F32
                )
                for both, right in pairs
            ],
            axis=2,
        )
        full = full.astype(BF).reshape(full.shape[0], ny * nx, nc, strip, -1)
        summed = lax.psum_scatter(full, ("y", "x"), scatter_dimension=1, tiled=False)
        return jnp.stack([take(summed, at_c, 1), take(summed, 1 - at_c, 1)], axis=1)

    def reduce_z(rows, *marks):
        return later(lax.all_to_all(rows, "z", 0, 0), marks)

    def reduce_z_steps(rows, *marks):
        got = [take(rows, at_z, 0)]
        for r in range(1, tn):
            sent = take(rows, (at_z + tn - r) % tn, 0)
            got.append(lax.ppermute(sent, "z", ring(tn, -r)))
        return jnp.stack(later(got, marks))

    def reduce_core(arrived):
        summed = jnp.sum(arrived.astype(F32), axis=0)
        own, got = summed[0], peer(summed[1].astype(BF)).astype(F32)
        first = at_c == 0
        return jnp.stack([jnp.where(first, own, got), jnp.where(first, got, own)])

    bins = jnp.arange(time_table.shape[0], dtype=jnp.int32)
    onehot = (time_bins[:, None] == bins[None, :]).astype(F32)
    cond_vec = conditioning + jnp.dot(onehot, time_table, precision=EXACT)
    cond_sig = jax.nn.sigmoid(cond_vec)
    silu_low = (cond_vec * cond_sig).astype(BF)
    mod = (dot(silu_low, w_ada) + b_ada).reshape(image_count, 6, width)
    bias_attn, bias_mlp = branch_bias[None, :width], branch_bias[None, width:]
    elementwise = functools.partial(by_image, lengths=lengths, mod=mod)
    a1_own, dm_own, sums_pre = elementwise(
        pre_attention, "pre_attention", rows_in=(patches, d_out), bias=bias_attn, outs=(BF, BF), sums=2
    )
    a1_all = (a1_own, peer(a1_own))
    facts = jnp.concatenate([positions.reshape(-1), lengths])
    facts_peer = peer(facts)
    lens = jnp.concatenate([lengths, facts_peer[2 * rows :]])
    pos = jnp.concatenate([positions, facts_peer[: 2 * rows].reshape(2, rows)], axis=1).astype(F32)
    quarter = HD // 4
    frequency = 10000.0 ** (-jnp.arange(quarter, dtype=F32) / quarter)
    angle = pos[:, None, :] * frequency[None, :, None]
    cosine, sine = jnp.cos(angle), jnp.sin(angle)
    cos = jnp.concatenate([cosine[0], cosine[0], cosine[1], cosine[1]], axis=0)
    sin = jnp.concatenate([sine[0], sine[0], sine[1], sine[1]], axis=0)
    def spread(value):
        return lax.all_to_all(jnp.broadcast_to(value[None], (devices,) + value.shape), axes, 0, 0)

    early = jnp.concatenate([silu_low.astype(F32), time_bins[:, None].astype(F32)], axis=1)
    own_heads = attn_fwd(
        lens, place, a1_all, heads_own[None], 1, tn, (), (), cos, sin, heads, seq
    )

    def attend(deps):
        return attn_fwd(
            lens, place, a1_all, heads_all, tn - 1, tn, tuple(own_heads[:4]), own_heads[4:],
            cos, sin, heads, seq, deps=deps,
        )

    def into_mlp(deps):
        return elementwise(
            pre_mlp,
            "pre_mlp",
            rows_in=(patches,) + att,
            bias=bias_attn,
            outs=(F32, BF),
            sums=1,
            deps=deps,
        )

    if square:
        gu_piece, near_heads = later((take(gu_own, at_q, 0), near_heads), (a1_own,))
        near_gu = along_z(gu_piece)
        pairs_heads = plane_first(plane_parts(near_heads))
        crossed_heads = plane_second(pairs_heads, own_heads[4])
        near_gu = later(near_gu, (crossed_heads,))
        parts_gu = plane_parts(near_gu)
        down_piece = later(take(down_own, at_q, 0), (near_gu,))
        near_down = along_z(down_piece)
        heads_all = assemble(
            place, heads_own, [chunk(near_heads, pairs_heads, crossed_heads)], deps=parts_gu
        )
        pairs_gu = plane_first(parts_gu, heads_all)
        q, k, v, attended, att_own, att_peer = attend(pairs_gu)
        crossed_gu = plane_second(pairs_gu, att_own)
        near_down = later(near_down, (att_own,))
        parts_down = plane_parts(near_down)
        att = (att_own, peer(att_peer))
        early = later(early, (near_down,))
        residual, a2_own, sums_att = into_mlp(crossed_gu + parts_down)
        pairs_down = plane_first(parts_down, a2_own)
        gu_all = assemble(place, gu_own, [chunk(near_gu, pairs_gu, crossed_gu)], deps=(a2_own,))
        early_all = spread(early)
        wait_mlp = pairs_down + (early_all,)
    else:
        q, k, v, attended, att_own, att_peer = attend(())
        att = (att_own, peer(att_peer))
        residual, a2_own, sums_att = into_mlp(())
        wait_mlp = ()
        early_all = spread(early)
    a2_all = (a2_own, peer(a2_own))
    dm_all = (dm_own, peer(dm_own))
    gate_up, hidden = mlp_fwd(a2_all, gu_all, deps=wait_mlp)

    def finish_mlp(deps):
        return elementwise(
            post_mlp,
            "post_mlp",
            rows_in=(residual, d_out, mlp_own, peer(mlp_peer)),
            bias=bias_mlp,
            outs=(F32,),
            sums=2,
            deps=deps,
        )

    def through_mlp(deps):
        return elementwise(
            back_mlp,
            "back_mlp",
            rows_in=(residual, d_out) + att + (da2_own, peer(da2_peer)),
            bias=bias_attn,
            outs=(F32, BF),
            sums=4,
            deps=deps,
        )

    def back_heads(deps):
        return attn_bwd(
            lens, da_all, heads_all, (0, tn), (), cos, sin, q, k, v, heads, seq, deps=deps
        )

    def through_attention(deps):
        return elementwise(
            back_attention,
            "back_attention",
            rows_in=(patches, dh, da1_own, peer(da1_peer)),
            bias=bias_attn,
            outs=(F32,),
            sums=2,
            deps=deps,
        )

    if square:
        crossed_down = plane_second(pairs_down, hidden)
        mid = tn // 2
        down_parts = ((0, units, "x", 0, tn),)
        gu_parts = (
            (0, units, "x", 0, mid),
            (units, units, "y", 0, mid),
            (0, units, "x", mid, tn),
            (units, units, "y", mid, tn),
        )
        rest = 4 * hw - 512
        heads_parts = (
            (0, 256, "x", 0, tn),
            (256, 256, "y", 0, tn),
            (512, rest, "x", 0, mid),
            (512, rest, "y", mid, tn),
        )
        down_state, down_sent = reduce_first([(dm_all, hidden)], down_parts, crossed_down)
        down_all = assemble(
            place, down_own, [chunk(near_down, pairs_down, crossed_down)], deps=down_sent
        )
        d_gate_up = mlp_mid(dm_all, down_all, gate_up, deps=down_sent)
        gu_state, gu_sent = reduce_first([(a2_all, d_gate_up)], gu_parts)
        one, two = ((gu_state[0][k : k + 2], gu_state[1][k : k + 2]) for k in (0, 2))
        down_sends = reduce_send(down_state, gu_sent)
        da2_own, da2_peer = back_out(d_gate_up, gu_all, "mlp_back", deps=gu_sent + down_sends)
        one_sends = reduce_send(one, da2_own)
        dh, da_own, sums_back = through_mlp(one_sends)
        da_all = (da_own, peer(da_own))
        two_sends = reduce_send(two, da_own)
        one_rows = reduce_second(one, one_sends, gu_parts[:2], da_own)
        d_qkv, da1_own, da1_peer = back_heads(down_sends + two_sends + one_rows)
        down_rows = reduce_second(down_state, down_sends, down_parts, d_qkv)
        two_rows = reduce_second(two, two_sends, gu_parts[2:], d_qkv)
        gu_rows = jnp.concatenate(
            [jnp.concatenate(half, axis=3) for half in (one_rows, two_rows)], axis=0
        )
        mlp_rows = jnp.concatenate([gu_rows, down_rows[0]], axis=3)
        heads_state, heads_sent = reduce_first(
            [(a1_all, d_qkv), (da_all, attended)], heads_parts, (mlp_rows,)
        )
        d_inputs, sums_one = through_attention(heads_sent)
        mlp_own, mlp_peer = back_out(hidden, down_all, "mlp_out", deps=(sums_one,))
        mlp_z = reduce_z(mlp_rows, mlp_own)
        heads_sends = reduce_send(heads_state, mlp_own)
        output, sums_mlp = finish_mlp(heads_sends)
        heads_rows = reduce_second(heads_state, heads_sends, heads_parts, sums_mlp)
        heads_rows = jnp.concatenate(
            heads_rows[:2] + (jnp.concatenate(heads_rows[2:], axis=0),), axis=3
        )
        grad_mlp = reduce_core(mlp_z)
        grad_gu, grad_down = grad_mlp[:, :, : 2 * units], grad_mlp[:, :, 2 * units :]
    else:
        d_gate_up = mlp_mid(dm_all, down_all, gate_up)
        da2_own, da2_peer = back_out(d_gate_up, gu_all, "mlp_back")
        dh, da_own, sums_back = through_mlp(())
        da_all = (da_own, peer(da_own))
        mlp_own, mlp_peer = back_out(hidden, down_all, "mlp_out")
        output, sums_mlp = finish_mlp(())
        d_qkv, da1_own, da1_peer = back_heads(())
        d_inputs, sums_one = through_attention(())
        grad_down, grad_gu, grad_heads = (
            reduce_core(reduce_z(reduce_plain(pairs)))
            for pairs in (
                [(dm_all, hidden)],
                [(a2_all, d_gate_up)],
                [(a1_all, d_qkv), (da_all, attended)],
            )
        )

    d_mod = jnp.concatenate([sums_one, sums_back[:, :3], sums_mlp[:, :1]], axis=1)
    d_mod = d_mod.reshape(image_count, 6 * width)
    d_bias = jnp.concatenate([jnp.sum(sums_back[:, 3], axis=0), jnp.sum(sums_pre[:, 0], axis=0)])
    sums = jnp.stack(
        [
            jnp.sum(sums_pre[:, 1]),
            jnp.sum(sums_att),
            jnp.sum(sums_mlp[:, 1]),
            jnp.sum(lengths).astype(F32),
        ]
    )
    ada_cols, bias_cols = 6 * width // devices, 2 * width // devices
    ready = jnp.concatenate(
        [
            d_mod.reshape(image_count, devices, ada_cols).transpose(1, 0, 2).reshape(devices, -1),
            d_bias.reshape(devices, bias_cols),
            jnp.broadcast_to(sums[None], (devices, 4)),
        ],
        axis=1,
    )
    if square:
        ready, mlp_z = lax.optimization_barrier((ready, mlp_z))
    arrived = lax.all_to_all(ready, axes, 0, 0, tiled=True)
    if square:
        d_mod, heads_rows = lax.optimization_barrier((d_mod, heads_rows))
    d_silu = dot_nt(d_mod.astype(BF), w_ada)
    d_cond = d_silu * cond_sig * (1.0 + cond_vec * (1.0 - cond_sig))
    if square:
        arrived, d_cond = lax.optimization_barrier((arrived, d_cond))
    d_cond_all = spread(d_cond).reshape(devices * image_count, width)
    if square:
        grad_heads = reduce_core(reduce_z_steps(heads_rows, d_cond_all))
    ends = np.cumsum([0, image_count * ada_cols, bias_cols, 4])
    d_mod_all, bias_all, sums_all = (
        arrived[:, start:stop] for start, stop in zip(ends[:-1], ends[1:])
    )
    d_mod_all = d_mod_all.reshape(devices * image_count, ada_cols)
    grad_b_ada = jnp.sum(d_mod_all, axis=0)
    grad_bias = jnp.sum(bias_all, axis=0)
    sums_all = jnp.sum(sums_all, axis=0)
    rms_values = jnp.sqrt(sums_all[:3] / (sums_all[3] * width))
    early_all = early_all.reshape(devices * image_count, -1)
    silu_all, bins_all = early_all[:, :width].astype(BF), early_all[:, width].astype(jnp.int32)
    grad_ada = dot_tn(silu_all, d_mod_all.astype(BF))
    table_rows = time_table.shape[0] // devices
    flat = (at_q * nc + at_c) * tn + at_z
    own_bins = flat * table_rows + jnp.arange(table_rows, dtype=jnp.int32)
    picks = (own_bins[:, None] == bins_all[None, :]).astype(F32)
    grad_table = jnp.dot(picks, d_cond_all, precision=EXACT)

    def joined(value, parts):
        both = [value[j].reshape(strip, parts, -1) for j in range(nc)]
        return jnp.concatenate(both, axis=2)

    return (
        output,
        d_inputs,
        d_cond,
        joined(grad_heads[:, :, : 3 * hw], 3),
        joined(grad_heads[:, :, 3 * hw :], 1)[:, 0].T,
        joined(grad_gu, 2),
        joined(grad_down, 1)[:, 0].T,
        grad_ada,
        grad_b_ada,
        grad_bias,
        grad_table,
        rms_values,
    )


def solution(mesh):
    groups, tn = mesh.shape["dp"], mesh.shape["tensor"]
    nc, nx = 2, 2
    sizes = {"y": groups // (nx * nc), "x": nx, "c": nc, "z": tn}
    fine = Mesh(mesh.devices.reshape(tuple(sizes.values())), tuple(sizes))
    dp = ("y", "x", "c")
    every = dp + ("z",)
    return jax.shard_map(
        functools.partial(local, sizes),
        mesh=fine,
        in_specs=(
            P(every, None),
            P(every, None),
            P(every),
            P(every),
            P(None, every),
            P(),
            P(),
            P(),
            P(None, None, "z"),
            P("z", None),
            P(),
            P(None, None, "z"),
            P("z", None),
            P(every, None),
        ),
        out_specs=(
            P(every, None),
            P(every, None),
            P(every, None),
            P(dp, None, "z"),
            P("z", dp),
            P(dp, None, "z"),
            P("z", dp),
            P(None, every),
            P(every),
            P(every),
            P(every, None),
            P(),
        ),
        check_vma=False,
    )
```

time: 614 us -> 499 us (0.81)
  waiting for transfers between devices: 164 us -> 72.2 us
  local copies, waits for them, and re-layouts: 79 us -> 45.6 us
  other arithmetic: 50.6 us -> 68.8 us
  Pallas kernels: 220 us -> 205 us
  starting transfers between devices: 65.9 us -> 73.3 us
    ppermute x46 -> x33, waiting for transfers between devices: 150 us -> 50.4 us  [the longest x9 18.2 us: reduce_second(): lax.ppermute(x, other[part[2]], swap)]
    all_to_all x2 -> x7, starting transfers between devices: 7.76 us -> 30.6 us  [the longest x3 14.5 us: along_z(): lax.all_to_all(jnp.broadcast_to(piece[None], (tn,) + piece.shape), 'z', 0...]
    convert_element_type x7 -> x19, other arithmetic: 8.34 us -> 25.3 us  [the longest x9 12.6 us: reduce_send(): (k[1].astype(F32) + g[1].astype(F32)).astype(BF)]
    ppermute x46 -> x33, starting transfers between devices: 56.4 us -> 40.1 us  [the longest x9 10.3 us: reduce_first(): lax.ppermute(x, part[2], swap)]
    pallas_call x22 -> x18, Pallas kernels: 220 us -> 205 us  [call(): pl.pallas_call(body, grid_spec=pltpu.PrefetchScalarGridSpec(num_scalar_pr...]
    squeeze x12 -> x0, local copies, waits for them, and re-layouts: 10.6 us -> none  [the longest x3 2.93 us: weight_gather(): second_x[j]]
    pallas_call x6 -> x0, local copies, waits for them, and re-layouts: 9.81 us -> none  [call(): pl.pallas_call(body, grid_spec=pltpu.PrefetchScalarGridSpec(num_scalar_pr...]
    all_to_all x2 -> x7, waiting for transfers between devices: 13.3 us -> 20.6 us  [the longest x1 14.2 us: local(): arrived = lax.all_to_all(ready, axes, 0, 0, tiled=True)]
  transfers between devices with their start and end apart: 60 -> 51, of which waited for: 20 -> 16; matrix products, arithmetic and copies ran while one was open for 22% -> 24% of each run, Pallas kernels for 36% -> 39%
where the time goes in v2:
time: 499 us; the launch traced here: 491 us
  Pallas kernels  205 us (41%)
  starting transfers between devices  73.3 us (15%)
  waiting for transfers between devices  72.2 us (14%)
  other arithmetic  68.8 us (14%)
  local copies, waits for them, and re-layouts  45.6 us (9%)
  matrix products  23.4 us (5%)
    pallas_call x18, Pallas kernels, call(): pl.pallas_call(body, grid_spec=pltpu.PrefetchScalarGridSpec(num_scalar_pr...  205 us
    ppermute x9, waiting for transfers between devices, reduce_second(): lax.ppermute(x, other[part[2]], swap)  18.2 us
    all_to_all x3, starting transfers between devices, along_z(): lax.all_to_all(jnp.broadcast_to(piece[None], (tn,) + piece.shape), 'z', 0...  14.5 us
    all_to_all x1, waiting for transfers between devices, local(): arrived = lax.all_to_all(ready, axes, 0, 0, tiled=True)  14.2 us
    convert_element_type x9, other arithmetic, reduce_send(): (k[1].astype(F32) + g[1].astype(F32)).astype(BF)  12.6 us
    convert_element_type x9, other arithmetic, reduce_second(): (k[0].astype(F32) + g[0].astype(F32) + h.astype(F32)).astype(BF)  12 us
    another operation x12, other arithmetic, plane_first(): return (jnp.stack([first, first_x]), jnp.stack([second, second_y]))  11.9 us
    ppermute x9, waiting for transfers between devices, reduce_first(): lax.ppermute(x, part[2], swap)  11.8 us
  transfers between devices with their start and end apart: 51, of which 16 were waited for; matrix products, arithmetic and copies ran while one was open for 24% of the time, Pallas kernels for 39%

profile of v2, /device:TPU:0, one launch (start us, length us, event | category | flops | bytes accessed | tf_op | source)
XLA Modules:
  0.0 491.3 jit_solution(17552748666364674068)
XLA Ops:
  6.4 6.0 %all-to-all-start = ((bf16[4,144,1152]{2,1,0:T(8,128)(2,1)}), bf16[4,144,1152]{2,1,0:T(8,128)(2,1)}, u32[]{:S(2)}, u32[]{:S(2)}) async-start(bf16[4,144,1152]{2,1,0:T(8,128)(2,1)} %broadcast_in_dim.23), calls=%async_computation | async-start | bytes 2654208 | tf_op jit(solution)/shard_map/all_to_all | solution.py:626
  13.6 3.1 fusion.36
  16.8 8.3 %convolution_add_fusion = f32[2,6912]{1,0:T(2,128)} fusion(bf16[1152,6912]{1,0:T(8,128)(2,1)} %param.23, f32[6912]{0:T(1024)S(1)} %copy-done.64, f32[2,1152]{1,0:T(2,128)S(1)} %get-tuple-element.301), kind=kOutput, calls=%fused_computation | convolution fusion | flops 31875840 | bytes 16017408 | tf_op jit(solution)/shard_map/dot_general | solution.py:26
  26.6 4.8 pre_attention.1
  31.6 2.4 dynamic-slice_bitcast_fusion
  34.1 5.6 %copy.44 = bf16[2,384,1152]{2,1,0:T(8,128)(2,1)S(1)} copy(bf16[2,384,1152]{1,0,2:T(2,128)(2,1)} %dynamic-slice_bitcast_fusion) | data formatting | bytes 3538944 | tf_op jit(solution)/shard_map/dynamic_slice | solution.py:620
  46.2 3.8 all-to-all-start.1
  58.4 6.0 %collective-permute-done.3 = bf16[3,64,1152]{2,1,0:T(8,128)(2,1)} collective-permute-done((bf16[3,64,1152]{2,1,0:T(8,128)(2,1)}, bf16[3,64,1152]{2,1,0:T(8,128)(2,1)}, u32[]{:S(2)}, u32[]{:S(2)}) %collective-permute-start.3) | collective-permute-done | bytes 442400 | tf_op jit(solution)/shard_map/ppermute | solution.py:636
  67.1 4.1 collective-permute-done.2
  77.3 10.5 %attn_fwd.2 = (bf16[4,2,72,1024]{3,2,1,0:T(8,128)(2,1)}, bf16[4,2,72,1024]{3,2,1,0:T(8,128)(2,1)}, bf16[4,2,72,1024]{3,2,1,0:T(8,128)(2,1)}, bf16[4,144,1024]{2,...) custom-call(s32[4]{0:T(128)} %pad_add_fusion.1.refs_0_, s32[3]{0:T(128)} %pad_add_fusion.2.refs_1_.refs_0_, ...), custom_call_target="tpu_custom_call" | custom-call | flops 3112173568 | bytes 20000000 | tf_op jit(solution)/shard_map/attn_fwd/pallas_call | solution.py:52
  89.0 8.2 %collective-permute-done.4.refs_5_ = bf16[2,3,80,1152]{3,2,1,0:T(8,128)(2,1)S(1)} collective-permute-done((bf16[2,3,80,1152]{3,2,1,0:T(8,128)(2,1)S(1)}, bf16[2,3,80,1152]{3,2,1,0:T(8,128)(2,1)S(1)}, u32[]{:S(2)}, u32[]{:S(2)}) %collective-permute-start.4) | collective-permute-done | bytes 1105952 | tf_op jit(solution)/shard_map/ppermute | solution.py:641
  103.7 4.7 all-to-all-start.2
  108.4 6.5 %assemble.3.refs_7_.refs_9_ = bf16[4,4,144,1152]{3,2,1,0:T(8,128)(2,1)} custom-call(s32[3]{0:T(128)} %pad_add_fusion.2.refs_1_.refs_0_, bf16[4,144,1152]{2,1,0:T(8,128)(2,1)} %get-tuple-element.261.refs_1_, bf16[4,144,1152]{2,1,0:T(8,128)(2,1)} %all-to-all-done.refs_2_, bf16[2,3,80,1152]{3,2,1,0:T(8,128)(2,1)} %copy-done.8, ...), custom_call_target="tpu_custom_call" | custom-call | bytes 10616832 | tf_op jit(solution)/shard_map/assemble/pallas_call | solution.py:52
  114.9 2.4 pad_maximum_fusion.3.refs_11_.refs_4_
  118.1 2.3 pad_maximum_fusion.2.refs_10_.refs_3_
  121.9 23.6 %attn_fwd.3 = (bf16[4,2,72,1024]{3,2,1,0:T(8,128)(2,1)}, bf16[4,2,72,1024]{3,2,1,0:T(8,128)(2,1)}, bf16[4,2,72,1024]{3,2,1,0:T(8,128)(2,1)}, bf16[4,144,1024]{2,...) custom-call(s32[4]{0:T(128)} %pad_add_fusion.1.refs_0_, ...), custom_call_target="tpu_custom_call", output_to_operand_aliasing={{0}: (12, {}), {1}: (13, {}), {2}: (14, {}), {3}: (15, {})} | custom-call | flops 9336520704 | bytes 20000000 | tf_op jit(solution)/shard_map/attn_fwd/pallas_call | solution.py:52
  149.0 5.1 %pre_mlp.1 = (f32[512,1152]{1,0:T(8,128)}, bf16[512,1152]{1,0:T(8,128)(2,1)}, f32[2,1,1152]{2,1,0:T(1,128)}) custom-call(s32[2]{0:T(128)} %refs_0_.9, f32[2,6,1152]{2,1,0:T(8,128)} %reshape.201.refs_1_, f32[1,1152]{1,0:T(1,128)} %broadcast_in_dim.21.refs_2_, f32[512,1152]{1,0:T(8,128)} %refs_3_.5, f32[512,1152]{1,0:T(8,128)} %get-tuple-element.131.refs_4_.refs_5_, ...), custom_call_target="tpu_custom_call" | custom-call | flops 1 | bytes 1 | tf_op jit(solution)/shard_map/pre_mlp/pallas_call | solution.py:52
  157.4 5.4 %all-to-all-start.3 = ((f32[32,2,1153]{2,1,0:T(2,128)}), f32[32,2,1153]{2,1,0:T(2,128)S(1)}, u32[]{:S(2)}, u32[]{:S(2)}) async-start(f32[32,2,1153]{2,1,0:T(2,128)} %broadcast_in_dim.27), calls=%async_computation.3 | async-start | bytes 655360 | tf_op jit(solution)/shard_map/all_to_all | solution.py:742
  163.2 7.6 %assemble.4.refs_2_.refs_1_ = bf16[4,4,192,1152]{3,2,1,0:T(8,128)(2,1)} custom-call(s32[3]{0:T(128)} %pad_add_fusion.2.refs_1_.refs_0_, bf16[4,192,1152]{2,1,0:T(8,128)(2,1)} %bitcast.181, bf16[4,192,1152]{2,1,0:T(8,128)(2,1)} %copy-done.2, bf16[2,3,96,1152]{3,2,1,0:T(8,128)(2,1)} %pad_maximum_fusion.2.refs_10_.refs_3_, ...), custom_call_target="tpu_custom_call" | custom-call | bytes 14155776 | tf_op jit(solution)/shard_map/assemble/pallas_call | solution.py:52
  175.1 13.8 %mlp_fwd.1 = (f32[4,1024,768]{2,1,0:T(8,128)}, bf16[4,1024,384]{2,1,0:T(8,128)(2,1)}) custom-call(bf16[512,1152]{1,0:T(8,128)(2,1)} %get-tuple-element.138.refs_7_.refs_0_.refs_1_, bf16[512,1152]{1,0:T(8,128)(2,1)} %collective-permute-done.11.refs_1_.refs_2_, bf16[4,4,192,1152]{3,2,1,0:T(8,128)(2,1)} %assemble.4.refs_2_.refs_1_, ...), custom_call_target="tpu_custom_call" | custom-call | flops 7247757312 | bytes 26000000 | tf_op jit(solution)/shard_map/mlp_fwd/pallas_call | solution.py:52
  189.8 10.2 %grad_split.3 = (bf16[2,4,2,144,384]{4,3,2,1,0:T(8,128)(2,1)}, bf16[2,4,2,144,384]{4,3,2,1,0:T(8,128)(2,1)}) custom-call(s32[3]{0:T(128)} %pad_add_fusion.2.refs_1_.refs_0_, bf16[512,1152]{1,0:T(8,128)(2,1)} %get-tuple-element.145.refs_1_.refs_0_, bf16[512,1152]{1,0:T(8,128)(2,1)} %collective-permute-done.16.refs_2_.refs_1_, ...), custom_call_target="tpu_custom_call" | custom-call | flops 3623878656 | bytes 9043968 | tf_op jit(solution)/shard_map/grad_split/pallas_call | solution.py:52
  201.1 5.5 %assemble.5.refs_2_.refs_1_ = bf16[4,4,96,1152]{3,2,1,0:T(8,128)(2,1)} custom-call(s32[3]{0:T(128)} %pad_add_fusion.2.refs_1_.refs_0_, bf16[4,96,1152]{2,1,0:T(8,128)(2,1)} %bitcast.183, bf16[4,96,1152]{2,1,0:T(8,128)(2,1)} %copy-done.4, bf16[2,3,48,1152]{3,2,1,0:T(8,128)(2,1)} %copy-done.13, bf16[2,3,48,1152]{3,2,1,0:T(8,128)(2,1)} %copy-done.11, ...), custom_call_target="tpu_custom_call" | custom-call | bytes 7077888 | tf_op jit(solution)/shard_map/assemble/pallas_call | solution.py:52
  206.7 12.2 %mlp_mid.1.refs_3_.refs_0_ = bf16[4,1024,768]{2,1,0:T(8,128)(2,1)} custom-call(bf16[512,1152]{1,0:T(8,128)(2,1)} %get-tuple-element.145.refs_1_.refs_0_, bf16[512,1152]{1,0:T(8,128)(2,1)} %collective-permute-done.16.refs_2_.refs_1_, bf16[4,4,96,1152]{3,2,1,0:T(8,128)(2,1)} %assemble.5.refs_2_.refs_1_, f32[4,1024,768]{2,1,0:T(8,128)} %get-tuple-element.147.refs_3_, ...), custom_call_target="tpu_custom_call" | custom-call | flops 3623878656 | bytes 26000000 | tf_op jit(solution)/shard_map/mlp_mid/pallas_call | solution.py:52
  218.8 14.6 %grad_split.4 = (bf16[2,2,2,144,384]{4,3,2,1,0:T(8,128)(2,1)}, bf16[2,2,2,144,384]{4,3,2,1,0:T(8,128)(2,1)}, bf16[2,2,2,144,384]{4,3,2,1,0:T(8,128)(2,1)}, bf16[...) custom-call(s32[3]{0:T(128)} %pad_add_fusion.2.refs_1_.refs_0_, ...), custom_call_target="tpu_custom_call" | custom-call | flops 7247757312 | bytes 15728640 | tf_op jit(solution)/shard_map/grad_split/pallas_call | solution.py:52
  235.8 5.9 %collective-permute-done.17 = bf16[2,4,2,144,384]{4,3,2,1,0:T(8,128)(2,1)S(1)} collective-permute-done((bf16[2,4,2,144,384]{4,3,2,1,0:T(8,128)(2,1)}, bf16[2,4,2,144,384]{4,3,2,1,0:T(8,128)(2,1)S(1)}, u32[]{:S(2)}, u32[]{:S(2)}) %collective-permute-start.17) | collective-permute-done | bytes 1769504 | tf_op jit(solution)/shard_map/ppermute | solution.py:672
  242.9 14.0 %mlp_back.1 = (f32[512,1152]{1,0:T(8,128)}, bf16[512,1152]{1,0:T(8,128)(2,1)}) custom-call(bf16[4,1024,768]{2,1,0:T(8,128)(2,1)} %mlp_mid.1.refs_3_.refs_0_, bf16[4,4,192,1152]{3,2,1,0:T(8,128)(2,1)} %assemble.4.refs_2_.refs_1_, bf16[2,2,2,144,384]{4,3,2,1,0:T(8,128)(2,1)} %get-tuple-element.148.refs_2_, ...), custom_call_target="tpu_custom_call" | custom-call | flops 7247757312 | bytes 16908288 | tf_op jit(solution)/shard_map/mlp_back/pallas_call | solution.py:52
  265.2 8.2 %back_mlp.1 = (f32[512,1152]{1,0:T(8,128)}, bf16[512,1152]{1,0:T(8,128)(2,1)}, f32[2,4,1152]{2,1,0:T(4,128)}) custom-call(s32[2]{0:T(128)} %refs_0_.9, f32[2,6,1152]{2,1,0:T(8,128)} %reshape.201.refs_1_, f32[1,1152]{1,0:T(1,128)} %broadcast_in_dim.21.refs_2_, f32[512,1152]{1,0:T(8,128)} %get-tuple-element.137.refs_3_, f32[512,1152]{1,0:T(8,128)} %refs_4_.5, ...), custom_call_target="tpu_custom_call" | custom-call | flops 1 | bytes 1 | tf_op jit(solution)/shard_map/back_mlp/pallas_call | solution.py:52
  273.5 15.2 %collective-permute-done.25 = bf16[2,2,144,384]{3,2,1,0:T(8,128)(2,1)} collective-permute-done((bf16[2,2,144,384]{3,2,1,0:T(8,128)(2,1)S(1)}, bf16[2,2,144,384]{3,2,1,0:T(8,128)(2,1)}, u32[]{:S(2)}, u32[]{:S(2)}) %collective-permute-start.25) | collective-permute-done | bytes 442400 | tf_op jit(solution)/shard_map/ppermute | solution.py:681
  290.2 2.0 fusion.16.refs_12_
  295.9 2.1 fusion.7.refs_14_
  299.9 30.8 %attn_bwd.1 = (bf16[4,432,1024]{2,1,0:T(8,128)(2,1)}, f32[512,1152]{1,0:T(8,128)}, bf16[512,1152]{1,0:T(8,128)(2,1)}) custom-call(s32[4]{0:T(128)} %pad_add_fusion.1.refs_0_, bf16[512,1152]{1,0:T(8,128)(2,1)} %get-tuple-element.164.refs_1_.refs_3_, bf16[512,1152]{1,0:T(8,128)(2,1)} %collective-permute-done.21.refs_2_.refs_4_, ...), custom_call_target="tpu_custom_call" | custom-call | flops 16173236224 | bytes 20000000 | tf_op jit(solution)/shard_map/attn_bwd/pallas_call | solution.py:52
  336.3 15.9 %grad_split.5 = (bf16[2,4,2,144,256]{4,3,2,1,0:T(8,128)(2,1)}, bf16[2,4,2,144,256]{4,3,2,1,0:T(8,128)(2,1)}, bf16[2,4,2,144,256]{4,3,2,1,0:T(8,128)(2,1)}, bf16[...) custom-call(s32[3]{0:T(128)} %pad_add_fusion.2.refs_1_.refs_0_, ...), custom_call_target="tpu_custom_call" | custom-call | flops 5435817984 | bytes 12386304 | tf_op jit(solution)/shard_map/grad_split/pallas_call | solution.py:52
  359.3 4.8 all-to-all-start.4
  365.8 6.2 %back_attention.1 = (f32[512,1152]{1,0:T(8,128)}, f32[2,2,1152]{2,1,0:T(2,128)}) custom-call(s32[2]{0:T(128)} %refs_0_.9, f32[2,6,1152]{2,1,0:T(8,128)} %reshape.201.refs_1_, f32[1,1152]{1,0:T(1,128)} %broadcast_in_dim.21.refs_2_, f32[512,1152]{1,0:T(8,128)} %refs_3_.5, f32[512,1152]{1,0:T(8,128)} %get-tuple-element.163.refs_4_, ...), custom_call_target="tpu_custom_call" | custom-call | flops 1 | bytes 1 | tf_op jit(solution)/shard_map/back_attention/pallas_call | solution.py:52
  372.0 9.8 %mlp_out.1 = (f32[512,1152]{1,0:T(8,128)}, bf16[512,1152]{1,0:T(8,128)(2,1)}) custom-call(bf16[4,1024,384]{2,1,0:T(8,128)(2,1)} %get-tuple-element.142.refs_3_.refs_0_, bf16[4,4,96,1152]{3,2,1,0:T(8,128)(2,1)} %assemble.5.refs_2_.refs_1_, f32[2,2,1152]{2,1,0:T(2,128)} %get-tuple-element.187.refs_2_), custom_call_target="tpu_custom_call" | custom-call | flops 3623878656 | bytes 10223616 | tf_op jit(solution)/shard_map/mlp_out/pallas_call | solution.py:52
  381.7 4.7 collective-permute-done.33
  389.5 2.0 fusion.11.refs_7_
  401.9 5.7 %post_mlp.1 = (f32[512,1152]{1,0:T(8,128)}, f32[2,2,1152]{2,1,0:T(2,128)}) custom-call(s32[2]{0:T(128)} %refs_0_.9, f32[2,6,1152]{2,1,0:T(8,128)} %reshape.201.refs_1_, f32[1,1152]{1,0:T(1,128)} %broadcast_in_dim.20.refs_2_, f32[512,1152]{1,0:T(8,128)} %get-tuple-element.137.refs_3_, f32[512,1152]{1,0:T(8,128)} %refs_4_.5, ...), custom_call_target="tpu_custom_call" | custom-call | flops 1 | bytes 1 | tf_op jit(solution)/shard_map/post_mlp/pallas_call | solution.py:52
  407.6 2.9 collective-permute-done.37
  419.2 2.3 dynamic-slice_bitcast_fusion.3
  423.1 2.4 collective-permute-start.40
  429.4 9.7 %fusion = f32[2,1152]{1,0:T(2,128)S(1)} fusion(bf16[1152,6912]{1,0:T(8,128)(2,1)} %param.23, bf16[2,6912]{1,0:T(2,128)(2,1)S(1)} %bitcast.197, f32[2,1152]{1,0:T(2,128)S(1)} %get-tuple-element.301), kind=kOutput, calls=%fused_computation.6 | convolution fusion | flops 31868928 | bytes 15971328 | tf_op jit(solution)/shard_map/dot_general | solution.py:30
  441.3 2.6 all-to-all-start.5
  445.2 14.2 %all-to-all-done.5 = f32[32,1,508]{2,1,0:T(1,128)S(1)} async-done(((f32[32,1,508]{2,1,0:T(1,128)}), f32[32,1,508]{2,1,0:T(1,128)S(1)}, u32[]{:S(2)}, u32[]{:S(2)}) %all-to-all-start.5) | async-done | bytes 65056 | tf_op jit(solution)/shard_map/all_to_all | solution.py:930
  462.7 3.3 all-to-all-start.6
  471.7 4.9 all-to-all-done.6
  484.6 2.3 pad_maximum_fusion.6
  486.9 2.3 copy.51
  (344 shorter events, 137.3 us)
Async XLA Ops:
  2.9 54.7 %collective-permute-start = (s32[1026]{0:T(1024)}, s32[1026]{0:T(1024)}, u32[]{:S(2)}, u32[]{:S(2)}) collective-permute-start(s32[1026]{0:T(1024)} %pad_add_fusion), channel_id=1, source_target_pairs={{0,4},{4,0},{1,5},{5,1},{2,6},{6,2},{3,7},{7,3},{8,12},{12,8},{9,1... | collective-permute-start | bytes 12320 | tf_op jit(solution)/shard_map/ppermute | solution.py:616
  6.4 38.5 %all-to-all-start = ((bf16[4,144,1152]{2,1,0:T(8,128)(2,1)}), bf16[4,144,1152]{2,1,0:T(8,128)(2,1)}, u32[]{:S(2)}, u32[]{:S(2)}) async-start(bf16[4,144,1152]{2,1,0:T(8,128)(2,1)} %broadcast_in_dim.23), calls=%async_computation | async-start | bytes 2654208 | tf_op jit(solution)/shard_map/all_to_all | solution.py:626
  31.4 45.9 %collective-permute-start.1 = (bf16[512,1152]{1,0:T(8,128)(2,1)}, bf16[512,1152]{1,0:T(8,128)(2,1)}, u32[]{:S(2)}, u32[]{:S(2)}) collective-permute-start(bf16[512,1152]{1,0:T(8,128)(2,1)} %get-tuple-element.117.refs_2_.refs_1_), channel_id=1, source_target_pairs={{0,4},{4,0},{1,5},{5,1},{2,6},{6,2},{3,7},{7,3},{8,12},{12,8},{9,1... | collective-permute-start | bytes 3538952 | tf_op jit(solution)/shard_map/ppermute | solution.py:616
  46.2 51.9 %all-to-all-start.1 = ((bf16[4,192,1152]{2,1,0:T(8,128)(2,1)}), bf16[4,192,1152]{2,1,0:T(8,128)(2,1)S(1)}, u32[]{:S(2)}, u32[]{:S(2)}) async-start(bf16[4,192,1152]{2,1,0:T(8,128)(2,1)} %broadcast_in_dim.25), calls=%async_computation.1 | async-start | bytes 3538944 | tf_op jit(solution)/shard_map/all_to_all | solution.py:626
  51.9 12.4 %collective-permute-start.3 = (bf16[3,64,1152]{2,1,0:T(8,128)(2,1)}, bf16[3,64,1152]{2,1,0:T(8,128)(2,1)}, u32[]{:S(2)}, u32[]{:S(2)}) collective-permute-start(bf16[3,64,1152]{2,1,0:T(8,128)(2,1)} %get-tuple-element.285), channel_id=1, source_target_pairs={{0,16},{16,0},{1,17},{17,1},{2,18},{18,2},{3,19},{19,3},{4,20},{20... | collective-permute-start | bytes 1327112 | tf_op jit(solution)/shard_map/ppermute | solution.py:636
  55.5 15.6 %collective-permute-start.2 = (bf16[3,80,1152]{2,1,0:T(8,128)(2,1)}, bf16[3,80,1152]{2,1,0:T(8,128)(2,1)S(1)}, u32[]{:S(2)}, u32[]{:S(2)}) collective-permute-start(bf16[3,80,1152]{2,1,0:T(8,128)(2,1)} %get-tuple-element.283), channel_id=1, source_target_pairs={{0,8},{8,0},{1,9},{9,1},{2,10},{10,2},{3,11},{11,3},{4,12},{12,4},... | collective-permute-start | bytes 1658888 | tf_op jit(solution)/shard_map/ppermute | solution.py:635
  65.5 23.5 %collective-permute-start.5 = (bf16[2,3,64,1152]{3,2,1,0:T(8,128)(2,1)S(1)}, bf16[2,3,64,1152]{3,2,1,0:T(8,128)(2,1)}, u32[]{:S(2)}, u32[]{:S(2)}) collective-permute-start(bf16[2,3,64,1152]{3,2,1,0:T(8,128)(2,1)S(1)} %pad_maximum_fusion.5.refs_4_), channel_id=1, source_target_pairs={{0,8},{8,0},{1,9},{9,1},{2,10},{10,2},{3,11},{11,3},{4,12},{12,4},... | collective-permute-start | bytes 2654216 | tf_op jit(solution)/shard_map/ppermute | solution.py:641
  73.1 24.0 %collective-permute-start.4 = (bf16[2,3,80,1152]{3,2,1,0:T(8,128)(2,1)S(1)}, bf16[2,3,80,1152]{3,2,1,0:T(8,128)(2,1)S(1)}, u32[]{:S(2)}, u32[]{:S(2)}) collective-permute-start(bf16[2,3,80,1152]{3,2,1,0:T(8,128)(2,1)S(1)} %pad_maximum_fusion.4.refs_3_), channel_id=1, source_target_pairs={{0,16},{16,0},{1,17},{17,1},{2,18},{18,2},{3,19},{19,3},{4,20},{20... | collective-permute-start | bytes 3317768 | tf_op jit(solution)/shard_map/ppermute | solution.py:641
  99.4 15.5 %collective-permute-start.7 = (bf16[3,96,1152]{2,1,0:T(8,128)(2,1)S(1)}, bf16[3,96,1152]{2,1,0:T(8,128)(2,1)}, u32[]{:S(2)}, u32[]{:S(2)}) collective-permute-start(bf16[3,96,1152]{2,1,0:T(8,128)(2,1)S(1)} %get-tuple-element.277.refs_8_), channel_id=1, source_target_pairs={{0,16},{16,0},{1,17},{17,1},{2,18},{18,2},{3,19},{19,3},{4,20},{20... | collective-permute-start | bytes 1990664 | tf_op jit(solution)/shard_map/ppermute | solution.py:636
  100.9 14.1 %collective-permute-start.6 = (bf16[3,96,1152]{2,1,0:T(8,128)(2,1)S(1)}, bf16[3,96,1152]{2,1,0:T(8,128)(2,1)}, u32[]{:S(2)}, u32[]{:S(2)}) collective-permute-start(bf16[3,96,1152]{2,1,0:T(8,128)(2,1)S(1)} %get-tuple-element.279.refs_7_), channel_id=1, source_target_pairs={{0,8},{8,0},{1,9},{9,1},{2,10},{10,2},{3,11},{11,3},{4,12},{12,4},... | collective-permute-start | bytes 1990664 | tf_op jit(solution)/shard_map/ppermute | solution.py:635
  103.7 41.8 %all-to-all-start.2 = ((bf16[4,96,1152]{2,1,0:T(8,128)(2,1)}), bf16[4,96,1152]{2,1,0:T(8,128)(2,1)S(1)}, u32[]{:S(2)}, u32[]{:S(2)}) async-start(bf16[4,96,1152]{2,1,0:T(8,128)(2,1)} %broadcast_in_dim.26), calls=%async_computation.2 | async-start | bytes 1769472 | tf_op jit(solution)/shard_map/all_to_all | solution.py:626
  117.4 30.1 %collective-permute-start.10 = (bf16[2,3,96,1152]{3,2,1,0:T(8,128)(2,1)}, bf16[2,3,96,1152]{3,2,1,0:T(8,128)(2,1)S(1)}, u32[]{:S(2)}, u32[]{:S(2)}) collective-permute-start(bf16[2,3,96,1152]{3,2,1,0:T(8,128)(2,1)} %pad_maximum_fusion.3.refs_11_.refs_4_), channel_id=1, source_target_pairs={{0,8},{8,0},{1,9},{9,1},{2,10},{10,2},{3,11},{11,3},{4,12},{12,4},... | collective-permute-start | bytes 3981320 | tf_op jit(solution)/shard_map/ppermute | solution.py:641
  120.4 27.1 %collective-permute-start.9 = (bf16[2,3,96,1152]{3,2,1,0:T(8,128)(2,1)}, bf16[2,3,96,1152]{3,2,1,0:T(8,128)(2,1)S(1)}, u32[]{:S(2)}, u32[]{:S(2)}) collective-permute-start(bf16[2,3,96,1152]{3,2,1,0:T(8,128)(2,1)} %pad_maximum_fusion.2.refs_10_.refs_3_), channel_id=1, source_target_pairs={{0,16},{16,0},{1,17},{17,1},{2,18},{18,2},{3,19},{19,3},{4,20},{20... | collective-permute-start | bytes 3981320 | tf_op jit(solution)/shard_map/ppermute | solution.py:641
  154.2 20.2 %collective-permute-start.11 = (bf16[512,1152]{1,0:T(8,128)(2,1)}, bf16[512,1152]{1,0:T(8,128)(2,1)}, u32[]{:S(2)}, u32[]{:S(2)}) collective-permute-start(bf16[512,1152]{1,0:T(8,128)(2,1)} %get-tuple-element.138.refs_7_.refs_0_.refs_1_), channel_id=1, source_target_pairs={{0,4},{4,0},{1,5},{5,1},{2,6},{6,2},{3,7},{7,3},{8,12},{12,8},{9,1... | collective-permute-start | bytes 3538952 | tf_op jit(solution)/shard_map/ppermute | solution.py:616
  154.6 16.2 %collective-permute-start.13 = (bf16[3,48,1152]{2,1,0:T(8,128)(2,1)S(1)}, bf16[3,48,1152]{2,1,0:T(8,128)(2,1)S(1)}, u32[]{:S(2)}, u32[]{:S(2)}) collective-permute-start(bf16[3,48,1152]{2,1,0:T(8,128)(2,1)S(1)} %copy-done.22), channel_id=1, source_target_pairs={{0,16},{16,0},{1,17},{17,1},{2,18},{18,2},{3,19},{19,3},{4,20},{20... | collective-permute-start | bytes 995336 | tf_op jit(solution)/shard_map/ppermute | solution.py:636
  155.1 15.7 %collective-permute-start.12 = (bf16[3,48,1152]{2,1,0:T(8,128)(2,1)S(1)}, bf16[3,48,1152]{2,1,0:T(8,128)(2,1)S(1)}, u32[]{:S(2)}, u32[]{:S(2)}) collective-permute-start(bf16[3,48,1152]{2,1,0:T(8,128)(2,1)S(1)} %copy-done.23), channel_id=1, source_target_pairs={{0,8},{8,0},{1,9},{9,1},{2,10},{10,2},{3,11},{11,3},{4,12},{12,4},... | collective-permute-start | bytes 995336 | tf_op jit(solution)/shard_map/ppermute | solution.py:635
  157.4 16.9 %all-to-all-start.3 = ((f32[32,2,1153]{2,1,0:T(2,128)}), f32[32,2,1153]{2,1,0:T(2,128)S(1)}, u32[]{:S(2)}, u32[]{:S(2)}) async-start(f32[32,2,1153]{2,1,0:T(2,128)} %broadcast_in_dim.27), calls=%async_computation.3 | async-start | bytes 655360 | tf_op jit(solution)/shard_map/all_to_all | solution.py:742
  162.8 27.1 %collective-permute-start.16 = (bf16[512,1152]{1,0:T(8,128)(2,1)}, bf16[512,1152]{1,0:T(8,128)(2,1)}, u32[]{:S(2)}, u32[]{:S(2)}) collective-permute-start(bf16[512,1152]{1,0:T(8,128)(2,1)} %get-tuple-element.145.refs_1_.refs_0_), channel_id=1, source_target_pairs={{0,4},{4,0},{1,5},{5,1},{2,6},{6,2},{3,7},{7,3},{8,12},{12,8},{9,1... | collective-permute-start | bytes 3538952 | tf_op jit(solution)/shard_map/ppermute | solution.py:616
  170.9 17.9 %collective-permute-start.15 = (bf16[2,3,48,1152]{3,2,1,0:T(8,128)(2,1)S(1)}, bf16[2,3,48,1152]{3,2,1,0:T(8,128)(2,1)S(1)}, u32[]{:S(2)}, u32[]{:S(2)}) collective-permute-start(bf16[2,3,48,1152]{3,2,1,0:T(8,128)(2,1)S(1)} %pad_maximum_fusion.11.refs_4_), channel_id=1, source_target_pairs={{0,8},{8,0},{1,9},{9,1},{2,10},{10,2},{3,11},{11,3},{4,12},{12,4},... | collective-permute-start | bytes 1990664 | tf_op jit(solution)/shard_map/ppermute | solution.py:641
  172.8 17.1 %collective-permute-start.14 = (bf16[2,3,48,1152]{3,2,1,0:T(8,128)(2,1)S(1)}, bf16[2,3,48,1152]{3,2,1,0:T(8,128)(2,1)}, u32[]{:S(2)}, u32[]{:S(2)}) collective-permute-start(bf16[2,3,48,1152]{3,2,1,0:T(8,128)(2,1)S(1)} %pad_maximum_fusion.10.refs_3_), channel_id=1, source_target_pairs={{0,16},{16,0},{1,17},{17,1},{2,18},{18,2},{3,19},{19,3},{4,20},{20... | collective-permute-start | bytes 1990664 | tf_op jit(solution)/shard_map/ppermute | solution.py:641
  200.1 41.7 %collective-permute-start.17 = (bf16[2,4,2,144,384]{4,3,2,1,0:T(8,128)(2,1)}, bf16[2,4,2,144,384]{4,3,2,1,0:T(8,128)(2,1)S(1)}, u32[]{:S(2)}, u32[]{:S(2)}) collective-permute-start(bf16[2,4,2,144,384]{4,3,2,1,0:T(8,128)(2,1)} %get-tuple-element.146.refs_7_.refs_4_), channel_id=1, source_target_pairs={{0,8},{8,0},{1,9},{9,1},{2,10},{10,2},{3,11},{11,3},{4,12},{12,4},... | collective-permute-start | bytes 5308424 | tf_op jit(solution)/shard_map/ppermute | solution.py:672
  233.4 26.5 %collective-permute-start.19 = (bf16[2,2,2,144,384]{4,3,2,1,0:T(8,128)(2,1)}, bf16[2,2,2,144,384]{4,3,2,1,0:T(8,128)(2,1)S(1)}, u32[]{:S(2)}, u32[]{:S(2)}) collective-permute-start(bf16[2,2,2,144,384]{4,3,2,1,0:T(8,128)(2,1)} %get-tuple-element.148.refs_2_), channel_id=1, source_target_pairs={{0,8},{8,0},{1,9},{9,1},{2,10},{10,2},{3,11},{11,3},{4,12},{12,4},... | collective-permute-start | bytes 2654216 | tf_op jit(solution)/shard_map/ppermute | solution.py:672
  234.3 25.6 %collective-permute-start.20 = (bf16[2,2,2,144,384]{4,3,2,1,0:T(8,128)(2,1)}, bf16[2,2,2,144,384]{4,3,2,1,0:T(8,128)(2,1)}, u32[]{:S(2)}, u32[]{:S(2)}) collective-permute-start(bf16[2,2,2,144,384]{4,3,2,1,0:T(8,128)(2,1)} %get-tuple-element.149.refs_3_), channel_id=1, source_target_pairs={{0,16},{16,0},{1,17},{17,1},{2,18},{18,2},{3,19},{19,3},{4,20},{20... | collective-permute-start | bytes 2654216 | tf_op jit(solution)/shard_map/ppermute | solution.py:672
  256.9 33.4 %collective-permute-start.22 = (bf16[2,2,2,144,384]{4,3,2,1,0:T(8,128)(2,1)}, bf16[2,2,2,144,384]{4,3,2,1,0:T(8,128)(2,1)}, u32[]{:S(2)}, u32[]{:S(2)}) collective-permute-start(bf16[2,2,2,144,384]{4,3,2,1,0:T(8,128)(2,1)} %get-tuple-element.150.refs_4_), channel_id=1, source_target_pairs={{0,8},{8,0},{1,9},{9,1},{2,10},{10,2},{3,11},{11,3},{4,12},{12,4},... | collective-permute-start | bytes 2654216 | tf_op jit(solution)/shard_map/ppermute | solution.py:672
  258.0 32.2 %collective-permute-start.23 = (bf16[2,2,2,144,384]{4,3,2,1,0:T(8,128)(2,1)}, bf16[2,2,2,144,384]{4,3,2,1,0:T(8,128)(2,1)}, u32[]{:S(2)}, u32[]{:S(2)}) collective-permute-start(bf16[2,2,2,144,384]{4,3,2,1,0:T(8,128)(2,1)} %get-tuple-element.151.refs_5_), channel_id=1, source_target_pairs={{0,16},{16,0},{1,17},{17,1},{2,18},{18,2},{3,19},{19,3},{4,20},{20... | collective-permute-start | bytes 2654216 | tf_op jit(solution)/shard_map/ppermute | solution.py:672
  261.9 26.8 %collective-permute-start.25 = (bf16[2,2,144,384]{3,2,1,0:T(8,128)(2,1)S(1)}, bf16[2,2,144,384]{3,2,1,0:T(8,128)(2,1)}, u32[]{:S(2)}, u32[]{:S(2)}) collective-permute-start(bf16[2,2,144,384]{3,2,1,0:T(8,128)(2,1)S(1)} %fusion.14.refs_10_), channel_id=1, source_target_pairs={{0,8},{8,0},{1,9},{9,1},{2,10},{10,2},{3,11},{11,3},{4,12},{12,4},... | collective-permute-start | bytes 1327112 | tf_op jit(solution)/shard_map/ppermute | solution.py:681
  264.2 26.0 %collective-permute-start.24 = (bf16[2,2,144,384]{3,2,1,0:T(8,128)(2,1)S(1)}, bf16[2,2,144,384]{3,2,1,0:T(8,128)(2,1)}, u32[]{:S(2)}, u32[]{:S(2)}) collective-permute-start(bf16[2,2,144,384]{3,2,1,0:T(8,128)(2,1)S(1)} %fusion.13.refs_9_), channel_id=1, source_target_pairs={{0,16},{16,0},{1,17},{17,1},{2,18},{18,2},{3,19},{19,3},{4,20},{20... | collective-permute-start | bytes 1327112 | tf_op jit(solution)/shard_map/ppermute | solution.py:681
  273.4 26.5 %collective-permute-start.21 = (bf16[512,1152]{1,0:T(8,128)(2,1)}, bf16[512,1152]{1,0:T(8,128)(2,1)}, u32[]{:S(2)}, u32[]{:S(2)}) collective-permute-start(bf16[512,1152]{1,0:T(8,128)(2,1)} %get-tuple-element.164.refs_1_.refs_3_), channel_id=1, source_target_pairs={{0,4},{4,0},{1,5},{5,1},{2,6},{6,2},{3,7},{7,3},{8,12},{12,8},{9,1... | collective-permute-start | bytes 3538952 | tf_op jit(solution)/shard_map/ppermute | solution.py:616
  288.7 41.9 %collective-permute-start.29 = (bf16[4,2,144,384]{3,2,1,0:T(8,128)(2,1)}, bf16[4,2,144,384]{3,2,1,0:T(8,128)(2,1)S(1)}, u32[]{:S(2)}, u32[]{:S(2)}) collective-permute-start(bf16[4,2,144,384]{3,2,1,0:T(8,128)(2,1)} %fusion.4.refs_6_.refs_10_), channel_id=1, source_target_pairs={{0,16},{16,0},{1,17},{17,1},{2,18},{18,2},{3,19},{19,3},{4,20},{20... | collective-permute-start | bytes 2654216 | tf_op jit(solution)/shard_map/ppermute | solution.py:681
  292.3 38.4 %collective-permute-start.28 = (bf16[2,2,144,384]{3,2,1,0:T(8,128)(2,1)}, bf16[2,2,144,384]{3,2,1,0:T(8,128)(2,1)}, u32[]{:S(2)}, u32[]{:S(2)}) collective-permute-start(bf16[2,2,144,384]{3,2,1,0:T(8,128)(2,1)} %fusion.16.refs_12_), channel_id=1, source_target_pairs={{0,8},{8,0},{1,9},{9,1},{2,10},{10,2},{3,11},{11,3},{4,12},{12,4},... | collective-permute-start | bytes 1327112 | tf_op jit(solution)/shard_map/ppermute | solution.py:681
  295.3 35.4 %collective-permute-start.27 = (bf16[2,2,144,384]{3,2,1,0:T(8,128)(2,1)}, bf16[2,2,144,384]{3,2,1,0:T(8,128)(2,1)}, u32[]{:S(2)}, u32[]{:S(2)}) collective-permute-start(bf16[2,2,144,384]{3,2,1,0:T(8,128)(2,1)} %fusion.15.refs_11_), channel_id=1, source_target_pairs={{0,16},{16,0},{1,17},{17,1},{2,18},{18,2},{3,19},{19,3},{4,20},{20... | collective-permute-start | bytes 1327112 | tf_op jit(solution)/shard_map/ppermute | solution.py:681
  330.7 35.1 %collective-permute-start.26 = (bf16[512,1152]{1,0:T(8,128)(2,1)}, bf16[512,1152]{1,0:T(8,128)(2,1)}, u32[]{:S(2)}, u32[]{:S(2)}) collective-permute-start(bf16[512,1152]{1,0:T(8,128)(2,1)} %get-tuple-element.177), channel_id=1, source_target_pairs={{0,4},{4,0},{1,5},{5,1},{2,6},{6,2},{3,7},{7,3},{8,12},{12,8},{9,1... | collective-permute-start | bytes 3538952 | tf_op jit(solution)/shard_map/ppermute | solution.py:616
  352.1 35.1 %collective-permute-start.31 = (bf16[2,4,2,144,256]{4,3,2,1,0:T(8,128)(2,1)}, bf16[2,4,2,144,256]{4,3,2,1,0:T(8,128)(2,1)}, u32[]{:S(2)}, u32[]{:S(2)}) collective-permute-start(bf16[2,4,2,144,256]{4,3,2,1,0:T(8,128)(2,1)} %get-tuple-element.183.refs_7_), channel_id=1, source_target_pairs={{0,8},{8,0},{1,9},{9,1},{2,10},{10,2},{3,11},{11,3},{4,12},{12,4},... | collective-permute-start | bytes 3538952 | tf_op jit(solution)/shard_map/ppermute | solution.py:672
  353.3 33.9 %collective-permute-start.32 = (bf16[2,4,2,144,256]{4,3,2,1,0:T(8,128)(2,1)}, bf16[2,4,2,144,256]{4,3,2,1,0:T(8,128)(2,1)}, u32[]{:S(2)}, u32[]{:S(2)}) collective-permute-start(bf16[2,4,2,144,256]{4,3,2,1,0:T(8,128)(2,1)} %get-tuple-element.184.refs_8_), channel_id=1, source_target_pairs={{0,16},{16,0},{1,17},{17,1},{2,18},{18,2},{3,19},{19,3},{4,20},{20... | collective-permute-start | bytes 3538952 | tf_op jit(solution)/shard_map/ppermute | solution.py:672
  359.3 79.8 %all-to-all-start.4 = ((bf16[4,2,144,1152]{3,2,1,0:T(8,128)(2,1)}), bf16[4,2,144,1152]{3,2,1,0:T(8,128)(2,1)S(1)}, u32[]{:S(2)}, u32[]{:S(2)}) async-start(bf16[4,2,144,1152]{3,2,1,0:T(8,128)(2,1)} %pad_maximum_fusion.refs_7_), calls=%async_computation.4 | async-start | bytes 5308416 | tf_op jit(solution)/shard_map/all_to_all | solution.py:704
  364.1 22.3 %collective-permute-start.33 = (bf16[2,2,2,144,64]{4,3,2,1,0:T(8,128)(2,1)S(1)}, bf16[2,2,2,144,64]{4,3,2,1,0:T(8,128)(2,1)S(1)}, u32[]{:S(2)}, u32[]{:S(2)}) collective-permute-start(bf16[2,2,2,144,64]{4,3,2,1,0:T(8,128)(2,1)S(1)} %copy-done.49), channel_id=1, source_target_pairs={{0,8},{8,0},{1,9},{9,1},{2,10},{10,2},{3,11},{11,3},{4,12},{12,4},... | collective-permute-start | bytes 442376 | tf_op jit(solution)/shard_map/ppermute | solution.py:672
  365.1 22.1 %collective-permute-start.34 = (bf16[2,2,2,144,64]{4,3,2,1,0:T(8,128)(2,1)S(1)}, bf16[2,2,2,144,64]{4,3,2,1,0:T(8,128)(2,1)S(1)}, u32[]{:S(2)}, u32[]{:S(2)}) collective-permute-start(bf16[2,2,2,144,64]{4,3,2,1,0:T(8,128)(2,1)S(1)} %copy-done.48), channel_id=1, source_target_pairs={{0,16},{16,0},{1,17},{17,1},{2,18},{18,2},{3,19},{19,3},{4,20},{20... | collective-permute-start | bytes 442376 | tf_op jit(solution)/shard_map/ppermute | solution.py:672
  387.2 14.6 %collective-permute-start.30 = (bf16[512,1152]{1,0:T(8,128)(2,1)}, bf16[512,1152]{1,0:T(8,128)(2,1)}, u32[]{:S(2)}, u32[]{:S(2)}) collective-permute-start(bf16[512,1152]{1,0:T(8,128)(2,1)} %get-tuple-element.189), channel_id=1, source_target_pairs={{0,4},{4,0},{1,5},{5,1},{2,6},{6,2},{3,7},{7,3},{8,12},{12,8},{9,1... | collective-permute-start | bytes 3538952 | tf_op jit(solution)/shard_map/ppermute | solution.py:616
  388.6 21.9 %collective-permute-start.36 = (bf16[4,2,144,256]{3,2,1,0:T(8,128)(2,1)S(1)}, bf16[4,2,144,256]{3,2,1,0:T(8,128)(2,1)}, u32[]{:S(2)}, u32[]{:S(2)}) collective-permute-start(bf16[4,2,144,256]{3,2,1,0:T(8,128)(2,1)S(1)} %fusion.12.refs_8_), channel_id=1, source_target_pairs={{0,8},{8,0},{1,9},{9,1},{2,10},{10,2},{3,11},{11,3},{4,12},{12,4},... | collective-permute-start | bytes 1769480 | tf_op jit(solution)/shard_map/ppermute | solution.py:681
  391.6 18.9 %collective-permute-start.35 = (bf16[4,2,144,256]{3,2,1,0:T(8,128)(2,1)}, bf16[4,2,144,256]{3,2,1,0:T(8,128)(2,1)}, u32[]{:S(2)}, u32[]{:S(2)}) collective-permute-start(bf16[4,2,144,256]{3,2,1,0:T(8,128)(2,1)} %fusion.11.refs_7_), channel_id=1, source_target_pairs={{0,16},{16,0},{1,17},{17,1},{2,18},{18,2},{3,19},{19,3},{4,20},{20... | collective-permute-start | bytes 1769480 | tf_op jit(solution)/shard_map/ppermute | solution.py:681
  396.2 11.4 %collective-permute-start.38 = (bf16[2,2,144,64]{3,2,1,0:T(8,128)(2,1)S(1)}, bf16[2,2,144,64]{3,2,1,0:T(8,128)(2,1)}, u32[]{:S(2)}, u32[]{:S(2)}) collective-permute-start(bf16[2,2,144,64]{3,2,1,0:T(8,128)(2,1)S(1)} %fusion.24.refs_10_), channel_id=1, source_target_pairs={{0,8},{8,0},{1,9},{9,1},{2,10},{10,2},{3,11},{11,3},{4,12},{12,4},... | collective-permute-start | bytes 221192 | tf_op jit(solution)/shard_map/ppermute | solution.py:681
  398.2 12.3 %collective-permute-start.37 = (bf16[2,2,144,64]{3,2,1,0:T(8,128)(2,1)S(1)}, bf16[2,2,144,64]{3,2,1,0:T(8,128)(2,1)}, u32[]{:S(2)}, u32[]{:S(2)}) collective-permute-start(bf16[2,2,144,64]{3,2,1,0:T(8,128)(2,1)S(1)} %fusion.23.refs_9_), channel_id=1, source_target_pairs={{0,16},{16,0},{1,17},{17,1},{2,18},{18,2},{3,19},{19,3},{4,20},{20... | collective-permute-start | bytes 221192 | tf_op jit(solution)/shard_map/ppermute | solution.py:681
  421.5 56.2 %collective-permute-start.41 = (bf16[2,144,576]{2,1,0:T(8,128)(2,1)}, bf16[2,144,576]{2,1,0:T(8,128)(2,1)}, u32[]{:S(2)}, u32[]{:S(2)}) collective-permute-start(bf16[2,144,576]{2,1,0:T(8,128)(2,1)} %get-tuple-element.256), channel_id=1, source_target_pairs={{0,1},{1,2},{2,3},{3,0},{4,5},{5,6},{6,7},{7,4},{8,9},{9,10},{10,1... | collective-permute-start | bytes 995336 | tf_op jit(solution)/shard_map/ppermute | solution.py:710
  423.1 54.7 %collective-permute-start.40 = (bf16[2,144,576]{2,1,0:T(8,128)(2,1)}, bf16[2,144,576]{2,1,0:T(8,128)(2,1)}, u32[]{:S(2)}, u32[]{:S(2)}) collective-permute-start(bf16[2,144,576]{2,1,0:T(8,128)(2,1)} %get-tuple-element.257), channel_id=1, source_target_pairs={{0,2},{1,3},{2,0},{3,1},{4,6},{5,7},{6,4},{7,5},{8,10},{9,11},{10,... | collective-permute-start | bytes 995336 | tf_op jit(solution)/shard_map/ppermute | solution.py:710
  425.5 52.3 %collective-permute-start.39 = (bf16[2,144,576]{2,1,0:T(8,128)(2,1)}, bf16[2,144,576]{2,1,0:T(8,128)(2,1)}, u32[]{:S(2)}, u32[]{:S(2)}) collective-permute-start(bf16[2,144,576]{2,1,0:T(8,128)(2,1)} %get-tuple-element.258), channel_id=1, source_target_pairs={{0,3},{1,0},{2,1},{3,2},{4,7},{5,4},{6,5},{7,6},{8,11},{9,8},{10,9... | collective-permute-start | bytes 995336 | tf_op jit(solution)/shard_map/ppermute | solution.py:710
  441.3 18.1 %all-to-all-start.5 = ((f32[32,1,508]{2,1,0:T(1,128)}), f32[32,1,508]{2,1,0:T(1,128)S(1)}, u32[]{:S(2)}, u32[]{:S(2)}) async-start(f32[32,1,508]{2,1,0:T(1,128)} %copy.47), calls=%async_computation.5 | async-start | bytes 131072 | tf_op jit(solution)/shard_map/all_to_all | solution.py:930
  445.0 22.9 %collective-permute-start.43 = (bf16[144,1152]{1,0:T(8,128)(2,1)S(1)}, bf16[144,1152]{1,0:T(8,128)(2,1)}, u32[]{:S(2)}, u32[]{:S(2)}) collective-permute-start(bf16[144,1152]{1,0:T(8,128)(2,1)S(1)} %fusion.19), channel_id=1, source_target_pairs={{0,4},{4,0},{1,5},{5,1},{2,6},{6,2},{3,7},{7,3},{8,12},{12,8},{9,1... | collective-permute-start | bytes 995336 | tf_op jit(solution)/shard_map/ppermute | solution.py:616
  462.7 13.9 %all-to-all-start.6 = ((f32[32,2,1152]{2,1,0:T(2,128)}), f32[32,2,1152]{2,1,0:T(2,128)}, u32[]{:S(2)}, u32[]{:S(2)}) async-start(f32[32,2,1152]{2,1,0:T(2,128)} %broadcast_in_dim.29), calls=%async_computation.6 | async-start | bytes 589824 | tf_op jit(solution)/shard_map/all_to_all | solution.py:742
  (76 other events, 623.0 us)

commit v3 on v2

--- a/solution.py
+++ b/solution.py
@@ -98,6 +98,16 @@
             if starts:
                 value = value + starts[j][at, :]
             ref[at, :] = value.astype(ref.dtype)
+
+
+def add_into(step, acc, rows, part):
+    @pl.when(step == 0)
+    def _():
+        acc[rows, :] = part
+
+    @pl.when(step > 0)
+    def _():
+        acc[rows, :] = acc[rows, :] + part
 
 
 def at_step(step, count, body):
@@ -484,6 +494,85 @@
     )[0]
 
 
+def place_heads(place, own, got, hw):
+    strip = own.shape[0]
+
+    def kernel(place, own, got, qkv_ref, out_ref):
+        first = place[1] == 0
+        low = jnp.where(first, own[...], got[...].astype(F32))
+        high = jnp.where(first, got[...].astype(F32), own[...])
+        for j in range(3):
+            at = slice(j * hw, (j + 1) * hw)
+            qkv_ref[j] = jnp.concatenate([low[:, at], high[:, at]], axis=1)
+        out_ref[...] = jnp.concatenate([low[:, 3 * hw :], high[:, 3 * hw :]], axis=1)
+
+    return call(
+        kernel,
+        "place_heads",
+        (1,),
+        [(own, None, None), (got, None, None)],
+        [(shape((3, strip, 2 * hw), F32), None, None), (shape((strip, 2 * hw), F32), None, None)],
+        scalars=(place,),
+    )
+
+
+def last_sums(arrived, early, bins, own_bins, cols, bias_cols):
+    sources, images, width = early.shape[0], early.shape[1], early.shape[2]
+    ends = [int(x) for x in np.cumsum([images * width] + [cols] * images + [bias_cols, 4])]
+    table_rows = own_bins.shape[0]
+
+    def kernel(got, early, bins, own_bins, ada_ref, b_ref, bias_ref, rms_ref, table_ref):
+        ada, table, flat = 0.0, 0.0, 0.0
+        for i in range(images):
+            d_mod = got[:, ends[i] : ends[i + 1]]
+            flat = flat + total(d_mod)
+            ada = ada + dot_tn(d_mod.astype(BF), early[:, i, :].astype(BF))
+            picks = jnp.where(own_bins[...] == bins[i : i + 1, :], 1.0, 0.0).astype(F32)
+            d_cond = got[:, i * width : (i + 1) * width]
+            table = table + jnp.dot(picks, d_cond, precision=EXACT, preferred_element_type=F32)
+        ada_ref[...] = ada
+        b_ref[...] = flat
+        bias_ref[...] = total(got[:, ends[images] : ends[images + 1]])
+        sums = total(got[:, ends[images + 1] :])
+        rms_ref[...] = jnp.sqrt(sums[:, :3] / (sums[:, 3:] * width))
+        table_ref[...] = table
+
+    return call(
+        kernel,
+        "last_sums",
+        (1,),
+        [(x, None, None) for x in (arrived, early, bins, own_bins)],
+        [
+            (shape((cols, width), F32), None, None),
+            (shape((1, cols), F32), None, None),
+            (shape((1, bias_cols), F32), None, None),
+            (shape((1, 3), F32), None, None),
+            (shape((table_rows, width), F32), None, None),
+        ],
+    )
+
+
+def ada_back(d_mod, w_ada, deps=()):
+    images, wide = d_mod.shape
+    width = w_ada.shape[0]
+    padded = jnp.zeros((16, wide), BF).at[:images].set(d_mod.astype(BF))
+
+    def kernel(d_ref, w_ref, out_ref):
+        part = dot_nt(d_ref[...], w_ref[...])
+        add_into(pl.program_id(0), out_ref, slice(None), part)
+
+    return call(
+        kernel,
+        "ada_back",
+        (wide // width,),
+        [(padded, (16, width), lambda k: (0, k)), (w_ada, (width, width), lambda k: (0, k))],
+        [(shape((16, width), F32), None, None)],
+        flops=20_000_000_000,
+        moved=2 * w_ada.size,
+        deps=deps,
+    )[0][:images]
+
+
 def norm(x):
     centered = x - jnp.mean(x, axis=-1, keepdims=True)
     inverse = lax.rsqrt(jnp.mean(centered * centered, axis=-1, keepdims=True) + EPSILON)
@@ -506,7 +595,7 @@
 SHIFT_ONE, SCALE_ONE, GATE_ONE, SHIFT_TWO, SCALE_TWO, GATE_TWO = range(6)
 
 
-def by_image(body, name, lengths, mod, rows_in, bias, outs, sums, deps=()):
+def by_image(body, name, lengths, mod, rows_in, bias, outs, sums, deps=(), moved=1):
     images, _, width = mod.shape
     seq = rows_in[0].shape[0] // images
     count = len(rows_in)
@@ -532,7 +621,7 @@
         + [(shape((images, sums, width), F32), (1, sums, width), lambda i: (i, 0, 0))],
         scalars=(lengths,),
         flops=1,
-        moved=1,
+        moved=moved,
         deps=deps,
     )
 
@@ -703,12 +792,16 @@
     def reduce_z(rows, *marks):
         return later(lax.all_to_all(rows, "z", 0, 0), marks)
 
-    def reduce_z_steps(rows, *marks):
-        got = [take(rows, at_z, 0)]
-        for r in range(1, tn):
-            sent = take(rows, (at_z + tn - r) % tn, 0)
-            got.append(lax.ppermute(sent, "z", ring(tn, -r)))
-        return jnp.stack(later(got, marks))
+    def z_sends(rows):
+        return [take(rows, (at_z + tn - r) % tn, 0) for r in range(tn)]
+
+    def reduce_z_steps(sends, *marks):
+        got = [lax.ppermute(sends[r], "z", ring(tn, -r)) for r in range(1, tn)]
+        return jnp.stack([sends[0]] + list(later(got, marks)))
+
+    def swap_core(arrived):
+        summed = jnp.sum(arrived.astype(F32), axis=0)
+        return summed[0], peer(summed[1].astype(BF))
 
     def reduce_core(arrived):
         summed = jnp.sum(arrived.astype(F32), axis=0)
@@ -781,18 +874,15 @@
         near_down = later(near_down, (att_own,))
         parts_down = plane_parts(near_down)
         att = (att_own, peer(att_peer))
-        early = later(early, (near_down,))
         residual, a2_own, sums_att = into_mlp(crossed_gu + parts_down)
         pairs_down = plane_first(parts_down, a2_own)
         gu_all = assemble(place, gu_own, [chunk(near_gu, pairs_gu, crossed_gu)], deps=(a2_own,))
-        early_all = spread(early)
-        wait_mlp = pairs_down + (early_all,)
+        wait_mlp = pairs_down
     else:
         q, k, v, attended, att_own, att_peer = attend(())
         att = (att_own, peer(att_peer))
         residual, a2_own, sums_att = into_mlp(())
         wait_mlp = ()
-        early_all = spread(early)
     a2_all = (a2_own, peer(a2_own))
     dm_all = (dm_own, peer(dm_own))
     gate_up, hidden = mlp_fwd(a2_all, gu_all, deps=wait_mlp)
@@ -817,6 +907,7 @@
             outs=(F32, BF),
             sums=4,
             deps=deps,
+            moved=30_000_000,
         )
 
     def back_heads(deps):
@@ -838,7 +929,7 @@
     if square:
         crossed_down = plane_second(pairs_down, hidden)
         mid = tn // 2
-        down_parts = ((0, units, "x", 0, tn),)
+        down_parts = ((0, units, "x", 0, mid), (0, units, "y", mid, tn))
         gu_parts = (
             (0, units, "x", 0, mid),
             (units, units, "y", 0, mid),
@@ -862,21 +953,23 @@
         down_sends = reduce_send(down_state, gu_sent)
         da2_own, da2_peer = back_out(d_gate_up, gu_all, "mlp_back", deps=gu_sent + down_sends)
         one_sends = reduce_send(one, da2_own)
+        early_all = spread(later(early, (da2_own,)))
         dh, da_own, sums_back = through_mlp(one_sends)
         da_all = (da_own, peer(da_own))
+        bins_all = early_all[:, :, width].T.astype(jnp.int32)
         two_sends = reduce_send(two, da_own)
-        one_rows = reduce_second(one, one_sends, gu_parts[:2], da_own)
-        d_qkv, da1_own, da1_peer = back_heads(down_sends + two_sends + one_rows)
-        down_rows = reduce_second(down_state, down_sends, down_parts, d_qkv)
-        two_rows = reduce_second(two, two_sends, gu_parts[2:], d_qkv)
+        d_qkv, da1_own, da1_peer = back_heads((early_all,) + two_sends)
+        heads_state, heads_sent = reduce_first(
+            [(a1_all, d_qkv), (da_all, attended)], heads_parts, two_sends
+        )
+        one_rows = reduce_second(one, one_sends, gu_parts[:2], d_qkv, heads_sent)
+        down_rows = reduce_second(down_state, down_sends, down_parts, heads_sent)
+        two_rows = reduce_second(two, two_sends, gu_parts[2:], heads_sent)
         gu_rows = jnp.concatenate(
             [jnp.concatenate(half, axis=3) for half in (one_rows, two_rows)], axis=0
         )
-        mlp_rows = jnp.concatenate([gu_rows, down_rows[0]], axis=3)
-        heads_state, heads_sent = reduce_first(
-            [(a1_all, d_qkv), (da_all, attended)], heads_parts, (mlp_rows,)
-        )
-        d_inputs, sums_one = through_attention(heads_sent)
+        mlp_rows = jnp.concatenate([gu_rows, jnp.concatenate(down_rows, axis=0)], axis=3)
+        d_inputs, sums_one = through_attention(heads_sent + (mlp_rows,))
         mlp_own, mlp_peer = back_out(hidden, down_all, "mlp_out", deps=(sums_one,))
         mlp_z = reduce_z(mlp_rows, mlp_own)
         heads_sends = reduce_send(heads_state, mlp_own)
@@ -885,9 +978,9 @@
         heads_rows = jnp.concatenate(
             heads_rows[:2] + (jnp.concatenate(heads_rows[2:], axis=0),), axis=3
         )
-        grad_mlp = reduce_core(mlp_z)
-        grad_gu, grad_down = grad_mlp[:, :, : 2 * units], grad_mlp[:, :, 2 * units :]
     else:
+        early_all = spread(early)
+        bins_all = early_all[:, :, width].T.astype(jnp.int32)
         d_gate_up = mlp_mid(dm_all, down_all, gate_up)
         da2_own, da2_peer = back_out(d_gate_up, gu_all, "mlp_back")
         dh, da_own, sums_back = through_mlp(())
@@ -896,14 +989,11 @@
         output, sums_mlp = finish_mlp(())
         d_qkv, da1_own, da1_peer = back_heads(())
         d_inputs, sums_one = through_attention(())
-        grad_down, grad_gu, grad_heads = (
+        grad_down, grad_gu = (
             reduce_core(reduce_z(reduce_plain(pairs)))
-            for pairs in (
-                [(dm_all, hidden)],
-                [(a2_all, d_gate_up)],
-                [(a1_all, d_qkv), (da_all, attended)],
-            )
-        )
+            for pairs in ([(dm_all, hidden)], [(a2_all, d_gate_up)])
+        )
+        swapped = swap_core(reduce_z(reduce_plain([(a1_all, d_qkv), (da_all, attended)])))
 
     d_mod = jnp.concatenate([sums_one, sums_back[:, :3], sums_mlp[:, :1]], axis=1)
     d_mod = d_mod.reshape(image_count, 6 * width)
@@ -926,52 +1016,47 @@
         axis=1,
     )
     if square:
-        ready, mlp_z = lax.optimization_barrier((ready, mlp_z))
-    arrived = lax.all_to_all(ready, axes, 0, 0, tiled=True)
+        heads_blocks = z_sends(heads_rows)
+        d_silu = ada_back(d_mod, w_ada, deps=(ready, mlp_z) + tuple(heads_blocks))
+    else:
+        d_silu = ada_back(d_mod, w_ada)
+    d_cond = d_silu * cond_sig * (1.0 + cond_vec * (1.0 - cond_sig))
+    message = jnp.concatenate(
+        [jnp.broadcast_to(d_cond.reshape(1, -1), (devices, image_count * width)), ready], axis=1
+    )
     if square:
-        d_mod, heads_rows = lax.optimization_barrier((d_mod, heads_rows))
-    d_silu = dot_nt(d_mod.astype(BF), w_ada)
-    d_cond = d_silu * cond_sig * (1.0 + cond_vec * (1.0 - cond_sig))
-    if square:
-        arrived, d_cond = lax.optimization_barrier((arrived, d_cond))
-    d_cond_all = spread(d_cond).reshape(devices * image_count, width)
-    if square:
-        grad_heads = reduce_core(reduce_z_steps(heads_rows, d_cond_all))
-    ends = np.cumsum([0, image_count * ada_cols, bias_cols, 4])
-    d_mod_all, bias_all, sums_all = (
-        arrived[:, start:stop] for start, stop in zip(ends[:-1], ends[1:])
-    )
-    d_mod_all = d_mod_all.reshape(devices * image_count, ada_cols)
-    grad_b_ada = jnp.sum(d_mod_all, axis=0)
-    grad_bias = jnp.sum(bias_all, axis=0)
-    sums_all = jnp.sum(sums_all, axis=0)
-    rms_values = jnp.sqrt(sums_all[:3] / (sums_all[3] * width))
-    early_all = early_all.reshape(devices * image_count, -1)
-    silu_all, bins_all = early_all[:, :width].astype(BF), early_all[:, width].astype(jnp.int32)
-    grad_ada = dot_tn(silu_all, d_mod_all.astype(BF))
+        heads_z = reduce_z_steps(heads_blocks, d_cond)
+        message, heads_z, mlp_z = lax.optimization_barrier((message, heads_z, mlp_z))
+        swapped = swap_core(heads_z)
+        grad_mlp = reduce_core(mlp_z)
+        grad_gu, grad_down = grad_mlp[:, :, : 2 * units], grad_mlp[:, :, 2 * units :]
+    arrived = lax.all_to_all(message, axes, 0, 0, tiled=True)
     table_rows = time_table.shape[0] // devices
     flat = (at_q * nc + at_c) * tn + at_z
     own_bins = flat * table_rows + jnp.arange(table_rows, dtype=jnp.int32)
-    picks = (own_bins[:, None] == bins_all[None, :]).astype(F32)
-    grad_table = jnp.dot(picks, d_cond_all, precision=EXACT)
+    grad_ada, grad_b_ada, grad_bias, rms_values, grad_table = last_sums(
+        arrived, early_all[:, :, :width], bins_all, own_bins[:, None], ada_cols, bias_cols
+    )
 
     def joined(value, parts):
         both = [value[j].reshape(strip, parts, -1) for j in range(nc)]
         return jnp.concatenate(both, axis=2)
+
+    grad_qkv, grad_out = place_heads(place, *swapped, hw)
 
     return (
         output,
         d_inputs,
         d_cond,
-        joined(grad_heads[:, :, : 3 * hw], 3),
-        joined(grad_heads[:, :, 3 * hw :], 1)[:, 0].T,
+        grad_qkv.transpose(1, 0, 2),
+        grad_out.T,
         joined(grad_gu, 2),
         joined(grad_down, 1)[:, 0].T,
-        grad_ada,
-        grad_b_ada,
-        grad_bias,
+        grad_ada.T,
+        grad_b_ada[0],
+        grad_bias[0],
         grad_table,
-        rms_values,
+        rms_values[0],
     )
 
 

time: 499 us -> 474 us (0.950)
  waiting for transfers between devices: 72.2 us -> 43.4 us
  Pallas kernels: 205 us -> 221 us
  matrix products: 23.4 us -> 11.5 us
  other arithmetic: 68.8 us -> 63.7 us
    ppermute x9 -> x10, waiting for transfers between devices: 18.2 us -> 0.03 us  [reduce_second(): lax.ppermute(x, other[part[2]], swap)]
    all_to_all x1, waiting for transfers between devices: 0.01 us -> 16.6 us  [reduce_z(): return later(lax.all_to_all(rows, 'z', 0, 0), marks)]
    pallas_call x18 -> x21, Pallas kernels: 205 us -> 221 us  [call(): pl.pallas_call(body, grid_spec=pltpu.PrefetchScalarGridSpec(num_scalar_pr...]
    dot_general x3 -> x0, matrix products: 11.9 us -> none  [the longest x1 9.72 us: dot_nt(): return lax.dot_general(a, b, NT, preferred_element_type=F32)]
    all_to_all x1, waiting for transfers between devices: 14.2 us -> 2.35 us  [local(): arrived = lax.all_to_all(message, axes, 0, 0, tiled=True)]
    ppermute x9 -> x10, waiting for transfers between devices: 11.8 us -> 0.15 us  [reduce_first(): lax.ppermute(x, part[2], swap)]
    unnamed x151 -> x178, local copies, waits for them, and re-layouts: 9.86 us -> 15.5 us
    convert_element_type x9 -> x10, other arithmetic: 12.6 us -> 14.9 us  [reduce_send(): (k[1].astype(F32) + g[1].astype(F32)).astype(BF)]
  transfers between devices with their start and end apart: 51 -> 52, of which waited for: 16 -> 13; matrix products, arithmetic and copies ran while one was open for 24% -> 23% of each run, Pallas kernels for 39% -> 43%
where the time goes in v3:
time: 474 us; the launch traced here: 466 us
  Pallas kernels  221 us (47%)
  starting transfers between devices  73.7 us (16%)
  other arithmetic  63.7 us (13%)
  local copies, waits for them, and re-layouts  50.5 us (11%)
  waiting for transfers between devices  43.4 us (9%)
  matrix products  11.5 us (2%)
    pallas_call x21, Pallas kernels, call(): pl.pallas_call(body, grid_spec=pltpu.PrefetchScalarGridSpec(num_scalar_pr...  221 us
    all_to_all x1, waiting for transfers between devices, reduce_z(): return later(lax.all_to_all(rows, 'z', 0, 0), marks)  16.6 us
    unnamed x178, local copies, waits for them, and re-layouts  15.5 us
    convert_element_type x10, other arithmetic, reduce_send(): (k[1].astype(F32) + g[1].astype(F32)).astype(BF)  14.9 us
    all_to_all x3, starting transfers between devices, along_z(): lax.all_to_all(jnp.broadcast_to(piece[None], (tn,) + piece.shape), 'z', 0...  14.5 us
    convert_element_type x10, other arithmetic, reduce_second(): (k[0].astype(F32) + g[0].astype(F32) + h.astype(F32)).astype(BF)  13.2 us
    another operation x12, other arithmetic, plane_first(): return (jnp.stack([first, first_x]), jnp.stack([second, second_y]))  11.8 us
    ppermute x10, starting transfers between devices, reduce_second(): lax.ppermute(x, other[part[2]], swap)  11.8 us
  transfers between devices with their start and end apart: 52, of which 13 were waited for; matrix products, arithmetic and copies ran while one was open for 23% of the time, Pallas kernels for 43%

profile of v3, /device:TPU:0, one launch (start us, length us, event | category | flops | bytes accessed | tf_op | source)
XLA Modules:
  0.0 466.5 jit_solution(1352320679049971137)
XLA Ops:
  6.4 6.0 %all-to-all-start = ((bf16[4,144,1152]{2,1,0:T(8,128)(2,1)}), bf16[4,144,1152]{2,1,0:T(8,128)(2,1)}, u32[]{:S(2)}, u32[]{:S(2)}) async-start(bf16[4,144,1152]{2,1,0:T(8,128)(2,1)} %broadcast_in_dim.25), calls=%async_computation | async-start | bytes 2654208 | tf_op jit(solution)/shard_map/all_to_all | solution.py:715
  13.6 3.1 fusion.28
  16.8 8.3 %convolution_add_fusion = f32[2,6912]{1,0:T(2,128)} fusion(bf16[1152,6912]{1,0:T(8,128)(2,1)} %refs_1_.1, f32[6912]{0:T(1024)S(1)} %copy-done.78, f32[2,1152]{1,0:T(2,128)S(1)} %get-tuple-element.305), kind=kOutput, calls=%fused_computation | convolution fusion | flops 31875840 | bytes 16017408 | tf_op jit(solution)/shard_map/dot_general | solution.py:26
  26.6 4.8 %pre_attention.1 = (bf16[512,1152]{1,0:T(8,128)(2,1)}, bf16[512,1152]{1,0:T(8,128)(2,1)}, f32[2,2,1152]{2,1,0:T(2,128)}) custom-call(s32[2]{0:T(128)} %refs_0_.9, f32[2,6,1152]{2,1,0:T(8,128)} %reshape.221.refs_1_, f32[1,1152]{1,0:T(1,128)} %broadcast_in_dim.23.refs_2_, f32[512,1152]{1,0:T(8,128)} %refs_3_.5, f32[512,1152]{1,0:T(8,128)} %refs_4_.5), custom_call_target="tpu_custom_call" | custom-call | flops 1 | bytes 1 | tf_op jit(solution)/shard_map/pre_attention/pallas_call | solution.py:52
  31.6 2.4 dynamic-slice_bitcast_fusion
  34.1 5.6 %copy.45 = bf16[2,384,1152]{2,1,0:T(8,128)(2,1)S(1)} copy(bf16[2,384,1152]{1,0,2:T(2,128)(2,1)} %dynamic-slice_bitcast_fusion) | data formatting | bytes 3538944 | tf_op jit(solution)/shard_map/dynamic_slice | solution.py:709
  39.7 1.9 dynamic-slice_bitcast_fusion.1
  46.2 3.8 all-to-all-start.1
  58.4 6.0 %collective-permute-done.3 = bf16[3,64,1152]{2,1,0:T(8,128)(2,1)S(1)} collective-permute-done((bf16[3,64,1152]{2,1,0:T(8,128)(2,1)}, bf16[3,64,1152]{2,1,0:T(8,128)(2,1)S(1)}, u32[]{:S(2)}, u32[]{:S(2)}) %collective-permute-start.3) | collective-permute-done | bytes 442400 | tf_op jit(solution)/shard_map/ppermute | solution.py:725
  68.0 3.4 collective-permute-done.2
  76.2 10.5 %attn_fwd.2 = (bf16[4,2,72,1024]{3,2,1,0:T(8,128)(2,1)}, bf16[4,2,72,1024]{3,2,1,0:T(8,128)(2,1)}, bf16[4,2,72,1024]{3,2,1,0:T(8,128)(2,1)}, bf16[4,144,1024]{2,...) custom-call(s32[4]{0:T(128)} %pad_add_fusion.1.refs_0_, s32[3]{0:T(128)} %pad_add_fusion.2.refs_1_.refs_0_, ...), custom_call_target="tpu_custom_call" | custom-call | flops 3112173568 | bytes 20000000 | tf_op jit(solution)/shard_map/attn_fwd/pallas_call | solution.py:52
  86.8 2.4 collective-permute-done.5.refs_6_
  89.1 7.5 %collective-permute-done.4.refs_5_ = bf16[2,3,80,1152]{3,2,1,0:T(8,128)(2,1)S(1)} collective-permute-done((bf16[2,3,80,1152]{3,2,1,0:T(8,128)(2,1)S(1)}, bf16[2,3,80,1152]{3,2,1,0:T(8,128)(2,1)S(1)}, u32[]{:S(2)}, u32[]{:S(2)}) %collective-permute-start.4) | collective-permute-done | bytes 1105952 | tf_op jit(solution)/shard_map/ppermute | solution.py:730
  103.2 4.7 %all-to-all-start.2 = ((bf16[4,96,1152]{2,1,0:T(8,128)(2,1)}), bf16[4,96,1152]{2,1,0:T(8,128)(2,1)S(1)}, u32[]{:S(2)}, u32[]{:S(2)}) async-start(bf16[4,96,1152]{2,1,0:T(8,128)(2,1)} %broadcast_in_dim.28), calls=%async_computation.2 | async-start | bytes 1769472 | tf_op jit(solution)/shard_map/all_to_all | solution.py:715
  107.9 6.5 %assemble.3.refs_7_.refs_9_ = bf16[4,4,144,1152]{3,2,1,0:T(8,128)(2,1)} custom-call(s32[3]{0:T(128)} %pad_add_fusion.2.refs_1_.refs_0_, bf16[4,144,1152]{2,1,0:T(8,128)(2,1)} %get-tuple-element.267.refs_1_, bf16[4,144,1152]{2,1,0:T(8,128)(2,1)} %all-to-all-done.refs_2_, bf16[2,3,80,1152]{3,2,1,0:T(8,128)(2,1)} %copy-done.10, ...), custom_call_target="tpu_custom_call" | custom-call | bytes 10616832 | tf_op jit(solution)/shard_map/assemble/pallas_call | solution.py:52
  114.5 2.4 pad_maximum_fusion.3.refs_11_.refs_4_
  118.1 2.3 pad_maximum_fusion.2.refs_10_.refs_3_
  121.4 23.4 %attn_fwd.3 = (bf16[4,2,72,1024]{3,2,1,0:T(8,128)(2,1)}, bf16[4,2,72,1024]{3,2,1,0:T(8,128)(2,1)}, bf16[4,2,72,1024]{3,2,1,0:T(8,128)(2,1)}, bf16[4,144,1024]{2,...) custom-call(s32[4]{0:T(128)} %pad_add_fusion.1.refs_0_, ...), custom_call_target="tpu_custom_call", output_to_operand_aliasing={{0}: (12, {}), {1}: (13, {}), {2}: (14, {}), {3}: (15, {})} | custom-call | flops 9336520704 | bytes 20000000 | tf_op jit(solution)/shard_map/attn_fwd/pallas_call | solution.py:52
  148.5 5.1 %pre_mlp.1 = (f32[512,1152]{1,0:T(8,128)}, bf16[512,1152]{1,0:T(8,128)(2,1)}, f32[2,1,1152]{2,1,0:T(1,128)}) custom-call(s32[2]{0:T(128)} %refs_0_.9, f32[2,6,1152]{2,1,0:T(8,128)} %reshape.221.refs_1_, f32[1,1152]{1,0:T(1,128)} %broadcast_in_dim.23.refs_2_, f32[512,1152]{1,0:T(8,128)} %refs_3_.5, f32[512,1152]{1,0:T(8,128)} %get-tuple-element.152.refs_4_.refs_5_, ...), custom_call_target="tpu_custom_call" | custom-call | flops 1 | bytes 1 | tf_op jit(solution)/shard_map/pre_mlp/pallas_call | solution.py:52
  155.6 7.6 %assemble.4.refs_2_.refs_1_ = bf16[4,4,192,1152]{3,2,1,0:T(8,128)(2,1)} custom-call(s32[3]{0:T(128)} %pad_add_fusion.2.refs_1_.refs_0_, bf16[4,192,1152]{2,1,0:T(8,128)(2,1)} %bitcast.169, bf16[4,192,1152]{2,1,0:T(8,128)(2,1)} %copy-done.2, bf16[2,3,96,1152]{3,2,1,0:T(8,128)(2,1)} %pad_maximum_fusion.2.refs_10_.refs_3_, ...), custom_call_target="tpu_custom_call" | custom-call | bytes 14155776 | tf_op jit(solution)/shard_map/assemble/pallas_call | solution.py:52
  166.9 13.8 %mlp_fwd.1 = (f32[4,1024,768]{2,1,0:T(8,128)}, bf16[4,1024,384]{2,1,0:T(8,128)(2,1)}) custom-call(bf16[512,1152]{1,0:T(8,128)(2,1)} %get-tuple-element.159.refs_7_.refs_0_.refs_1_, bf16[512,1152]{1,0:T(8,128)(2,1)} %collective-permute-done.11.refs_1_.refs_2_, bf16[4,4,192,1152]{3,2,1,0:T(8,128)(2,1)} %assemble.4.refs_2_.refs_1_, ...), custom_call_target="tpu_custom_call" | custom-call | flops 7247757312 | bytes 26000000 | tf_op jit(solution)/shard_map/mlp_fwd/pallas_call | solution.py:52
  183.7 10.7 %grad_split.3 = (bf16[2,2,2,144,384]{4,3,2,1,0:T(8,128)(2,1)}, bf16[2,2,2,144,384]{4,3,2,1,0:T(8,128)(2,1)}, bf16[2,2,2,144,384]{4,3,2,1,0:T(8,128)(2,1)}, bf16[2,2,2,144,384]{4,3,2,1,0:T(8,128)(2,1)}) custom-call(s32[3]{0:T(128)} %pad_add_fusion.2.refs_1_.refs_0_, bf16[512,1152]{1,0:T(8,128)(2,1)} %get-tuple-element.165.refs_1_.refs_0_, ...), custom_call_target="tpu_custom_call" | custom-call | flops 3623878656 | bytes 9043968 | tf_op jit(solution)/shard_map/grad_split/pallas_call | solution.py:52
  195.2 5.6 %assemble.5.refs_2_.refs_1_ = bf16[4,4,96,1152]{3,2,1,0:T(8,128)(2,1)} custom-call(s32[3]{0:T(128)} %pad_add_fusion.2.refs_1_.refs_0_, bf16[4,96,1152]{2,1,0:T(8,128)(2,1)} %bitcast.171, bf16[4,96,1152]{2,1,0:T(8,128)(2,1)} %copy-done.6, bf16[2,3,48,1152]{3,2,1,0:T(8,128)(2,1)} %copy-done.17, bf16[2,3,48,1152]{3,2,1,0:T(8,128)(2,1)} %copy-done.15, ...), custom_call_target="tpu_custom_call" | custom-call | bytes 7077888 | tf_op jit(solution)/shard_map/assemble/pallas_call | solution.py:52
  202.3 12.5 %mlp_mid.1.refs_3_.refs_0_ = bf16[4,1024,768]{2,1,0:T(8,128)(2,1)} custom-call(bf16[512,1152]{1,0:T(8,128)(2,1)} %get-tuple-element.165.refs_1_.refs_0_, bf16[512,1152]{1,0:T(8,128)(2,1)} %copy-done.32, bf16[4,4,96,1152]{3,2,1,0:T(8,128)(2,1)} %assemble.5.refs_2_.refs_1_, f32[4,1024,768]{2,1,0:T(8,128)} %get-tuple-element.168.refs_3_, ...), custom_call_target="tpu_custom_call" | custom-call | flops 3623878656 | bytes 26000000 | tf_op jit(solution)/shard_map/mlp_mid/pallas_call | solution.py:52
  214.9 14.5 %grad_split.4 = (bf16[2,2,2,144,384]{4,3,2,1,0:T(8,128)(2,1)}, bf16[2,2,2,144,384]{4,3,2,1,0:T(8,128)(2,1)}, bf16[2,2,2,144,384]{4,3,2,1,0:T(8,128)(2,1)}, bf16[...) custom-call(s32[3]{0:T(128)} %pad_add_fusion.2.refs_1_.refs_0_, ...), custom_call_target="tpu_custom_call" | custom-call | flops 7247757312 | bytes 15728640 | tf_op jit(solution)/shard_map/grad_split/pallas_call | solution.py:52
  233.1 13.9 %mlp_back.1 = (f32[512,1152]{1,0:T(8,128)}, bf16[512,1152]{1,0:T(8,128)(2,1)}) custom-call(bf16[4,1024,768]{2,1,0:T(8,128)(2,1)} %mlp_mid.1.refs_3_.refs_0_, bf16[4,4,192,1152]{3,2,1,0:T(8,128)(2,1)} %assemble.4.refs_2_.refs_1_, bf16[2,2,2,144,384]{4,3,2,1,0:T(8,128)(2,1)} %get-tuple-element.169.refs_2_, ...), custom_call_target="tpu_custom_call" | custom-call | flops 7247757312 | bytes 16908288 | tf_op jit(solution)/shard_map/mlp_back/pallas_call | solution.py:52
  249.6 2.0 fusion.14.refs_9_
  254.6 8.2 %back_mlp.1 = (f32[512,1152]{1,0:T(8,128)}, bf16[512,1152]{1,0:T(8,128)(2,1)}, f32[2,4,1152]{2,1,0:T(4,128)}) custom-call(s32[2]{0:T(128)} %refs_0_.9, f32[2,6,1152]{2,1,0:T(8,128)} %reshape.221.refs_1_, f32[1,1152]{1,0:T(1,128)} %broadcast_in_dim.23.refs_2_, f32[512,1152]{1,0:T(8,128)} %get-tuple-element.158.refs_3_, f32[512,1152]{1,0:T(8,128)} %refs_4_.5, ...), custom_call_target="tpu_custom_call" | custom-call | flops 1 | bytes 30000000 | tf_op jit(solution)/shard_map/back_mlp/pallas_call | solution.py:52
  264.5 5.8 %all-to-all-start.3 = ((f32[32,2,1153]{2,1,0:T(2,128)}), f32[32,2,1153]{2,1,0:T(2,128)S(1)}, u32[]{:S(2)}, u32[]{:S(2)}) async-start(f32[32,2,1153]{2,1,0:T(2,128)} %broadcast_in_dim.29), calls=%async_computation.3 | async-start | bytes 655360 | tf_op jit(solution)/shard_map/all_to_all | solution.py:835
  274.1 1.9 collective-permute-start.31
  278.2 2.0 fusion.16.refs_11_.refs_7_
  280.2 1.9 fusion.17.refs_12_.refs_8_
  284.7 30.8 %attn_bwd.1 = (bf16[4,432,1024]{2,1,0:T(8,128)(2,1)}, f32[512,1152]{1,0:T(8,128)}, bf16[512,1152]{1,0:T(8,128)(2,1)}) custom-call(s32[4]{0:T(128)} %pad_add_fusion.1.refs_0_, bf16[512,1152]{1,0:T(8,128)(2,1)} %get-tuple-element.188.refs_1_.refs_3_, bf16[512,1152]{1,0:T(8,128)(2,1)} %collective-permute-done.22.refs_2_.refs_4_, ...), custom_call_target="tpu_custom_call" | custom-call | flops 16173236224 | bytes 20000000 | tf_op jit(solution)/shard_map/attn_bwd/pallas_call | solution.py:52
  317.1 15.9 %grad_split.5 = (bf16[2,4,2,144,256]{4,3,2,1,0:T(8,128)(2,1)}, bf16[2,4,2,144,256]{4,3,2,1,0:T(8,128)(2,1)}, bf16[2,4,2,144,256]{4,3,2,1,0:T(8,128)(2,1)}, bf16[...) custom-call(s32[3]{0:T(128)} %pad_add_fusion.2.refs_1_.refs_0_, ...), custom_call_target="tpu_custom_call" | custom-call | flops 5435817984 | bytes 12386304 | tf_op jit(solution)/shard_map/grad_split/pallas_call | solution.py:52
  344.1 4.8 %all-to-all-start.4 = ((bf16[4,2,144,1152]{3,2,1,0:T(8,128)(2,1)}), bf16[4,2,144,1152]{3,2,1,0:T(8,128)(2,1)S(1)}, u32[]{:S(2)}, u32[]{:S(2)}) async-start(bf16[4,2,144,1152]{3,2,1,0:T(8,128)(2,1)} %maximum_maximum_fusion.refs_11_), calls=%async_computation.4 | async-start | bytes 5308416 | tf_op jit(solution)/shard_map/all_to_all | solution.py:793
  354.0 6.2 %back_attention.1 = (f32[512,1152]{1,0:T(8,128)}, f32[2,2,1152]{2,1,0:T(2,128)}) custom-call(s32[2]{0:T(128)} %refs_0_.9, f32[2,6,1152]{2,1,0:T(8,128)} %reshape.221.refs_1_, f32[1,1152]{1,0:T(1,128)} %broadcast_in_dim.23.refs_2_, f32[512,1152]{1,0:T(8,128)} %refs_3_.5, f32[512,1152]{1,0:T(8,128)} %get-tuple-element.187.refs_4_, ...), custom_call_target="tpu_custom_call" | custom-call | flops 1 | bytes 1 | tf_op jit(solution)/shard_map/back_attention/pallas_call | solution.py:52
  360.2 9.8 %mlp_out.1 = (f32[512,1152]{1,0:T(8,128)}, bf16[512,1152]{1,0:T(8,128)(2,1)}) custom-call(bf16[4,1024,384]{2,1,0:T(8,128)(2,1)} %get-tuple-element.162.refs_3_.refs_0_, bf16[4,4,96,1152]{3,2,1,0:T(8,128)(2,1)} %assemble.5.refs_2_.refs_1_, f32[2,2,1152]{2,1,0:T(2,128)} %get-tuple-element.213.refs_2_), custom_call_target="tpu_custom_call" | custom-call | flops 3623878656 | bytes 10223616 | tf_op jit(solution)/shard_map/mlp_out/pallas_call | solution.py:52
  376.3 2.0 fusion.10.refs_7_
  380.7 5.5 %post_mlp.1 = (f32[512,1152]{1,0:T(8,128)}, f32[2,2,1152]{2,1,0:T(2,128)}) custom-call(s32[2]{0:T(128)} %refs_0_.9, f32[2,6,1152]{2,1,0:T(8,128)} %reshape.221.refs_1_, f32[1,1152]{1,0:T(1,128)} %broadcast_in_dim.22.refs_2_, f32[512,1152]{1,0:T(8,128)} %get-tuple-element.158.refs_3_, f32[512,1152]{1,0:T(8,128)} %refs_4_.5, ...), custom_call_target="tpu_custom_call" | custom-call | flops 1 | bytes 1 | tf_op jit(solution)/shard_map/post_mlp/pallas_call | solution.py:52
  400.4 2.0 collective-permute-start.43
  402.4 2.4 collective-permute-start.42
  406.9 2.0 pad_maximum_fusion.20
  409.7 16.6 %all-to-all-done.4.refs_3_ = bf16[4,2,144,1152]{3,2,1,0:T(8,128)(2,1)S(1)} async-done(((bf16[4,2,144,1152]{3,2,1,0:T(8,128)(2,1)}), bf16[4,2,144,1152]{3,2,1,0:T(8,128)(2,1)S(1)}, u32[]{:S(2)}, u32[]{:S(2)}) %all-to-all-start.4) | async-done | bytes 2654240 | tf_op jit(solution)/shard_map/all_to_all | solution.py:793
  427.8 9.9 %ada_back.1 = f32[16,1152]{1,0:T(8,128)} custom-call(bf16[16,6912]{1,0:T(8,128)(2,1)} %scatter.4.refs_0_, bf16[1152,6912]{1,0:T(8,128)(2,1)} %refs_1_.1, f32[32,508]{1,0:T(8,128)} %pad_maximum_fusion.18.refs_2_, bf16[4,2,144,1152]{3,2,1,0:T(8,128)(2,1)} %copy-done.3, bf16[2,144,576]{2,1,0:T(8,128)(2,1)} %bitcast.172, bf16[2,144,576]{2,1,0:T(8,128)(2,1)} %copy-done.63, ...), custom_call_target="tpu_custom_call" | custom-call | flops 20000000000 | bytes 15925248 | tf_op jit(solution)/shard_map/ada_back/pallas_call | solution.py:52
  444.8 5.6 %all-to-all-start.5 = ((f32[32,1,2812]{2,1,0:T(1,128)}), f32[32,1,2812]{2,1,0:T(1,128)}, u32[]{:S(2)}, u32[]{:S(2)}) async-start(f32[32,1,2812]{2,1,0:T(1,128)} %all_to_all.27), calls=%async_computation.5 | async-start | bytes 720896 | tf_op jit(solution)/shard_map/all_to_all | solution.py:1033
  451.8 2.8 place_heads.1
  459.4 2.3 all-to-all-done.5
  463.5 2.7 last_sums.1
  (368 shorter events, 131.7 us)
Async XLA Ops:
  2.9 54.8 %collective-permute-start = (s32[1026]{0:T(1024)}, s32[1026]{0:T(1024)}, u32[]{:S(2)}, u32[]{:S(2)}) collective-permute-start(s32[1026]{0:T(1024)} %pad_add_fusion), channel_id=1, source_target_pairs={{0,4},{4,0},{1,5},{5,1},{2,6},{6,2},{3,7},{7,3},{8,12},{12,8},{9,1... | collective-permute-start | bytes 12320 | tf_op jit(solution)/shard_map/ppermute | solution.py:705
  6.4 38.5 %all-to-all-start = ((bf16[4,144,1152]{2,1,0:T(8,128)(2,1)}), bf16[4,144,1152]{2,1,0:T(8,128)(2,1)}, u32[]{:S(2)}, u32[]{:S(2)}) async-start(bf16[4,144,1152]{2,1,0:T(8,128)(2,1)} %broadcast_in_dim.25), calls=%async_computation | async-start | bytes 2654208 | tf_op jit(solution)/shard_map/all_to_all | solution.py:715
  31.4 44.9 %collective-permute-start.1 = (bf16[512,1152]{1,0:T(8,128)(2,1)}, bf16[512,1152]{1,0:T(8,128)(2,1)}, u32[]{:S(2)}, u32[]{:S(2)}) collective-permute-start(bf16[512,1152]{1,0:T(8,128)(2,1)} %get-tuple-element.138.refs_2_.refs_1_), channel_id=1, source_target_pairs={{0,4},{4,0},{1,5},{5,1},{2,6},{6,2},{3,7},{7,3},{8,12},{12,8},{9,1... | collective-permute-start | bytes 3538952 | tf_op jit(solution)/shard_map/ppermute | solution.py:705
  46.2 51.4 %all-to-all-start.1 = ((bf16[4,192,1152]{2,1,0:T(8,128)(2,1)}), bf16[4,192,1152]{2,1,0:T(8,128)(2,1)S(1)}, u32[]{:S(2)}, u32[]{:S(2)}) async-start(bf16[4,192,1152]{2,1,0:T(8,128)(2,1)} %broadcast_in_dim.27), calls=%async_computation.1 | async-start | bytes 3538944 | tf_op jit(solution)/shard_map/all_to_all | solution.py:715
  52.1 12.3 %collective-permute-start.3 = (bf16[3,64,1152]{2,1,0:T(8,128)(2,1)}, bf16[3,64,1152]{2,1,0:T(8,128)(2,1)S(1)}, u32[]{:S(2)}, u32[]{:S(2)}) collective-permute-start(bf16[3,64,1152]{2,1,0:T(8,128)(2,1)} %get-tuple-element.289), channel_id=1, source_target_pairs={{0,16},{16,0},{1,17},{17,1},{2,18},{18,2},{3,19},{19,3},{4,20},{20... | collective-permute-start | bytes 1327112 | tf_op jit(solution)/shard_map/ppermute | solution.py:725
  55.6 15.8 %collective-permute-start.2 = (bf16[3,80,1152]{2,1,0:T(8,128)(2,1)}, bf16[3,80,1152]{2,1,0:T(8,128)(2,1)}, u32[]{:S(2)}, u32[]{:S(2)}) collective-permute-start(bf16[3,80,1152]{2,1,0:T(8,128)(2,1)} %get-tuple-element.287), channel_id=1, source_target_pairs={{0,8},{8,0},{1,9},{9,1},{2,10},{10,2},{3,11},{11,3},{4,12},{12,4},... | collective-permute-start | bytes 1658888 | tf_op jit(solution)/shard_map/ppermute | solution.py:724
  66.4 22.7 %collective-permute-start.5 = (bf16[2,3,64,1152]{3,2,1,0:T(8,128)(2,1)S(1)}, bf16[2,3,64,1152]{3,2,1,0:T(8,128)(2,1)}, u32[]{:S(2)}, u32[]{:S(2)}) collective-permute-start(bf16[2,3,64,1152]{3,2,1,0:T(8,128)(2,1)S(1)} %pad_maximum_fusion.5.refs_4_), channel_id=1, source_target_pairs={{0,8},{8,0},{1,9},{9,1},{2,10},{10,2},{3,11},{11,3},{4,12},{12,4},... | collective-permute-start | bytes 2654216 | tf_op jit(solution)/shard_map/ppermute | solution.py:730
  72.6 24.0 %collective-permute-start.4 = (bf16[2,3,80,1152]{3,2,1,0:T(8,128)(2,1)S(1)}, bf16[2,3,80,1152]{3,2,1,0:T(8,128)(2,1)S(1)}, u32[]{:S(2)}, u32[]{:S(2)}) collective-permute-start(bf16[2,3,80,1152]{3,2,1,0:T(8,128)(2,1)S(1)} %pad_maximum_fusion.4.refs_3_), channel_id=1, source_target_pairs={{0,16},{16,0},{1,17},{17,1},{2,18},{18,2},{3,19},{19,3},{4,20},{20... | collective-permute-start | bytes 3317768 | tf_op jit(solution)/shard_map/ppermute | solution.py:730
  98.9 15.5 %collective-permute-start.7 = (bf16[3,96,1152]{2,1,0:T(8,128)(2,1)S(1)}, bf16[3,96,1152]{2,1,0:T(8,128)(2,1)}, u32[]{:S(2)}, u32[]{:S(2)}) collective-permute-start(bf16[3,96,1152]{2,1,0:T(8,128)(2,1)S(1)} %get-tuple-element.281.refs_8_), channel_id=1, source_target_pairs={{0,16},{16,0},{1,17},{17,1},{2,18},{18,2},{3,19},{19,3},{4,20},{20... | collective-permute-start | bytes 1990664 | tf_op jit(solution)/shard_map/ppermute | solution.py:725
  100.4 14.1 %collective-permute-start.6 = (bf16[3,96,1152]{2,1,0:T(8,128)(2,1)S(1)}, bf16[3,96,1152]{2,1,0:T(8,128)(2,1)}, u32[]{:S(2)}, u32[]{:S(2)}) collective-permute-start(bf16[3,96,1152]{2,1,0:T(8,128)(2,1)S(1)} %get-tuple-element.283.refs_7_), channel_id=1, source_target_pairs={{0,8},{8,0},{1,9},{9,1},{2,10},{10,2},{3,11},{11,3},{4,12},{12,4},... | collective-permute-start | bytes 1990664 | tf_op jit(solution)/shard_map/ppermute | solution.py:724
  103.2 41.7 %all-to-all-start.2 = ((bf16[4,96,1152]{2,1,0:T(8,128)(2,1)}), bf16[4,96,1152]{2,1,0:T(8,128)(2,1)S(1)}, u32[]{:S(2)}, u32[]{:S(2)}) async-start(bf16[4,96,1152]{2,1,0:T(8,128)(2,1)} %broadcast_in_dim.28), calls=%async_computation.2 | async-start | bytes 1769472 | tf_op jit(solution)/shard_map/all_to_all | solution.py:715
  116.9 29.8 %collective-permute-start.10 = (bf16[2,3,96,1152]{3,2,1,0:T(8,128)(2,1)}, bf16[2,3,96,1152]{3,2,1,0:T(8,128)(2,1)S(1)}, u32[]{:S(2)}, u32[]{:S(2)}) collective-permute-start(bf16[2,3,96,1152]{3,2,1,0:T(8,128)(2,1)} %pad_maximum_fusion.3.refs_11_.refs_4_), channel_id=1, source_target_pairs={{0,8},{8,0},{1,9},{9,1},{2,10},{10,2},{3,11},{11,3},{4,12},{12,4},... | collective-permute-start | bytes 3981320 | tf_op jit(solution)/shard_map/ppermute | solution.py:730
  120.4 27.0 %collective-permute-start.9 = (bf16[2,3,96,1152]{3,2,1,0:T(8,128)(2,1)}, bf16[2,3,96,1152]{3,2,1,0:T(8,128)(2,1)S(1)}, u32[]{:S(2)}, u32[]{:S(2)}) collective-permute-start(bf16[2,3,96,1152]{3,2,1,0:T(8,128)(2,1)} %pad_maximum_fusion.2.refs_10_.refs_3_), channel_id=1, source_target_pairs={{0,16},{16,0},{1,17},{17,1},{2,18},{18,2},{3,19},{19,3},{4,20},{20... | collective-permute-start | bytes 3981320 | tf_op jit(solution)/shard_map/ppermute | solution.py:730
  153.6 13.3 %collective-permute-start.11 = (bf16[512,1152]{1,0:T(8,128)(2,1)}, bf16[512,1152]{1,0:T(8,128)(2,1)}, u32[]{:S(2)}, u32[]{:S(2)}) collective-permute-start(bf16[512,1152]{1,0:T(8,128)(2,1)} %get-tuple-element.159.refs_7_.refs_0_.refs_1_), channel_id=1, source_target_pairs={{0,4},{4,0},{1,5},{5,1},{2,6},{6,2},{3,7},{7,3},{8,12},{12,8},{9,1... | collective-permute-start | bytes 3538952 | tf_op jit(solution)/shard_map/ppermute | solution.py:705
  153.7 10.1 %collective-permute-start.13 = (bf16[3,48,1152]{2,1,0:T(8,128)(2,1)S(1)}, bf16[3,48,1152]{2,1,0:T(8,128)(2,1)S(1)}, u32[]{:S(2)}, u32[]{:S(2)}) collective-permute-start(bf16[3,48,1152]{2,1,0:T(8,128)(2,1)S(1)} %copy-done.26), channel_id=1, source_target_pairs={{0,16},{16,0},{1,17},{17,1},{2,18},{18,2},{3,19},{19,3},{4,20},{20... | collective-permute-start | bytes 995336 | tf_op jit(solution)/shard_map/ppermute | solution.py:725
  155.6 26.2 %collective-permute-start.16 = (bf16[512,1152]{1,0:T(8,128)(2,1)S(1)}, bf16[512,1152]{1,0:T(8,128)(2,1)S(1)}, u32[]{:S(2)}, u32[]{:S(2)}) collective-permute-start(bf16[512,1152]{1,0:T(8,128)(2,1)S(1)} %copy-done.31), channel_id=1, source_target_pairs={{0,4},{4,0},{1,5},{5,1},{2,6},{6,2},{3,7},{7,3},{8,12},{12,8},{9,1... | collective-permute-start | bytes 3538952 | tf_op jit(solution)/shard_map/ppermute | solution.py:705
  164.4 16.3 %collective-permute-start.15 = (bf16[2,3,48,1152]{3,2,1,0:T(8,128)(2,1)S(1)}, bf16[2,3,48,1152]{3,2,1,0:T(8,128)(2,1)S(1)}, u32[]{:S(2)}, u32[]{:S(2)}) collective-permute-start(bf16[2,3,48,1152]{3,2,1,0:T(8,128)(2,1)S(1)} %pad_maximum_fusion.10.refs_4_), channel_id=1, source_target_pairs={{0,8},{8,0},{1,9},{9,1},{2,10},{10,2},{3,11},{11,3},{4,12},{12,4},... | collective-permute-start | bytes 1990664 | tf_op jit(solution)/shard_map/ppermute | solution.py:730
  165.4 16.4 %collective-permute-start.14 = (bf16[2,3,48,1152]{3,2,1,0:T(8,128)(2,1)S(1)}, bf16[2,3,48,1152]{3,2,1,0:T(8,128)(2,1)S(1)}, u32[]{:S(2)}, u32[]{:S(2)}) collective-permute-start(bf16[2,3,48,1152]{3,2,1,0:T(8,128)(2,1)S(1)} %pad_maximum_fusion.9.refs_3_), channel_id=1, source_target_pairs={{0,16},{16,0},{1,17},{17,1},{2,18},{18,2},{3,19},{19,3},{4,20},{20... | collective-permute-start | bytes 1990664 | tf_op jit(solution)/shard_map/ppermute | solution.py:730
  194.4 36.9 %collective-permute-start.17 = (bf16[2,2,2,144,384]{4,3,2,1,0:T(8,128)(2,1)}, bf16[2,2,2,144,384]{4,3,2,1,0:T(8,128)(2,1)S(1)}, u32[]{:S(2)}, u32[]{:S(2)}) collective-permute-start(bf16[2,2,2,144,384]{4,3,2,1,0:T(8,128)(2,1)} %get-tuple-element.166.refs_7_.refs_4_), channel_id=1, source_target_pairs={{0,8},{8,0},{1,9},{9,1},{2,10},{10,2},{3,11},{11,3},{4,12},{12,4},... | collective-permute-start | bytes 2654216 | tf_op jit(solution)/shard_map/ppermute | solution.py:761
  200.8 30.4 %collective-permute-start.18 = (bf16[2,2,2,144,384]{4,3,2,1,0:T(8,128)(2,1)S(1)}, bf16[2,2,2,144,384]{4,3,2,1,0:T(8,128)(2,1)S(1)}, u32[]{:S(2)}, u32[]{:S(2)}) collective-permute-start(bf16[2,2,2,144,384]{4,3,2,1,0:T(8,128)(2,1)S(1)} %copy-done.14), channel_id=1, source_target_pairs={{0,16},{16,0},{1,17},{17,1},{2,18},{18,2},{3,19},{19,3},{4,20},{20... | collective-permute-start | bytes 2654216 | tf_op jit(solution)/shard_map/ppermute | solution.py:761
  229.4 20.1 %collective-permute-start.20 = (bf16[2,2,2,144,384]{4,3,2,1,0:T(8,128)(2,1)}, bf16[2,2,2,144,384]{4,3,2,1,0:T(8,128)(2,1)}, u32[]{:S(2)}, u32[]{:S(2)}) collective-permute-start(bf16[2,2,2,144,384]{4,3,2,1,0:T(8,128)(2,1)} %get-tuple-element.169.refs_2_), channel_id=1, source_target_pairs={{0,8},{8,0},{1,9},{9,1},{2,10},{10,2},{3,11},{11,3},{4,12},{12,4},... | collective-permute-start | bytes 2654216 | tf_op jit(solution)/shard_map/ppermute | solution.py:761
  230.2 19.4 %collective-permute-start.21 = (bf16[2,2,2,144,384]{4,3,2,1,0:T(8,128)(2,1)}, bf16[2,2,2,144,384]{4,3,2,1,0:T(8,128)(2,1)}, u32[]{:S(2)}, u32[]{:S(2)}) collective-permute-start(bf16[2,2,2,144,384]{4,3,2,1,0:T(8,128)(2,1)} %get-tuple-element.170.refs_3_), channel_id=1, source_target_pairs={{0,16},{16,0},{1,17},{17,1},{2,18},{18,2},{3,19},{19,3},{4,20},{20... | collective-permute-start | bytes 2654216 | tf_op jit(solution)/shard_map/ppermute | solution.py:761
  247.1 30.3 %collective-permute-start.23 = (bf16[2,2,2,144,384]{4,3,2,1,0:T(8,128)(2,1)}, bf16[2,2,2,144,384]{4,3,2,1,0:T(8,128)(2,1)}, u32[]{:S(2)}, u32[]{:S(2)}) collective-permute-start(bf16[2,2,2,144,384]{4,3,2,1,0:T(8,128)(2,1)} %get-tuple-element.171.refs_4_), channel_id=1, source_target_pairs={{0,8},{8,0},{1,9},{9,1},{2,10},{10,2},{3,11},{11,3},{4,12},{12,4},... | collective-permute-start | bytes 2654216 | tf_op jit(solution)/shard_map/ppermute | solution.py:761
  248.0 30.0 %collective-permute-start.24 = (bf16[2,2,2,144,384]{4,3,2,1,0:T(8,128)(2,1)}, bf16[2,2,2,144,384]{4,3,2,1,0:T(8,128)(2,1)}, u32[]{:S(2)}, u32[]{:S(2)}) collective-permute-start(bf16[2,2,2,144,384]{4,3,2,1,0:T(8,128)(2,1)} %get-tuple-element.172.refs_5_), channel_id=1, source_target_pairs={{0,16},{16,0},{1,17},{17,1},{2,18},{18,2},{3,19},{19,3},{4,20},{20... | collective-permute-start | bytes 2654216 | tf_op jit(solution)/shard_map/ppermute | solution.py:761
  262.8 19.3 %collective-permute-start.22 = (bf16[512,1152]{1,0:T(8,128)(2,1)}, bf16[512,1152]{1,0:T(8,128)(2,1)}, u32[]{:S(2)}, u32[]{:S(2)}) collective-permute-start(bf16[512,1152]{1,0:T(8,128)(2,1)} %get-tuple-element.188.refs_1_.refs_3_), channel_id=1, source_target_pairs={{0,4},{4,0},{1,5},{5,1},{2,6},{6,2},{3,7},{7,3},{8,12},{12,8},{9,1... | collective-permute-start | bytes 3538952 | tf_op jit(solution)/shard_map/ppermute | solution.py:705
  264.5 19.5 %all-to-all-start.3 = ((f32[32,2,1153]{2,1,0:T(2,128)}), f32[32,2,1153]{2,1,0:T(2,128)S(1)}, u32[]{:S(2)}, u32[]{:S(2)}) async-start(f32[32,2,1153]{2,1,0:T(2,128)} %broadcast_in_dim.29), calls=%async_computation.3 | async-start | bytes 655360 | tf_op jit(solution)/shard_map/all_to_all | solution.py:835
  274.1 41.5 %collective-permute-start.31 = (bf16[2,2,144,384]{3,2,1,0:T(8,128)(2,1)S(1)}, bf16[2,2,144,384]{3,2,1,0:T(8,128)(2,1)S(1)}, u32[]{:S(2)}, u32[]{:S(2)}) collective-permute-start(bf16[2,2,144,384]{3,2,1,0:T(8,128)(2,1)S(1)} %copy-done.61), channel_id=1, source_target_pairs={{0,8},{8,0},{1,9},{9,1},{2,10},{10,2},{3,11},{11,3},{4,12},{12,4},... | collective-permute-start | bytes 1327112 | tf_op jit(solution)/shard_map/ppermute | solution.py:770
  276.0 57.1 %collective-permute-start.30 = (bf16[2,2,144,384]{3,2,1,0:T(8,128)(2,1)}, bf16[2,2,144,384]{3,2,1,0:T(8,128)(2,1)}, u32[]{:S(2)}, u32[]{:S(2)}) collective-permute-start(bf16[2,2,144,384]{3,2,1,0:T(8,128)(2,1)} %fusion.12.refs_6_), channel_id=1, source_target_pairs={{0,16},{16,0},{1,17},{17,1},{2,18},{18,2},{3,19},{19,3},{4,20},{20... | collective-permute-start | bytes 1327112 | tf_op jit(solution)/shard_map/ppermute | solution.py:770
  277.4 57.0 %collective-permute-start.27 = (bf16[2,2,144,384]{3,2,1,0:T(8,128)(2,1)S(1)}, bf16[2,2,144,384]{3,2,1,0:T(8,128)(2,1)}, u32[]{:S(2)}, u32[]{:S(2)}) collective-permute-start(bf16[2,2,144,384]{3,2,1,0:T(8,128)(2,1)S(1)} %copy-done.24), channel_id=1, source_target_pairs={{0,8},{8,0},{1,9},{9,1},{2,10},{10,2},{3,11},{11,3},{4,12},{12,4},... | collective-permute-start | bytes 1327112 | tf_op jit(solution)/shard_map/ppermute | solution.py:770
  278.0 56.5 %collective-permute-start.26 = (bf16[2,2,144,384]{3,2,1,0:T(8,128)(2,1)S(1)}, bf16[2,2,144,384]{3,2,1,0:T(8,128)(2,1)}, u32[]{:S(2)}, u32[]{:S(2)}) collective-permute-start(bf16[2,2,144,384]{3,2,1,0:T(8,128)(2,1)S(1)} %copy-done.23), channel_id=1, source_target_pairs={{0,16},{16,0},{1,17},{17,1},{2,18},{18,2},{3,19},{19,3},{4,20},{20... | collective-permute-start | bytes 1327112 | tf_op jit(solution)/shard_map/ppermute | solution.py:770
  282.1 51.6 %collective-permute-start.29 = (bf16[2,2,144,384]{3,2,1,0:T(8,128)(2,1)}, bf16[2,2,144,384]{3,2,1,0:T(8,128)(2,1)}, u32[]{:S(2)}, u32[]{:S(2)}) collective-permute-start(bf16[2,2,144,384]{3,2,1,0:T(8,128)(2,1)} %fusion.17.refs_12_.refs_8_), channel_id=1, source_target_pairs={{0,8},{8,0},{1,9},{9,1},{2,10},{10,2},{3,11},{11,3},{4,12},{12,4},... | collective-permute-start | bytes 1327112 | tf_op jit(solution)/shard_map/ppermute | solution.py:770
  315.6 18.9 %collective-permute-start.28 = (bf16[2,2,144,384]{3,2,1,0:T(8,128)(2,1)S(1)}, bf16[2,2,144,384]{3,2,1,0:T(8,128)(2,1)S(1)}, u32[]{:S(2)}, u32[]{:S(2)}) collective-permute-start(bf16[2,2,144,384]{3,2,1,0:T(8,128)(2,1)S(1)} %copy-done.62), channel_id=1, source_target_pairs={{0,16},{16,0},{1,17},{17,1},{2,18},{18,2},{3,19},{19,3},{4,20},{20... | collective-permute-start | bytes 1327112 | tf_op jit(solution)/shard_map/ppermute | solution.py:770
  333.0 37.0 %collective-permute-start.33 = (bf16[2,4,2,144,256]{4,3,2,1,0:T(8,128)(2,1)}, bf16[2,4,2,144,256]{4,3,2,1,0:T(8,128)(2,1)}, u32[]{:S(2)}, u32[]{:S(2)}) collective-permute-start(bf16[2,4,2,144,256]{4,3,2,1,0:T(8,128)(2,1)} %get-tuple-element.203.refs_7_), channel_id=1, source_target_pairs={{0,8},{8,0},{1,9},{9,1},{2,10},{10,2},{3,11},{11,3},{4,12},{12,4},... | collective-permute-start | bytes 3538952 | tf_op jit(solution)/shard_map/ppermute | solution.py:761
  333.7 36.4 %collective-permute-start.34 = (bf16[2,4,2,144,256]{4,3,2,1,0:T(8,128)(2,1)}, bf16[2,4,2,144,256]{4,3,2,1,0:T(8,128)(2,1)}, u32[]{:S(2)}, u32[]{:S(2)}) collective-permute-start(bf16[2,4,2,144,256]{4,3,2,1,0:T(8,128)(2,1)} %get-tuple-element.204.refs_8_), channel_id=1, source_target_pairs={{0,16},{16,0},{1,17},{17,1},{2,18},{18,2},{3,19},{19,3},{4,20},{20... | collective-permute-start | bytes 3538952 | tf_op jit(solution)/shard_map/ppermute | solution.py:761
  334.5 19.6 %collective-permute-start.25 = (bf16[512,1152]{1,0:T(8,128)(2,1)}, bf16[512,1152]{1,0:T(8,128)(2,1)}, u32[]{:S(2)}, u32[]{:S(2)}) collective-permute-start(bf16[512,1152]{1,0:T(8,128)(2,1)} %get-tuple-element.200), channel_id=1, source_target_pairs={{0,4},{4,0},{1,5},{5,1},{2,6},{6,2},{3,7},{7,3},{8,12},{12,8},{9,1... | collective-permute-start | bytes 3538952 | tf_op jit(solution)/shard_map/ppermute | solution.py:705
  344.1 82.1 %all-to-all-start.4 = ((bf16[4,2,144,1152]{3,2,1,0:T(8,128)(2,1)}), bf16[4,2,144,1152]{3,2,1,0:T(8,128)(2,1)S(1)}, u32[]{:S(2)}, u32[]{:S(2)}) async-start(bf16[4,2,144,1152]{3,2,1,0:T(8,128)(2,1)} %maximum_maximum_fusion.refs_11_), calls=%async_computation.4 | async-start | bytes 5308416 | tf_op jit(solution)/shard_map/all_to_all | solution.py:793
  351.2 18.8 %collective-permute-start.35 = (bf16[2,2,2,144,64]{4,3,2,1,0:T(8,128)(2,1)}, bf16[2,2,2,144,64]{4,3,2,1,0:T(8,128)(2,1)}, u32[]{:S(2)}, u32[]{:S(2)}) collective-permute-start(bf16[2,2,2,144,64]{4,3,2,1,0:T(8,128)(2,1)} %get-tuple-element.205.refs_9_), channel_id=1, source_target_pairs={{0,8},{8,0},{1,9},{9,1},{2,10},{10,2},{3,11},{11,3},{4,12},{12,4},... | collective-permute-start | bytes 442376 | tf_op jit(solution)/shard_map/ppermute | solution.py:761
  352.8 17.3 %collective-permute-start.36 = (bf16[2,2,2,144,64]{4,3,2,1,0:T(8,128)(2,1)S(1)}, bf16[2,2,2,144,64]{4,3,2,1,0:T(8,128)(2,1)}, u32[]{:S(2)}, u32[]{:S(2)}) collective-permute-start(bf16[2,2,2,144,64]{4,3,2,1,0:T(8,128)(2,1)S(1)} %copy-done.65), channel_id=1, source_target_pairs={{0,16},{16,0},{1,17},{17,1},{2,18},{18,2},{3,19},{19,3},{4,20},{20... | collective-permute-start | bytes 442376 | tf_op jit(solution)/shard_map/ppermute | solution.py:761
  370.0 9.7 %collective-permute-start.32 = (bf16[512,1152]{1,0:T(8,128)(2,1)}, bf16[512,1152]{1,0:T(8,128)(2,1)S(1)}, u32[]{:S(2)}, u32[]{:S(2)}) collective-permute-start(bf16[512,1152]{1,0:T(8,128)(2,1)} %get-tuple-element.215), channel_id=1, source_target_pairs={{0,4},{4,0},{1,5},{5,1},{2,6},{6,2},{3,7},{7,3},{8,12},{12,8},{9,1... | collective-permute-start | bytes 3538952 | tf_op jit(solution)/shard_map/ppermute | solution.py:705
  371.2 22.6 %collective-permute-start.40 = (bf16[2,2,144,64]{3,2,1,0:T(8,128)(2,1)S(1)}, bf16[2,2,144,64]{3,2,1,0:T(8,128)(2,1)}, u32[]{:S(2)}, u32[]{:S(2)}) collective-permute-start(bf16[2,2,144,64]{3,2,1,0:T(8,128)(2,1)S(1)} %fusion.23.refs_10_), channel_id=1, source_target_pairs={{0,8},{8,0},{1,9},{9,1},{2,10},{10,2},{3,11},{11,3},{4,12},{12,4},... | collective-permute-start | bytes 221192 | tf_op jit(solution)/shard_map/ppermute | solution.py:770
  372.7 21.0 %collective-permute-start.39 = (bf16[2,2,144,64]{3,2,1,0:T(8,128)(2,1)S(1)}, bf16[2,2,144,64]{3,2,1,0:T(8,128)(2,1)}, u32[]{:S(2)}, u32[]{:S(2)}) collective-permute-start(bf16[2,2,144,64]{3,2,1,0:T(8,128)(2,1)S(1)} %fusion.22.refs_9_), channel_id=1, source_target_pairs={{0,16},{16,0},{1,17},{17,1},{2,18},{18,2},{3,19},{19,3},{4,20},{20... | collective-permute-start | bytes 221192 | tf_op jit(solution)/shard_map/ppermute | solution.py:770
  374.8 18.9 %collective-permute-start.38 = (bf16[4,2,144,256]{3,2,1,0:T(8,128)(2,1)S(1)}, bf16[4,2,144,256]{3,2,1,0:T(8,128)(2,1)}, u32[]{:S(2)}, u32[]{:S(2)}) collective-permute-start(bf16[4,2,144,256]{3,2,1,0:T(8,128)(2,1)S(1)} %fusion.11.refs_8_), channel_id=1, source_target_pairs={{0,8},{8,0},{1,9},{9,1},{2,10},{10,2},{3,11},{11,3},{4,12},{12,4},... | collective-permute-start | bytes 1769480 | tf_op jit(solution)/shard_map/ppermute | solution.py:770
  378.4 15.3 %collective-permute-start.37 = (bf16[4,2,144,256]{3,2,1,0:T(8,128)(2,1)}, bf16[4,2,144,256]{3,2,1,0:T(8,128)(2,1)}, u32[]{:S(2)}, u32[]{:S(2)}) collective-permute-start(bf16[4,2,144,256]{3,2,1,0:T(8,128)(2,1)} %fusion.10.refs_7_), channel_id=1, source_target_pairs={{0,16},{16,0},{1,17},{17,1},{2,18},{18,2},{3,19},{19,3},{4,20},{20... | collective-permute-start | bytes 1769480 | tf_op jit(solution)/shard_map/ppermute | solution.py:770
  400.4 39.0 %collective-permute-start.43 = (bf16[2,144,576]{2,1,0:T(8,128)(2,1)}, bf16[2,144,576]{2,1,0:T(8,128)(2,1)}, u32[]{:S(2)}, u32[]{:S(2)}) collective-permute-start(bf16[2,144,576]{2,1,0:T(8,128)(2,1)} %get-tuple-element.262.refs_7_), channel_id=1, source_target_pairs={{0,1},{1,2},{2,3},{3,0},{4,5},{5,6},{6,7},{7,4},{8,9},{9,10},{10,1... | collective-permute-start | bytes 995336 | tf_op jit(solution)/shard_map/ppermute | solution.py:799
  402.4 37.0 %collective-permute-start.42 = (bf16[2,144,576]{2,1,0:T(8,128)(2,1)S(1)}, bf16[2,144,576]{2,1,0:T(8,128)(2,1)}, u32[]{:S(2)}, u32[]{:S(2)}) collective-permute-start(bf16[2,144,576]{2,1,0:T(8,128)(2,1)S(1)} %get-tuple-element.263.refs_6_), channel_id=1, source_target_pairs={{0,2},{1,3},{2,0},{3,1},{4,6},{5,7},{6,4},{7,5},{8,10},{9,11},{10,... | collective-permute-start | bytes 995336 | tf_op jit(solution)/shard_map/ppermute | solution.py:799
  404.8 34.6 %collective-permute-start.41 = (bf16[2,144,576]{2,1,0:T(8,128)(2,1)S(1)}, bf16[2,144,576]{2,1,0:T(8,128)(2,1)}, u32[]{:S(2)}, u32[]{:S(2)}) collective-permute-start(bf16[2,144,576]{2,1,0:T(8,128)(2,1)S(1)} %get-tuple-element.264.refs_5_), channel_id=1, source_target_pairs={{0,3},{1,0},{2,1},{3,2},{4,7},{5,4},{6,5},{7,6},{8,11},{9,8},{10,9... | collective-permute-start | bytes 995336 | tf_op jit(solution)/shard_map/ppermute | solution.py:799
  443.1 11.5 %collective-permute-start.45 = (bf16[144,1152]{1,0:T(8,128)(2,1)S(1)}, bf16[144,1152]{1,0:T(8,128)(2,1)S(1)}, u32[]{:S(2)}, u32[]{:S(2)}) collective-permute-start(bf16[144,1152]{1,0:T(8,128)(2,1)S(1)} %fusion.18), channel_id=1, source_target_pairs={{0,4},{4,0},{1,5},{5,1},{2,6},{6,2},{3,7},{7,3},{8,12},{12,8},{9,1... | collective-permute-start | bytes 995336 | tf_op jit(solution)/shard_map/ppermute | solution.py:705
  444.8 16.9 %all-to-all-start.5 = ((f32[32,1,2812]{2,1,0:T(1,128)}), f32[32,1,2812]{2,1,0:T(1,128)}, u32[]{:S(2)}, u32[]{:S(2)}) async-start(f32[32,1,2812]{2,1,0:T(1,128)} %all_to_all.27), calls=%async_computation.5 | async-start | bytes 720896 | tf_op jit(solution)/shard_map/all_to_all | solution.py:1033
  (91 other events, 695.4 us)

commit v4 on v3

--- a/solution.py
+++ b/solution.py
@@ -516,24 +516,31 @@
     )
 
 
-def last_sums(arrived, early, bins, own_bins, cols, bias_cols):
-    sources, images, width = early.shape[0], early.shape[1], early.shape[2]
-    ends = [int(x) for x in np.cumsum([images * width] + [cols] * images + [bias_cols, 4])]
-    table_rows = own_bins.shape[0]
-
-    def kernel(got, early, bins, own_bins, ada_ref, b_ref, bias_ref, rms_ref, table_ref):
+def last_sums(arrived, own_bins, images, width, cols, bias_cols):
+    sizes = [images * width, images * width] + [cols] * images + [bias_cols, 4]
+    ends = [int(x) for x in np.cumsum(sizes)]
+    table_rows = own_bins.shape[1]
+
+    def kernel(got, own_bins, ada_ref, b_ref, bias_ref, rms_ref, table_ref):
         ada, table, flat = 0.0, 0.0, 0.0
         for i in range(images):
-            d_mod = got[:, ends[i] : ends[i + 1]]
+            d_mod = got[:, ends[1 + i] : ends[2 + i]]
             flat = flat + total(d_mod)
-            ada = ada + dot_tn(d_mod.astype(BF), early[:, i, :].astype(BF))
-            picks = jnp.where(own_bins[...] == bins[i : i + 1, :], 1.0, 0.0).astype(F32)
-            d_cond = got[:, i * width : (i + 1) * width]
-            table = table + jnp.dot(picks, d_cond, precision=EXACT, preferred_element_type=F32)
+            silu = got[:, ends[0] + i * width : ends[0] + (i + 1) * width]
+            ada = ada + dot_tn(d_mod.astype(BF), silu.astype(BF))
+            bins = got[:, ends[-1] + i : ends[-1] + i + 1]
+            picks = jnp.where(own_bins[...] == bins, 1.0, 0.0).astype(F32)
+            table = table + lax.dot_general(
+                picks,
+                got[:, i * width : (i + 1) * width],
+                TN,
+                precision=EXACT,
+                preferred_element_type=F32,
+            )
         ada_ref[...] = ada
         b_ref[...] = flat
-        bias_ref[...] = total(got[:, ends[images] : ends[images + 1]])
-        sums = total(got[:, ends[images + 1] :])
+        bias_ref[...] = total(got[:, ends[-3] : ends[-2]])
+        sums = total(got[:, ends[-2] : ends[-1]])
         rms_ref[...] = jnp.sqrt(sums[:, :3] / (sums[:, 3:] * width))
         table_ref[...] = table
 
@@ -541,7 +548,7 @@
         kernel,
         "last_sums",
         (1,),
-        [(x, None, None) for x in (arrived, early, bins, own_bins)],
+        [(x, None, None) for x in (arrived, own_bins)],
         [
             (shape((cols, width), F32), None, None),
             (shape((1, cols), F32), None, None),
@@ -831,10 +838,6 @@
     cosine, sine = jnp.cos(angle), jnp.sin(angle)
     cos = jnp.concatenate([cosine[0], cosine[0], cosine[1], cosine[1]], axis=0)
     sin = jnp.concatenate([sine[0], sine[0], sine[1], sine[1]], axis=0)
-    def spread(value):
-        return lax.all_to_all(jnp.broadcast_to(value[None], (devices,) + value.shape), axes, 0, 0)
-
-    early = jnp.concatenate([silu_low.astype(F32), time_bins[:, None].astype(F32)], axis=1)
     own_heads = attn_fwd(
         lens, place, a1_all, heads_own[None], 1, tn, (), (), cos, sin, heads, seq
     )
@@ -953,12 +956,10 @@
         down_sends = reduce_send(down_state, gu_sent)
         da2_own, da2_peer = back_out(d_gate_up, gu_all, "mlp_back", deps=gu_sent + down_sends)
         one_sends = reduce_send(one, da2_own)
-        early_all = spread(later(early, (da2_own,)))
         dh, da_own, sums_back = through_mlp(one_sends)
         da_all = (da_own, peer(da_own))
-        bins_all = early_all[:, :, width].T.astype(jnp.int32)
         two_sends = reduce_send(two, da_own)
-        d_qkv, da1_own, da1_peer = back_heads((early_all,) + two_sends)
+        d_qkv, da1_own, da1_peer = back_heads(two_sends)
         heads_state, heads_sent = reduce_first(
             [(a1_all, d_qkv), (da_all, attended)], heads_parts, two_sends
         )
@@ -979,8 +980,6 @@
             heads_rows[:2] + (jnp.concatenate(heads_rows[2:], axis=0),), axis=3
         )
     else:
-        early_all = spread(early)
-        bins_all = early_all[:, :, width].T.astype(jnp.int32)
         d_gate_up = mlp_mid(dm_all, down_all, gate_up)
         da2_own, da2_peer = back_out(d_gate_up, gu_all, "mlp_back")
         dh, da_own, sums_back = through_mlp(())
@@ -1012,9 +1011,12 @@
             d_mod.reshape(image_count, devices, ada_cols).transpose(1, 0, 2).reshape(devices, -1),
             d_bias.reshape(devices, bias_cols),
             jnp.broadcast_to(sums[None], (devices, 4)),
+            jnp.broadcast_to(time_bins.astype(F32)[None], (devices, image_count)),
         ],
         axis=1,
     )
+    kept = jnp.broadcast_to(silu_low.astype(F32).reshape(1, -1), (devices, image_count * width))
+    ready = jnp.concatenate([kept, ready], axis=1)
     if square:
         heads_blocks = z_sends(heads_rows)
         d_silu = ada_back(d_mod, w_ada, deps=(ready, mlp_z) + tuple(heads_blocks))
@@ -1035,7 +1037,7 @@
     flat = (at_q * nc + at_c) * tn + at_z
     own_bins = flat * table_rows + jnp.arange(table_rows, dtype=jnp.int32)
     grad_ada, grad_b_ada, grad_bias, rms_values, grad_table = last_sums(
-        arrived, early_all[:, :, :width], bins_all, own_bins[:, None], ada_cols, bias_cols
+        arrived, own_bins[None, :].astype(F32), image_count, width, ada_cols, bias_cols
     )
 
     def joined(value, parts):

time: 474 us -> 475 us (level)
  starting transfers between devices: 73.7 us -> 63.1 us
  waiting for transfers between devices: 43.4 us -> 53 us
    all_to_all x1, waiting for transfers between devices: 16.6 us -> 0.01 us  [reduce_z(): return later(lax.all_to_all(rows, 'z', 0, 0), marks)]
    ppermute x3, waiting for transfers between devices: 0.01 us -> 15 us  [reduce_z_steps(): got = [lax.ppermute(sends[r], 'z', ring(tn, -r)) for r in range(1, tn)]]
    all_to_all x1 -> x0, starting transfers between devices: 5.8 us -> none  [spread(): lax.all_to_all(jnp.broadcast_to(value[None], (devices,) + value.shape), a...]
    all_to_all x1, waiting for transfers between devices: 2.35 us -> 7.87 us  [local(): arrived = lax.all_to_all(message, axes, 0, 0, tiled=True)]
    ppermute x10, waiting for transfers between devices: 0.15 us -> 5.5 us  [reduce_first(): lax.ppermute(x, part[2], swap)]
    unnamed x178 -> x162, local copies, waits for them, and re-layouts: 15.5 us -> 16.8 us
  transfers between devices with their start and end apart: 52 -> 51, of which waited for: 13 -> 18; matrix products, arithmetic and copies ran while one was open for 23% -> 23% of each run, Pallas kernels for 43% -> 43%
where the time goes in v4:
time: 475 us; the launch traced here: 467 us
  Pallas kernels  221 us (47%)
  starting transfers between devices  63.1 us (13%)
  other arithmetic  61.7 us (13%)
  local copies, waits for them, and re-layouts  53.7 us (11%)
  waiting for transfers between devices  53 us (11%)
  matrix products  11.5 us (2%)
    pallas_call x21, Pallas kernels, call(): pl.pallas_call(body, grid_spec=pltpu.PrefetchScalarGridSpec(num_scalar_pr...  221 us
    unnamed x162, local copies, waits for them, and re-layouts  16.8 us
    all_to_all x3, starting transfers between devices, along_z(): lax.all_to_all(jnp.broadcast_to(piece[None], (tn,) + piece.shape), 'z', 0...  15.1 us
    ppermute x3, waiting for transfers between devices, reduce_z_steps(): got = [lax.ppermute(sends[r], 'z', ring(tn, -r)) for r in range(1, tn)]  15 us
    convert_element_type x10, other arithmetic, reduce_send(): (k[1].astype(F32) + g[1].astype(F32)).astype(BF)  13.9 us
    convert_element_type x10, other arithmetic, reduce_second(): (k[0].astype(F32) + g[0].astype(F32) + h.astype(F32)).astype(BF)  13.1 us
    another operation x12, other arithmetic, plane_first(): return (jnp.stack([first, first_x]), jnp.stack([second, second_y]))  11.8 us
    ppermute x10, starting transfers between devices, reduce_second(): lax.ppermute(x, other[part[2]], swap)  10.6 us
  transfers between devices with their start and end apart: 51, of which 18 were waited for; matrix products, arithmetic and copies ran while one was open for 23% of the time, Pallas kernels for 43%

profile of v4, /device:TPU:0, one launch (start us, length us, event | category | flops | bytes accessed | tf_op | source)
XLA Modules:
  0.0 466.6 jit_solution(7652721314008835767)
XLA Ops:
  6.4 6.0 %all-to-all-start = ((bf16[4,144,1152]{2,1,0:T(8,128)(2,1)}), bf16[4,144,1152]{2,1,0:T(8,128)(2,1)}, u32[]{:S(2)}, u32[]{:S(2)}) async-start(bf16[4,144,1152]{2,1,0:T(8,128)(2,1)} %broadcast_in_dim.32), calls=%async_computation | async-start | bytes 2654208 | tf_op jit(solution)/shard_map/all_to_all | solution.py:722
  12.4 3.1 fusion.28
  15.6 8.3 %convolution_add_fusion = f32[2,6912]{1,0:T(2,128)} fusion(bf16[1152,6912]{1,0:T(8,128)(2,1)} %refs_1_.1, f32[6912]{0:T(1024)S(1)} %copy-done.71, f32[2,1152]{1,0:T(2,128)S(1)} %get-tuple-element.303), kind=kOutput, calls=%fused_computation | convolution fusion | flops 31875840 | bytes 16017408 | tf_op jit(solution)/shard_map/dot_general | solution.py:26
  27.4 4.8 %pre_attention.1 = (bf16[512,1152]{1,0:T(8,128)(2,1)}, bf16[512,1152]{1,0:T(8,128)(2,1)}, f32[2,2,1152]{2,1,0:T(2,128)}) custom-call(s32[2]{0:T(128)} %refs_0_.9, f32[2,6,1152]{2,1,0:T(8,128)} %reshape.225.refs_1_, f32[1,1152]{1,0:T(1,128)} %broadcast_in_dim.30.refs_2_, f32[512,1152]{1,0:T(8,128)} %refs_3_.5, f32[512,1152]{1,0:T(8,128)} %refs_4_.5), custom_call_target="tpu_custom_call" | custom-call | flops 1 | bytes 1 | tf_op jit(solution)/shard_map/pre_attention/pallas_call | solution.py:52
  32.4 2.4 dynamic-slice_bitcast_fusion
  34.8 5.6 %copy.37 = bf16[2,384,1152]{2,1,0:T(8,128)(2,1)S(1)} copy(bf16[2,384,1152]{1,0,2:T(2,128)(2,1)} %dynamic-slice_bitcast_fusion) | data formatting | bytes 3538944 | tf_op jit(solution)/shard_map/dynamic_slice | solution.py:716
  40.5 1.9 dynamic-slice_bitcast_fusion.1
  46.2 4.4 all-to-all-start.1
  59.2 6.0 %collective-permute-done.3 = bf16[3,64,1152]{2,1,0:T(8,128)(2,1)S(1)} collective-permute-done((bf16[3,64,1152]{2,1,0:T(8,128)(2,1)}, bf16[3,64,1152]{2,1,0:T(8,128)(2,1)S(1)}, u32[]{:S(2)}, u32[]{:S(2)}) %collective-permute-start.3) | collective-permute-done | bytes 442400 | tf_op jit(solution)/shard_map/ppermute | solution.py:732
  68.7 3.3 collective-permute-done.2
  76.8 10.5 %attn_fwd.2 = (bf16[4,2,72,1024]{3,2,1,0:T(8,128)(2,1)}, bf16[4,2,72,1024]{3,2,1,0:T(8,128)(2,1)}, bf16[4,2,72,1024]{3,2,1,0:T(8,128)(2,1)}, bf16[4,144,1024]{2,...) custom-call(s32[4]{0:T(128)} %pad_add_fusion.1.refs_0_, s32[3]{0:T(128)} %pad_add_fusion.2.refs_1_.refs_0_, ...), custom_call_target="tpu_custom_call" | custom-call | flops 3112173568 | bytes 20000000 | tf_op jit(solution)/shard_map/attn_fwd/pallas_call | solution.py:52
  87.4 2.5 collective-permute-done.5.refs_6_
  89.9 7.6 %collective-permute-done.4.refs_5_ = bf16[2,3,80,1152]{3,2,1,0:T(8,128)(2,1)S(1)} collective-permute-done((bf16[2,3,80,1152]{3,2,1,0:T(8,128)(2,1)S(1)}, bf16[2,3,80,1152]{3,2,1,0:T(8,128)(2,1)S(1)}, u32[]{:S(2)}, u32[]{:S(2)}) %collective-permute-start.4) | collective-permute-done | bytes 1105952 | tf_op jit(solution)/shard_map/ppermute | solution.py:737
  103.1 6.5 %assemble.3.refs_7_.refs_9_ = bf16[4,4,144,1152]{3,2,1,0:T(8,128)(2,1)} custom-call(s32[3]{0:T(128)} %pad_add_fusion.2.refs_1_.refs_0_, bf16[4,144,1152]{2,1,0:T(8,128)(2,1)} %get-tuple-element.265.refs_1_, bf16[4,144,1152]{2,1,0:T(8,128)(2,1)} %all-to-all-done.refs_2_, bf16[2,3,80,1152]{3,2,1,0:T(8,128)(2,1)} %copy-done.10, ...), custom_call_target="tpu_custom_call" | custom-call | bytes 10616832 | tf_op jit(solution)/shard_map/assemble/pallas_call | solution.py:52
  110.5 4.7 %all-to-all-start.2 = ((bf16[4,96,1152]{2,1,0:T(8,128)(2,1)}), bf16[4,96,1152]{2,1,0:T(8,128)(2,1)S(1)}, u32[]{:S(2)}, u32[]{:S(2)}) async-start(bf16[4,96,1152]{2,1,0:T(8,128)(2,1)} %broadcast_in_dim.35), calls=%async_computation.2 | async-start | bytes 1769472 | tf_op jit(solution)/shard_map/all_to_all | solution.py:722
  115.9 2.3 pad_maximum_fusion.2.refs_10_.refs_3_
  119.2 2.3 pad_maximum_fusion.3.refs_11_.refs_4_
  122.0 23.6 %attn_fwd.3 = (bf16[4,2,72,1024]{3,2,1,0:T(8,128)(2,1)}, bf16[4,2,72,1024]{3,2,1,0:T(8,128)(2,1)}, bf16[4,2,72,1024]{3,2,1,0:T(8,128)(2,1)}, bf16[4,144,1024]{2,...) custom-call(s32[4]{0:T(128)} %pad_add_fusion.1.refs_0_, ...), custom_call_target="tpu_custom_call", output_to_operand_aliasing={{0}: (12, {}), {1}: (13, {}), {2}: (14, {}), {3}: (15, {})} | custom-call | flops 9336520704 | bytes 20000000 | tf_op jit(solution)/shard_map/attn_fwd/pallas_call | solution.py:52
  149.8 5.1 %pre_mlp.1 = (f32[512,1152]{1,0:T(8,128)}, bf16[512,1152]{1,0:T(8,128)(2,1)}, f32[2,1,1152]{2,1,0:T(1,128)}) custom-call(s32[2]{0:T(128)} %refs_0_.9, f32[2,6,1152]{2,1,0:T(8,128)} %reshape.225.refs_1_, f32[1,1152]{1,0:T(1,128)} %broadcast_in_dim.30.refs_2_, f32[512,1152]{1,0:T(8,128)} %refs_3_.5, f32[512,1152]{1,0:T(8,128)} %get-tuple-element.151.refs_4_.refs_5_, ...), custom_call_target="tpu_custom_call" | custom-call | flops 1 | bytes 1 | tf_op jit(solution)/shard_map/pre_mlp/pallas_call | solution.py:52
  157.0 7.6 %assemble.4.refs_2_.refs_1_ = bf16[4,4,192,1152]{3,2,1,0:T(8,128)(2,1)} custom-call(s32[3]{0:T(128)} %pad_add_fusion.2.refs_1_.refs_0_, bf16[4,192,1152]{2,1,0:T(8,128)(2,1)} %bitcast.165, bf16[4,192,1152]{2,1,0:T(8,128)(2,1)} %copy-done.2, bf16[2,3,96,1152]{3,2,1,0:T(8,128)(2,1)} %pad_maximum_fusion.2.refs_10_.refs_3_, ...), custom_call_target="tpu_custom_call" | custom-call | bytes 14155776 | tf_op jit(solution)/shard_map/assemble/pallas_call | solution.py:52
  167.7 13.8 %mlp_fwd.1 = (f32[4,1024,768]{2,1,0:T(8,128)}, bf16[4,1024,384]{2,1,0:T(8,128)(2,1)}) custom-call(bf16[512,1152]{1,0:T(8,128)(2,1)} %get-tuple-element.158.refs_7_.refs_0_.refs_1_, bf16[512,1152]{1,0:T(8,128)(2,1)} %collective-permute-done.11.refs_1_.refs_2_, bf16[4,4,192,1152]{3,2,1,0:T(8,128)(2,1)} %assemble.4.refs_2_.refs_1_, ...), custom_call_target="tpu_custom_call" | custom-call | flops 7247757312 | bytes 26000000 | tf_op jit(solution)/shard_map/mlp_fwd/pallas_call | solution.py:52
  184.8 10.7 %grad_split.3 = (bf16[2,2,2,144,384]{4,3,2,1,0:T(8,128)(2,1)}, bf16[2,2,2,144,384]{4,3,2,1,0:T(8,128)(2,1)}, bf16[2,2,2,144,384]{4,3,2,1,0:T(8,128)(2,1)}, bf16[2,2,2,144,384]{4,3,2,1,0:T(8,128)(2,1)}) custom-call(s32[3]{0:T(128)} %pad_add_fusion.2.refs_1_.refs_0_, bf16[512,1152]{1,0:T(8,128)(2,1)} %get-tuple-element.164.refs_1_.refs_0_, ...), custom_call_target="tpu_custom_call" | custom-call | flops 3623878656 | bytes 9043968 | tf_op jit(solution)/shard_map/grad_split/pallas_call | solution.py:52
  196.5 5.6 %assemble.5.refs_2_.refs_1_ = bf16[4,4,96,1152]{3,2,1,0:T(8,128)(2,1)} custom-call(s32[3]{0:T(128)} %pad_add_fusion.2.refs_1_.refs_0_, bf16[4,96,1152]{2,1,0:T(8,128)(2,1)} %bitcast.167, bf16[4,96,1152]{2,1,0:T(8,128)(2,1)} %copy-done.6, bf16[2,3,48,1152]{3,2,1,0:T(8,128)(2,1)} %copy-done.15, bf16[2,3,48,1152]{3,2,1,0:T(8,128)(2,1)} %copy-done.17, ...), custom_call_target="tpu_custom_call" | custom-call | bytes 7077888 | tf_op jit(solution)/shard_map/assemble/pallas_call | solution.py:52
  203.2 12.5 %mlp_mid.1.refs_3_.refs_0_ = bf16[4,1024,768]{2,1,0:T(8,128)(2,1)} custom-call(bf16[512,1152]{1,0:T(8,128)(2,1)} %get-tuple-element.164.refs_1_.refs_0_, bf16[512,1152]{1,0:T(8,128)(2,1)} %copy-done.31, bf16[4,4,96,1152]{3,2,1,0:T(8,128)(2,1)} %assemble.5.refs_2_.refs_1_, f32[4,1024,768]{2,1,0:T(8,128)} %get-tuple-element.167.refs_3_, ...), custom_call_target="tpu_custom_call" | custom-call | flops 3623878656 | bytes 26000000 | tf_op jit(solution)/shard_map/mlp_mid/pallas_call | solution.py:52
  215.8 14.5 %grad_split.4 = (bf16[2,2,2,144,384]{4,3,2,1,0:T(8,128)(2,1)}, bf16[2,2,2,144,384]{4,3,2,1,0:T(8,128)(2,1)}, bf16[2,2,2,144,384]{4,3,2,1,0:T(8,128)(2,1)}, bf16[...) custom-call(s32[3]{0:T(128)} %pad_add_fusion.2.refs_1_.refs_0_, ...), custom_call_target="tpu_custom_call" | custom-call | flops 7247757312 | bytes 15728640 | tf_op jit(solution)/shard_map/grad_split/pallas_call | solution.py:52
  234.2 14.0 %mlp_back.1 = (f32[512,1152]{1,0:T(8,128)}, bf16[512,1152]{1,0:T(8,128)(2,1)}) custom-call(bf16[4,1024,768]{2,1,0:T(8,128)(2,1)} %mlp_mid.1.refs_3_.refs_0_, bf16[4,4,192,1152]{3,2,1,0:T(8,128)(2,1)} %assemble.4.refs_2_.refs_1_, bf16[2,2,2,144,384]{4,3,2,1,0:T(8,128)(2,1)} %get-tuple-element.168.refs_2_, ...), custom_call_target="tpu_custom_call" | custom-call | flops 7247757312 | bytes 16908288 | tf_op jit(solution)/shard_map/mlp_back/pallas_call | solution.py:52
  250.8 1.9 fusion.14.refs_9_
  252.7 1.9 fusion.15.refs_10_
  255.6 8.2 %back_mlp.1 = (f32[512,1152]{1,0:T(8,128)}, bf16[512,1152]{1,0:T(8,128)(2,1)}, f32[2,4,1152]{2,1,0:T(4,128)}) custom-call(s32[2]{0:T(128)} %refs_0_.9, f32[2,6,1152]{2,1,0:T(8,128)} %reshape.225.refs_1_, f32[1,1152]{1,0:T(1,128)} %broadcast_in_dim.30.refs_2_, f32[512,1152]{1,0:T(8,128)} %get-tuple-element.157.refs_3_, f32[512,1152]{1,0:T(8,128)} %refs_4_.5, ...), custom_call_target="tpu_custom_call" | custom-call | flops 1 | bytes 30000000 | tf_op jit(solution)/shard_map/back_mlp/pallas_call | solution.py:52
  266.1 5.0 %collective-permute-done.23 = bf16[2,2,2,144,384]{4,3,2,1,0:T(8,128)(2,1)} collective-permute-done((bf16[2,2,2,144,384]{4,3,2,1,0:T(8,128)(2,1)}, bf16[2,2,2,144,384]{4,3,2,1,0:T(8,128)(2,1)}, u32[]{:S(2)}, u32[]{:S(2)}) %collective-permute-start.23) | collective-permute-done | bytes 884768 | tf_op jit(solution)/shard_map/ppermute | solution.py:768
  273.2 2.0 fusion.16.refs_10_.refs_7_
  275.2 1.9 fusion.17.refs_11_.refs_8_
  278.1 30.9 %attn_bwd.1 = (bf16[4,432,1024]{2,1,0:T(8,128)(2,1)}, f32[512,1152]{1,0:T(8,128)}, bf16[512,1152]{1,0:T(8,128)(2,1)}) custom-call(s32[4]{0:T(128)} %pad_add_fusion.1.refs_0_, bf16[512,1152]{1,0:T(8,128)(2,1)} %get-tuple-element.187.refs_1_.refs_3_, bf16[512,1152]{1,0:T(8,128)(2,1)} %collective-permute-done.22.refs_2_.refs_4_, ...), custom_call_target="tpu_custom_call" | custom-call | flops 16173236224 | bytes 20000000 | tf_op jit(solution)/shard_map/attn_bwd/pallas_call | solution.py:52
  310.1 15.9 %grad_split.5 = (bf16[2,4,2,144,256]{4,3,2,1,0:T(8,128)(2,1)}, bf16[2,4,2,144,256]{4,3,2,1,0:T(8,128)(2,1)}, bf16[2,4,2,144,256]{4,3,2,1,0:T(8,128)(2,1)}, bf16[...) custom-call(s32[3]{0:T(128)} %pad_add_fusion.2.refs_1_.refs_0_, ...), custom_call_target="tpu_custom_call" | custom-call | flops 5435817984 | bytes 12386304 | tf_op jit(solution)/shard_map/grad_split/pallas_call | solution.py:52
  337.6 4.9 %all-to-all-start.3 = ((bf16[4,2,144,1152]{3,2,1,0:T(8,128)(2,1)}), bf16[4,2,144,1152]{3,2,1,0:T(8,128)(2,1)S(1)}, u32[]{:S(2)}, u32[]{:S(2)}) async-start(bf16[4,2,144,1152]{3,2,1,0:T(8,128)(2,1)} %maximum_maximum_fusion.refs_11_), calls=%async_computation.3 | async-start | bytes 5308416 | tf_op jit(solution)/shard_map/all_to_all | solution.py:800
  351.0 6.2 %back_attention.1 = (f32[512,1152]{1,0:T(8,128)}, f32[2,2,1152]{2,1,0:T(2,128)}) custom-call(s32[2]{0:T(128)} %refs_0_.9, f32[2,6,1152]{2,1,0:T(8,128)} %reshape.225.refs_1_, f32[1,1152]{1,0:T(1,128)} %broadcast_in_dim.30.refs_2_, f32[512,1152]{1,0:T(8,128)} %refs_3_.5, f32[512,1152]{1,0:T(8,128)} %get-tuple-element.186.refs_4_, ...), custom_call_target="tpu_custom_call" | custom-call | flops 1 | bytes 1 | tf_op jit(solution)/shard_map/back_attention/pallas_call | solution.py:52
  357.1 9.8 %mlp_out.1 = (f32[512,1152]{1,0:T(8,128)}, bf16[512,1152]{1,0:T(8,128)(2,1)}) custom-call(bf16[4,1024,384]{2,1,0:T(8,128)(2,1)} %get-tuple-element.161.refs_3_.refs_0_, bf16[4,4,96,1152]{3,2,1,0:T(8,128)(2,1)} %assemble.5.refs_2_.refs_1_, f32[2,2,1152]{2,1,0:T(2,128)} %get-tuple-element.211.refs_2_), custom_call_target="tpu_custom_call" | custom-call | flops 3623878656 | bytes 10223616 | tf_op jit(solution)/shard_map/mlp_out/pallas_call | solution.py:52
  370.6 2.0 fusion.11.refs_8_
  378.3 5.5 %post_mlp.1 = (f32[512,1152]{1,0:T(8,128)}, f32[2,2,1152]{2,1,0:T(2,128)}) custom-call(s32[2]{0:T(128)} %refs_0_.9, f32[2,6,1152]{2,1,0:T(8,128)} %reshape.225.refs_1_, f32[1,1152]{1,0:T(1,128)} %broadcast_in_dim.29.refs_2_, f32[512,1152]{1,0:T(8,128)} %get-tuple-element.157.refs_3_, f32[512,1152]{1,0:T(8,128)} %refs_4_.5, ...), custom_call_target="tpu_custom_call" | custom-call | flops 1 | bytes 1 | tf_op jit(solution)/shard_map/post_mlp/pallas_call | solution.py:52
  398.3 3.8 collective-permute-start.41
  403.9 1.9 pad_maximum_fusion.18
  408.3 9.9 %ada_back.1 = f32[16,1152]{1,0:T(8,128)} custom-call(bf16[16,6912]{1,0:T(8,128)(2,1)} %scatter.4.refs_0_, bf16[1152,6912]{1,0:T(8,128)(2,1)} %refs_1_.1, f32[32,2814]{1,0:T(8,128)} %concatenate.87.refs_2_, bf16[4,2,144,1152]{3,2,1,0:T(8,128)(2,1)} %copy-done.3, bf16[2,144,576]{2,1,0:T(8,128)(2,1)} %bitcast.170, ...), custom_call_target="tpu_custom_call" | custom-call | flops 20000000000 | bytes 15925248 | tf_op jit(solution)/shard_map/ada_back/pallas_call | solution.py:52
  420.0 15.0 %collective-permute-done.42 = bf16[2,144,576]{2,1,0:T(8,128)(2,1)} collective-permute-done((bf16[2,144,576]{2,1,0:T(8,128)(2,1)}, bf16[2,144,576]{2,1,0:T(8,128)(2,1)}, u32[]{:S(2)}, u32[]{:S(2)}) %collective-permute-start.42) | collective-permute-done | bytes 331808 | tf_op jit(solution)/shard_map/ppermute | solution.py:806
  441.2 3.5 all-to-all-start.4
  446.1 2.8 place_heads.1
  453.7 7.9 %all-to-all-done.4 = f32[32,1,5118]{2,1,0:T(1,128)} async-done(((f32[32,1,5118]{2,1,0:T(1,128)}), f32[32,1,5118]{2,1,0:T(1,128)}, u32[]{:S(2)}, u32[]{:S(2)}) %all-to-all-start.4) | async-done | bytes 655136 | tf_op jit(solution)/shard_map/all_to_all | solution.py:1035
  461.5 2.0 copy.44
  463.6 2.7 last_sums.1
  (347 shorter events, 128.7 us)
Async XLA Ops:
  2.9 55.5 %collective-permute-start = (s32[1026]{0:T(1024)}, s32[1026]{0:T(1024)}, u32[]{:S(2)}, u32[]{:S(2)}) collective-permute-start(s32[1026]{0:T(1024)} %pad_add_fusion), channel_id=1, source_target_pairs={{0,4},{4,0},{1,5},{5,1},{2,6},{6,2},{3,7},{7,3},{8,12},{12,8},{9,1... | collective-permute-start | bytes 12320 | tf_op jit(solution)/shard_map/ppermute | solution.py:712
  6.4 38.5 %all-to-all-start = ((bf16[4,144,1152]{2,1,0:T(8,128)(2,1)}), bf16[4,144,1152]{2,1,0:T(8,128)(2,1)}, u32[]{:S(2)}, u32[]{:S(2)}) async-start(bf16[4,144,1152]{2,1,0:T(8,128)(2,1)} %broadcast_in_dim.32), calls=%async_computation | async-start | bytes 2654208 | tf_op jit(solution)/shard_map/all_to_all | solution.py:722
  32.2 44.7 %collective-permute-start.1 = (bf16[512,1152]{1,0:T(8,128)(2,1)}, bf16[512,1152]{1,0:T(8,128)(2,1)}, u32[]{:S(2)}, u32[]{:S(2)}) collective-permute-start(bf16[512,1152]{1,0:T(8,128)(2,1)} %get-tuple-element.137.refs_2_.refs_1_), channel_id=1, source_target_pairs={{0,4},{4,0},{1,5},{5,1},{2,6},{6,2},{3,7},{7,3},{8,12},{12,8},{9,1... | collective-permute-start | bytes 3538952 | tf_op jit(solution)/shard_map/ppermute | solution.py:712
  46.2 52.3 %all-to-all-start.1 = ((bf16[4,192,1152]{2,1,0:T(8,128)(2,1)}), bf16[4,192,1152]{2,1,0:T(8,128)(2,1)S(1)}, u32[]{:S(2)}, u32[]{:S(2)}) async-start(bf16[4,192,1152]{2,1,0:T(8,128)(2,1)} %broadcast_in_dim.34), calls=%async_computation.1 | async-start | bytes 3538944 | tf_op jit(solution)/shard_map/all_to_all | solution.py:722
  52.7 12.4 %collective-permute-start.3 = (bf16[3,64,1152]{2,1,0:T(8,128)(2,1)}, bf16[3,64,1152]{2,1,0:T(8,128)(2,1)S(1)}, u32[]{:S(2)}, u32[]{:S(2)}) collective-permute-start(bf16[3,64,1152]{2,1,0:T(8,128)(2,1)} %get-tuple-element.287), channel_id=1, source_target_pairs={{0,16},{16,0},{1,17},{17,1},{2,18},{18,2},{3,19},{19,3},{4,20},{20... | collective-permute-start | bytes 1327112 | tf_op jit(solution)/shard_map/ppermute | solution.py:732
  56.3 15.7 %collective-permute-start.2 = (bf16[3,80,1152]{2,1,0:T(8,128)(2,1)}, bf16[3,80,1152]{2,1,0:T(8,128)(2,1)}, u32[]{:S(2)}, u32[]{:S(2)}) collective-permute-start(bf16[3,80,1152]{2,1,0:T(8,128)(2,1)} %get-tuple-element.285), channel_id=1, source_target_pairs={{0,8},{8,0},{1,9},{9,1},{2,10},{10,2},{3,11},{11,3},{4,12},{12,4},... | collective-permute-start | bytes 1658888 | tf_op jit(solution)/shard_map/ppermute | solution.py:731
  67.2 22.7 %collective-permute-start.5 = (bf16[2,3,64,1152]{3,2,1,0:T(8,128)(2,1)S(1)}, bf16[2,3,64,1152]{3,2,1,0:T(8,128)(2,1)}, u32[]{:S(2)}, u32[]{:S(2)}) collective-permute-start(bf16[2,3,64,1152]{3,2,1,0:T(8,128)(2,1)S(1)} %pad_maximum_fusion.5.refs_4_), channel_id=1, source_target_pairs={{0,8},{8,0},{1,9},{9,1},{2,10},{10,2},{3,11},{11,3},{4,12},{12,4},... | collective-permute-start | bytes 2654216 | tf_op jit(solution)/shard_map/ppermute | solution.py:737
  73.2 24.3 %collective-permute-start.4 = (bf16[2,3,80,1152]{3,2,1,0:T(8,128)(2,1)S(1)}, bf16[2,3,80,1152]{3,2,1,0:T(8,128)(2,1)S(1)}, u32[]{:S(2)}, u32[]{:S(2)}) collective-permute-start(bf16[2,3,80,1152]{3,2,1,0:T(8,128)(2,1)S(1)} %pad_maximum_fusion.4.refs_3_), channel_id=1, source_target_pairs={{0,16},{16,0},{1,17},{17,1},{2,18},{18,2},{3,19},{19,3},{4,20},{20... | collective-permute-start | bytes 3317768 | tf_op jit(solution)/shard_map/ppermute | solution.py:737
  99.8 15.5 %collective-permute-start.6 = (bf16[3,96,1152]{2,1,0:T(8,128)(2,1)S(1)}, bf16[3,96,1152]{2,1,0:T(8,128)(2,1)}, u32[]{:S(2)}, u32[]{:S(2)}) collective-permute-start(bf16[3,96,1152]{2,1,0:T(8,128)(2,1)S(1)} %get-tuple-element.281.refs_7_), channel_id=1, source_target_pairs={{0,8},{8,0},{1,9},{9,1},{2,10},{10,2},{3,11},{11,3},{4,12},{12,4},... | collective-permute-start | bytes 1990664 | tf_op jit(solution)/shard_map/ppermute | solution.py:731
  102.2 13.6 %collective-permute-start.7 = (bf16[3,96,1152]{2,1,0:T(8,128)(2,1)S(1)}, bf16[3,96,1152]{2,1,0:T(8,128)(2,1)}, u32[]{:S(2)}, u32[]{:S(2)}) collective-permute-start(bf16[3,96,1152]{2,1,0:T(8,128)(2,1)S(1)} %get-tuple-element.279.refs_8_), channel_id=1, source_target_pairs={{0,16},{16,0},{1,17},{17,1},{2,18},{18,2},{3,19},{19,3},{4,20},{20... | collective-permute-start | bytes 1990664 | tf_op jit(solution)/shard_map/ppermute | solution.py:732
  110.5 35.1 %all-to-all-start.2 = ((bf16[4,96,1152]{2,1,0:T(8,128)(2,1)}), bf16[4,96,1152]{2,1,0:T(8,128)(2,1)S(1)}, u32[]{:S(2)}, u32[]{:S(2)}) async-start(bf16[4,96,1152]{2,1,0:T(8,128)(2,1)} %broadcast_in_dim.35), calls=%async_computation.2 | async-start | bytes 1769472 | tf_op jit(solution)/shard_map/all_to_all | solution.py:722
  118.2 29.2 %collective-permute-start.9 = (bf16[2,3,96,1152]{3,2,1,0:T(8,128)(2,1)}, bf16[2,3,96,1152]{3,2,1,0:T(8,128)(2,1)S(1)}, u32[]{:S(2)}, u32[]{:S(2)}) collective-permute-start(bf16[2,3,96,1152]{3,2,1,0:T(8,128)(2,1)} %pad_maximum_fusion.2.refs_10_.refs_3_), channel_id=1, source_target_pairs={{0,16},{16,0},{1,17},{17,1},{2,18},{18,2},{3,19},{19,3},{4,20},{20... | collective-permute-start | bytes 3981320 | tf_op jit(solution)/shard_map/ppermute | solution.py:737
  121.5 27.3 %collective-permute-start.10 = (bf16[2,3,96,1152]{3,2,1,0:T(8,128)(2,1)}, bf16[2,3,96,1152]{3,2,1,0:T(8,128)(2,1)S(1)}, u32[]{:S(2)}, u32[]{:S(2)}) collective-permute-start(bf16[2,3,96,1152]{3,2,1,0:T(8,128)(2,1)} %pad_maximum_fusion.3.refs_11_.refs_4_), channel_id=1, source_target_pairs={{0,8},{8,0},{1,9},{9,1},{2,10},{10,2},{3,11},{11,3},{4,12},{12,4},... | collective-permute-start | bytes 3981320 | tf_op jit(solution)/shard_map/ppermute | solution.py:737
  154.9 12.8 %collective-permute-start.11 = (bf16[512,1152]{1,0:T(8,128)(2,1)}, bf16[512,1152]{1,0:T(8,128)(2,1)}, u32[]{:S(2)}, u32[]{:S(2)}) collective-permute-start(bf16[512,1152]{1,0:T(8,128)(2,1)} %get-tuple-element.158.refs_7_.refs_0_.refs_1_), channel_id=1, source_target_pairs={{0,4},{4,0},{1,5},{5,1},{2,6},{6,2},{3,7},{7,3},{8,12},{12,8},{9,1... | collective-permute-start | bytes 3538952 | tf_op jit(solution)/shard_map/ppermute | solution.py:712
  154.9 10.2 %collective-permute-start.12 = (bf16[3,48,1152]{2,1,0:T(8,128)(2,1)S(1)}, bf16[3,48,1152]{2,1,0:T(8,128)(2,1)S(1)}, u32[]{:S(2)}, u32[]{:S(2)}) collective-permute-start(bf16[3,48,1152]{2,1,0:T(8,128)(2,1)S(1)} %copy-done.27), channel_id=1, source_target_pairs={{0,8},{8,0},{1,9},{9,1},{2,10},{10,2},{3,11},{11,3},{4,12},{12,4},... | collective-permute-start | bytes 995336 | tf_op jit(solution)/shard_map/ppermute | solution.py:731
  156.0 9.5 %collective-permute-start.13 = (bf16[3,48,1152]{2,1,0:T(8,128)(2,1)S(1)}, bf16[3,48,1152]{2,1,0:T(8,128)(2,1)S(1)}, u32[]{:S(2)}, u32[]{:S(2)}) collective-permute-start(bf16[3,48,1152]{2,1,0:T(8,128)(2,1)S(1)} %copy-done.28), channel_id=1, source_target_pairs={{0,16},{16,0},{1,17},{17,1},{2,18},{18,2},{3,19},{19,3},{4,20},{20... | collective-permute-start | bytes 995336 | tf_op jit(solution)/shard_map/ppermute | solution.py:732
  157.0 26.0 %collective-permute-start.16 = (bf16[512,1152]{1,0:T(8,128)(2,1)S(1)}, bf16[512,1152]{1,0:T(8,128)(2,1)S(1)}, u32[]{:S(2)}, u32[]{:S(2)}) collective-permute-start(bf16[512,1152]{1,0:T(8,128)(2,1)S(1)} %copy-done.30), channel_id=1, source_target_pairs={{0,4},{4,0},{1,5},{5,1},{2,6},{6,2},{3,7},{7,3},{8,12},{12,8},{9,1... | collective-permute-start | bytes 3538952 | tf_op jit(solution)/shard_map/ppermute | solution.py:712
  165.6 16.6 %collective-permute-start.14 = (bf16[2,3,48,1152]{3,2,1,0:T(8,128)(2,1)S(1)}, bf16[2,3,48,1152]{3,2,1,0:T(8,128)(2,1)S(1)}, u32[]{:S(2)}, u32[]{:S(2)}) collective-permute-start(bf16[2,3,48,1152]{3,2,1,0:T(8,128)(2,1)S(1)} %pad_maximum_fusion.9.refs_3_), channel_id=1, source_target_pairs={{0,16},{16,0},{1,17},{17,1},{2,18},{18,2},{3,19},{19,3},{4,20},{20... | collective-permute-start | bytes 1990664 | tf_op jit(solution)/shard_map/ppermute | solution.py:737
  166.7 16.2 %collective-permute-start.15 = (bf16[2,3,48,1152]{3,2,1,0:T(8,128)(2,1)S(1)}, bf16[2,3,48,1152]{3,2,1,0:T(8,128)(2,1)S(1)}, u32[]{:S(2)}, u32[]{:S(2)}) collective-permute-start(bf16[2,3,48,1152]{3,2,1,0:T(8,128)(2,1)S(1)} %pad_maximum_fusion.10.refs_4_), channel_id=1, source_target_pairs={{0,8},{8,0},{1,9},{9,1},{2,10},{10,2},{3,11},{11,3},{4,12},{12,4},... | collective-permute-start | bytes 1990664 | tf_op jit(solution)/shard_map/ppermute | solution.py:737
  195.5 36.9 %collective-permute-start.17 = (bf16[2,2,2,144,384]{4,3,2,1,0:T(8,128)(2,1)}, bf16[2,2,2,144,384]{4,3,2,1,0:T(8,128)(2,1)S(1)}, u32[]{:S(2)}, u32[]{:S(2)}) collective-permute-start(bf16[2,2,2,144,384]{4,3,2,1,0:T(8,128)(2,1)} %get-tuple-element.165.refs_7_.refs_4_), channel_id=1, source_target_pairs={{0,8},{8,0},{1,9},{9,1},{2,10},{10,2},{3,11},{11,3},{4,12},{12,4},... | collective-permute-start | bytes 2654216 | tf_op jit(solution)/shard_map/ppermute | solution.py:768
  202.2 30.2 %collective-permute-start.18 = (bf16[2,2,2,144,384]{4,3,2,1,0:T(8,128)(2,1)S(1)}, bf16[2,2,2,144,384]{4,3,2,1,0:T(8,128)(2,1)S(1)}, u32[]{:S(2)}, u32[]{:S(2)}) collective-permute-start(bf16[2,2,2,144,384]{4,3,2,1,0:T(8,128)(2,1)S(1)} %copy-done.14), channel_id=1, source_target_pairs={{0,16},{16,0},{1,17},{17,1},{2,18},{18,2},{3,19},{19,3},{4,20},{20... | collective-permute-start | bytes 2654216 | tf_op jit(solution)/shard_map/ppermute | solution.py:768
  230.3 20.1 %collective-permute-start.20 = (bf16[2,2,2,144,384]{4,3,2,1,0:T(8,128)(2,1)}, bf16[2,2,2,144,384]{4,3,2,1,0:T(8,128)(2,1)}, u32[]{:S(2)}, u32[]{:S(2)}) collective-permute-start(bf16[2,2,2,144,384]{4,3,2,1,0:T(8,128)(2,1)} %get-tuple-element.168.refs_2_), channel_id=1, source_target_pairs={{0,8},{8,0},{1,9},{9,1},{2,10},{10,2},{3,11},{11,3},{4,12},{12,4},... | collective-permute-start | bytes 2654216 | tf_op jit(solution)/shard_map/ppermute | solution.py:768
  231.3 19.5 %collective-permute-start.21 = (bf16[2,2,2,144,384]{4,3,2,1,0:T(8,128)(2,1)}, bf16[2,2,2,144,384]{4,3,2,1,0:T(8,128)(2,1)}, u32[]{:S(2)}, u32[]{:S(2)}) collective-permute-start(bf16[2,2,2,144,384]{4,3,2,1,0:T(8,128)(2,1)} %get-tuple-element.169.refs_3_), channel_id=1, source_target_pairs={{0,16},{16,0},{1,17},{17,1},{2,18},{18,2},{3,19},{19,3},{4,20},{20... | collective-permute-start | bytes 2654216 | tf_op jit(solution)/shard_map/ppermute | solution.py:768
  248.3 22.8 %collective-permute-start.23 = (bf16[2,2,2,144,384]{4,3,2,1,0:T(8,128)(2,1)}, bf16[2,2,2,144,384]{4,3,2,1,0:T(8,128)(2,1)}, u32[]{:S(2)}, u32[]{:S(2)}) collective-permute-start(bf16[2,2,2,144,384]{4,3,2,1,0:T(8,128)(2,1)} %get-tuple-element.170.refs_4_), channel_id=1, source_target_pairs={{0,8},{8,0},{1,9},{9,1},{2,10},{10,2},{3,11},{11,3},{4,12},{12,4},... | collective-permute-start | bytes 2654216 | tf_op jit(solution)/shard_map/ppermute | solution.py:768
  249.4 22.8 %collective-permute-start.24 = (bf16[2,2,2,144,384]{4,3,2,1,0:T(8,128)(2,1)}, bf16[2,2,2,144,384]{4,3,2,1,0:T(8,128)(2,1)}, u32[]{:S(2)}, u32[]{:S(2)}) collective-permute-start(bf16[2,2,2,144,384]{4,3,2,1,0:T(8,128)(2,1)} %get-tuple-element.171.refs_5_), channel_id=1, source_target_pairs={{0,16},{16,0},{1,17},{17,1},{2,18},{18,2},{3,19},{19,3},{4,20},{20... | collective-permute-start | bytes 2654216 | tf_op jit(solution)/shard_map/ppermute | solution.py:768
  263.8 13.3 %collective-permute-start.22 = (bf16[512,1152]{1,0:T(8,128)(2,1)}, bf16[512,1152]{1,0:T(8,128)(2,1)}, u32[]{:S(2)}, u32[]{:S(2)}) collective-permute-start(bf16[512,1152]{1,0:T(8,128)(2,1)} %get-tuple-element.187.refs_1_.refs_3_), channel_id=1, source_target_pairs={{0,4},{4,0},{1,5},{5,1},{2,6},{6,2},{3,7},{7,3},{8,12},{12,8},{9,1... | collective-permute-start | bytes 3538952 | tf_op jit(solution)/shard_map/ppermute | solution.py:712
  263.9 45.1 %collective-permute-start.30 = (bf16[2,2,144,384]{3,2,1,0:T(8,128)(2,1)}, bf16[2,2,144,384]{3,2,1,0:T(8,128)(2,1)}, u32[]{:S(2)}, u32[]{:S(2)}) collective-permute-start(bf16[2,2,144,384]{3,2,1,0:T(8,128)(2,1)} %fusion.12.refs_6_), channel_id=1, source_target_pairs={{0,16},{16,0},{1,17},{17,1},{2,18},{18,2},{3,19},{19,3},{4,20},{20... | collective-permute-start | bytes 1327112 | tf_op jit(solution)/shard_map/ppermute | solution.py:777
  264.9 61.1 %collective-permute-start.31 = (bf16[2,2,144,384]{3,2,1,0:T(8,128)(2,1)}, bf16[2,2,144,384]{3,2,1,0:T(8,128)(2,1)}, u32[]{:S(2)}, u32[]{:S(2)}) collective-permute-start(bf16[2,2,144,384]{3,2,1,0:T(8,128)(2,1)} %fusion.13.refs_7_), channel_id=1, source_target_pairs={{0,8},{8,0},{1,9},{9,1},{2,10},{10,2},{3,11},{11,3},{4,12},{12,4},... | collective-permute-start | bytes 1327112 | tf_op jit(solution)/shard_map/ppermute | solution.py:777
  271.1 57.0 %collective-permute-start.26 = (bf16[2,2,144,384]{3,2,1,0:T(8,128)(2,1)S(1)}, bf16[2,2,144,384]{3,2,1,0:T(8,128)(2,1)S(1)}, u32[]{:S(2)}, u32[]{:S(2)}) collective-permute-start(bf16[2,2,144,384]{3,2,1,0:T(8,128)(2,1)S(1)} %copy-done.25), channel_id=1, source_target_pairs={{0,16},{16,0},{1,17},{17,1},{2,18},{18,2},{3,19},{19,3},{4,20},{20... | collective-permute-start | bytes 1327112 | tf_op jit(solution)/shard_map/ppermute | solution.py:777
  272.2 55.9 %collective-permute-start.27 = (bf16[2,2,144,384]{3,2,1,0:T(8,128)(2,1)S(1)}, bf16[2,2,144,384]{3,2,1,0:T(8,128)(2,1)}, u32[]{:S(2)}, u32[]{:S(2)}) collective-permute-start(bf16[2,2,144,384]{3,2,1,0:T(8,128)(2,1)S(1)} %copy-done.24), channel_id=1, source_target_pairs={{0,8},{8,0},{1,9},{9,1},{2,10},{10,2},{3,11},{11,3},{4,12},{12,4},... | collective-permute-start | bytes 1327112 | tf_op jit(solution)/shard_map/ppermute | solution.py:777
  277.1 50.0 %collective-permute-start.28 = (bf16[2,2,144,384]{3,2,1,0:T(8,128)(2,1)}, bf16[2,2,144,384]{3,2,1,0:T(8,128)(2,1)}, u32[]{:S(2)}, u32[]{:S(2)}) collective-permute-start(bf16[2,2,144,384]{3,2,1,0:T(8,128)(2,1)} %fusion.16.refs_10_.refs_7_), channel_id=1, source_target_pairs={{0,16},{16,0},{1,17},{17,1},{2,18},{18,2},{3,19},{19,3},{4,20},{20... | collective-permute-start | bytes 1327112 | tf_op jit(solution)/shard_map/ppermute | solution.py:777
  309.0 19.1 %collective-permute-start.29 = (bf16[2,2,144,384]{3,2,1,0:T(8,128)(2,1)}, bf16[2,2,144,384]{3,2,1,0:T(8,128)(2,1)}, u32[]{:S(2)}, u32[]{:S(2)}) collective-permute-start(bf16[2,2,144,384]{3,2,1,0:T(8,128)(2,1)} %fusion.17.refs_11_.refs_8_), channel_id=1, source_target_pairs={{0,8},{8,0},{1,9},{9,1},{2,10},{10,2},{3,11},{11,3},{4,12},{12,4},... | collective-permute-start | bytes 1327112 | tf_op jit(solution)/shard_map/ppermute | solution.py:777
  326.0 42.4 %collective-permute-start.33 = (bf16[2,4,2,144,256]{4,3,2,1,0:T(8,128)(2,1)}, bf16[2,4,2,144,256]{4,3,2,1,0:T(8,128)(2,1)}, u32[]{:S(2)}, u32[]{:S(2)}) collective-permute-start(bf16[2,4,2,144,256]{4,3,2,1,0:T(8,128)(2,1)} %get-tuple-element.201.refs_7_), channel_id=1, source_target_pairs={{0,8},{8,0},{1,9},{9,1},{2,10},{10,2},{3,11},{11,3},{4,12},{12,4},... | collective-permute-start | bytes 3538952 | tf_op jit(solution)/shard_map/ppermute | solution.py:768
  327.1 41.4 %collective-permute-start.34 = (bf16[2,4,2,144,256]{4,3,2,1,0:T(8,128)(2,1)}, bf16[2,4,2,144,256]{4,3,2,1,0:T(8,128)(2,1)}, u32[]{:S(2)}, u32[]{:S(2)}) collective-permute-start(bf16[2,4,2,144,256]{4,3,2,1,0:T(8,128)(2,1)} %get-tuple-element.202.refs_8_), channel_id=1, source_target_pairs={{0,16},{16,0},{1,17},{17,1},{2,18},{18,2},{3,19},{19,3},{4,20},{20... | collective-permute-start | bytes 3538952 | tf_op jit(solution)/shard_map/ppermute | solution.py:768
  328.1 22.9 %collective-permute-start.25 = (bf16[512,1152]{1,0:T(8,128)(2,1)}, bf16[512,1152]{1,0:T(8,128)(2,1)}, u32[]{:S(2)}, u32[]{:S(2)}) collective-permute-start(bf16[512,1152]{1,0:T(8,128)(2,1)} %get-tuple-element.198), channel_id=1, source_target_pairs={{0,4},{4,0},{1,5},{5,1},{2,6},{6,2},{3,7},{7,3},{8,12},{12,8},{9,1... | collective-permute-start | bytes 3538952 | tf_op jit(solution)/shard_map/ppermute | solution.py:712
  337.6 69.2 %all-to-all-start.3 = ((bf16[4,2,144,1152]{3,2,1,0:T(8,128)(2,1)}), bf16[4,2,144,1152]{3,2,1,0:T(8,128)(2,1)S(1)}, u32[]{:S(2)}, u32[]{:S(2)}) async-start(bf16[4,2,144,1152]{3,2,1,0:T(8,128)(2,1)} %maximum_maximum_fusion.refs_11_), calls=%async_computation.3 | async-start | bytes 5308416 | tf_op jit(solution)/shard_map/all_to_all | solution.py:800
  349.0 19.4 %collective-permute-start.35 = (bf16[2,2,2,144,64]{4,3,2,1,0:T(8,128)(2,1)S(1)}, bf16[2,2,2,144,64]{4,3,2,1,0:T(8,128)(2,1)S(1)}, u32[]{:S(2)}, u32[]{:S(2)}) collective-permute-start(bf16[2,2,2,144,64]{4,3,2,1,0:T(8,128)(2,1)S(1)} %copy-done.56), channel_id=1, source_target_pairs={{0,8},{8,0},{1,9},{9,1},{2,10},{10,2},{3,11},{11,3},{4,12},{12,4},... | collective-permute-start | bytes 442376 | tf_op jit(solution)/shard_map/ppermute | solution.py:768
  349.6 18.8 %collective-permute-start.36 = (bf16[2,2,2,144,64]{4,3,2,1,0:T(8,128)(2,1)S(1)}, bf16[2,2,2,144,64]{4,3,2,1,0:T(8,128)(2,1)S(1)}, u32[]{:S(2)}, u32[]{:S(2)}) collective-permute-start(bf16[2,2,2,144,64]{4,3,2,1,0:T(8,128)(2,1)S(1)} %copy-done.55), channel_id=1, source_target_pairs={{0,16},{16,0},{1,17},{17,1},{2,18},{18,2},{3,19},{19,3},{4,20},{20... | collective-permute-start | bytes 442376 | tf_op jit(solution)/shard_map/ppermute | solution.py:768
  366.9 10.3 %collective-permute-start.32 = (bf16[512,1152]{1,0:T(8,128)(2,1)}, bf16[512,1152]{1,0:T(8,128)(2,1)S(1)}, u32[]{:S(2)}, u32[]{:S(2)}) collective-permute-start(bf16[512,1152]{1,0:T(8,128)(2,1)} %get-tuple-element.213), channel_id=1, source_target_pairs={{0,4},{4,0},{1,5},{5,1},{2,6},{6,2},{3,7},{7,3},{8,12},{12,8},{9,1... | collective-permute-start | bytes 3538952 | tf_op jit(solution)/shard_map/ppermute | solution.py:712
  369.9 21.6 %collective-permute-start.37 = (bf16[4,2,144,256]{3,2,1,0:T(8,128)(2,1)S(1)}, bf16[4,2,144,256]{3,2,1,0:T(8,128)(2,1)}, u32[]{:S(2)}, u32[]{:S(2)}) collective-permute-start(bf16[4,2,144,256]{3,2,1,0:T(8,128)(2,1)S(1)} %fusion.10.refs_7_), channel_id=1, source_target_pairs={{0,16},{16,0},{1,17},{17,1},{2,18},{18,2},{3,19},{19,3},{4,20},{20... | collective-permute-start | bytes 1769480 | tf_op jit(solution)/shard_map/ppermute | solution.py:777
  372.6 18.9 %collective-permute-start.38 = (bf16[4,2,144,256]{3,2,1,0:T(8,128)(2,1)}, bf16[4,2,144,256]{3,2,1,0:T(8,128)(2,1)}, u32[]{:S(2)}, u32[]{:S(2)}) collective-permute-start(bf16[4,2,144,256]{3,2,1,0:T(8,128)(2,1)} %fusion.11.refs_8_), channel_id=1, source_target_pairs={{0,8},{8,0},{1,9},{9,1},{2,10},{10,2},{3,11},{11,3},{4,12},{12,4},... | collective-permute-start | bytes 1769480 | tf_op jit(solution)/shard_map/ppermute | solution.py:777
  374.1 17.2 %collective-permute-start.39 = (bf16[2,2,144,64]{3,2,1,0:T(8,128)(2,1)S(1)}, bf16[2,2,144,64]{3,2,1,0:T(8,128)(2,1)}, u32[]{:S(2)}, u32[]{:S(2)}) collective-permute-start(bf16[2,2,144,64]{3,2,1,0:T(8,128)(2,1)S(1)} %fusion.22.refs_9_), channel_id=1, source_target_pairs={{0,16},{16,0},{1,17},{17,1},{2,18},{18,2},{3,19},{19,3},{4,20},{20... | collective-permute-start | bytes 221192 | tf_op jit(solution)/shard_map/ppermute | solution.py:777
  375.8 15.7 %collective-permute-start.40 = (bf16[2,2,144,64]{3,2,1,0:T(8,128)(2,1)S(1)}, bf16[2,2,144,64]{3,2,1,0:T(8,128)(2,1)}, u32[]{:S(2)}, u32[]{:S(2)}) collective-permute-start(bf16[2,2,144,64]{3,2,1,0:T(8,128)(2,1)S(1)} %fusion.23.refs_10_), channel_id=1, source_target_pairs={{0,8},{8,0},{1,9},{9,1},{2,10},{10,2},{3,11},{11,3},{4,12},{12,4},... | collective-permute-start | bytes 221192 | tf_op jit(solution)/shard_map/ppermute | solution.py:777
  398.3 21.7 %collective-permute-start.41 = (bf16[2,144,576]{2,1,0:T(8,128)(2,1)}, bf16[2,144,576]{2,1,0:T(8,128)(2,1)}, u32[]{:S(2)}, u32[]{:S(2)}) collective-permute-start(bf16[2,144,576]{2,1,0:T(8,128)(2,1)} %get-tuple-element.262.refs_5_), channel_id=1, source_target_pairs={{0,3},{1,0},{2,1},{3,2},{4,7},{5,4},{6,5},{7,6},{8,11},{9,8},{10,9... | collective-permute-start | bytes 995336 | tf_op jit(solution)/shard_map/ppermute | solution.py:806
  402.1 32.9 %collective-permute-start.42 = (bf16[2,144,576]{2,1,0:T(8,128)(2,1)}, bf16[2,144,576]{2,1,0:T(8,128)(2,1)}, u32[]{:S(2)}, u32[]{:S(2)}) collective-permute-start(bf16[2,144,576]{2,1,0:T(8,128)(2,1)} %get-tuple-element.261.refs_6_), channel_id=1, source_target_pairs={{0,2},{1,3},{2,0},{3,1},{4,6},{5,7},{6,4},{7,5},{8,10},{9,11},{10,... | collective-permute-start | bytes 995336 | tf_op jit(solution)/shard_map/ppermute | solution.py:806
  402.1 32.9 %collective-permute-start.43 = (bf16[2,144,576]{2,1,0:T(8,128)(2,1)}, bf16[2,144,576]{2,1,0:T(8,128)(2,1)}, u32[]{:S(2)}, u32[]{:S(2)}) collective-permute-start(bf16[2,144,576]{2,1,0:T(8,128)(2,1)} %get-tuple-element.260.refs_7_), channel_id=1, source_target_pairs={{0,1},{1,2},{2,3},{3,0},{4,5},{5,6},{6,7},{7,4},{8,9},{9,10},{10,1... | collective-permute-start | bytes 995336 | tf_op jit(solution)/shard_map/ppermute | solution.py:806
  438.6 10.3 %collective-permute-start.45 = (bf16[144,1152]{1,0:T(8,128)(2,1)S(1)}, bf16[144,1152]{1,0:T(8,128)(2,1)S(1)}, u32[]{:S(2)}, u32[]{:S(2)}) collective-permute-start(bf16[144,1152]{1,0:T(8,128)(2,1)S(1)} %fusion.18), channel_id=1, source_target_pairs={{0,4},{4,0},{1,5},{5,1},{2,6},{6,2},{3,7},{7,3},{8,12},{12,8},{9,1... | collective-permute-start | bytes 995336 | tf_op jit(solution)/shard_map/ppermute | solution.py:712
  441.2 20.4 %all-to-all-start.4 = ((f32[32,1,5118]{2,1,0:T(1,128)}), f32[32,1,5118]{2,1,0:T(1,128)}, u32[]{:S(2)}, u32[]{:S(2)}) async-start(f32[32,1,5118]{2,1,0:T(1,128)} %copy.39), calls=%async_computation.4 | async-start | bytes 1310720 | tf_op jit(solution)/shard_map/all_to_all | solution.py:1035
  (82 other events, 515.3 us)
